TPU v7x, 32 devices: a whole 2x2x4 slice. The times are simulated.
32 devices in a mesh: item: 4 (over y, x), seq: 8 (over z, core).
Axes of the slice: x: 2, y: 2, z: 4, core: 2. Of those that a mesh axis runs over, the one named last changes fastest.
Arguments:
- tokens: bfloat16 [8, 1024, 1536], P('item', 'seq'), may hold values from -6 to 6
- timestep: bfloat16 [8, 1536], replicated, may hold values from -6 to 6
- slot_item: int32 [8], replicated, may hold values from 0 to 7, each once
- slot_valid: int32 [8], replicated, may hold values 0 or 1
- cotangent: bfloat16 [8, 1024, 1536], P('item', 'seq'), may hold values from -6 to 6
- in_weight: bfloat16 [1536, 6144], P('seq'), may hold values from -0.15625 to 0.15625
- out_weight: bfloat16 [3072, 1536], P('seq'), may hold values from -0.109375 to 0.109375
- select_weight: bfloat16 [3072, 256], P('seq'), may hold values from -0.109375 to 0.109375
- modulation_weight: bfloat16 [1536, 4608], P('seq'), may hold values from -0.15625 to 0.15625
- delta_weight: bfloat16 [96, 6144], replicated, may hold values from -0.625 to 0.625
- filter_weight: bfloat16 [4, 6144], replicated, may hold values from -3 to 3
- filter_bias: bfloat16 [6144], replicated, may hold values from -3 to 3
- delta_bias: float32 [6144], replicated, may hold values from -4 to -1
- decay_log: float32 [16, 6144], replicated, may hold values from -9 to 1.4
- skip_gain: float32 [6144], replicated, may hold values from -40 to 40
- modulation_bias: bfloat16 [4608], replicated, may hold values from -3 to 3
Outputs:
- output: bfloat16 [8, 1024, 1536], P('item', 'seq')
- grad_tokens: bfloat16 [8, 1024, 1536], P('item', 'seq')
- grad_in_weight: float32 [1536, 6144], P('seq')
- grad_out_weight: float32 [3072, 1536], P('seq')
- grad_select_weight: float32 [3072, 256], P('seq')
- grad_modulation_weight: float32 [1536, 4608], P('seq')
- grad_delta_weight: float32 [96, 6144], replicated
- grad_filter_weight: float32 [4, 6144], replicated
- grad_filter_bias: float32 [6144], replicated
- grad_delta_bias: float32 [6144], replicated
- grad_decay_log: float32 [16, 6144], replicated
- grad_skip_gain: float32 [6144], replicated
- grad_modulation_bias: float32 [4608], replicated
Inputs may be any that keep to these rules, and one draw needn't show every extreme that they name: `slot_item`: each item index appears once. `slot_valid`: 1 marks a slot with a real item, 0 a padding slot.
All inputs are finite; a program needn't handle non-finite values.
Results may differ from a plain program's by a relative error of at most 0.015.
Values may be sent and summed in bfloat16 or wider, within the bound.
A program may use at most 320 MiB of HBM per device.

v0:
```python
import math

import jax
import jax.numpy as jnp
from jax import lax
from jax.sharding import PartitionSpec as P

epsilon = 1e-06
highest = lax.Precision.HIGHEST


def with_halo(x, sides, width):
    for axis, dim in sides:
        size, length = (lax.axis_size(axis), x.shape[dim])
        up = [(i, (i + 1) % size) for i in range(size - 1)]
        down = [(j, i) for i, j in up]
        last = lax.slice_in_dim(x, length - width, length, axis=dim)
        initial = lax.slice_in_dim(x, 0, width, axis=dim)
        before = lax.ppermute(last, axis, up)
        after = lax.ppermute(initial, axis, down)
        x = jnp.concatenate([before, x, after], axis=dim)
    return x


def entering(value, axis, join, neutral, backward):
    count, mine = (lax.axis_size(axis), lax.axis_index(axis))
    pieces = jax.tree.map(lambda part: lax.all_gather(part, axis), value)
    if backward:
        pieces = jax.tree.map(lambda part: part[::-1], pieces)
        mine = count - 1 - mine
    so_far = jax.tree.map(
        lambda part, zero: jnp.full_like(part, 0) + jnp.asarray(zero, part.dtype), value, neutral
    )

    def step(position, so_far):
        longer = join(so_far, jax.tree.map(lambda part: part[position], pieces))
        return jax.tree.map(lambda new, old: jnp.where(position < mine, new, old), longer, so_far)

    return lax.fori_loop(0, count - 1, step, so_far)


def entering_2(x, axis, join, neutral, backward):
    count = lax.axis_size(axis)
    place = lax.axis_index(axis)
    ahead = count - 1 - place if backward else place
    gathered = jax.tree.map(
        lambda a, kind: lax.all_gather(a.astype(kind), axis), x, (jnp.bfloat16, jnp.bfloat16)
    )
    state = jax.tree.map(lambda a, e: jnp.zeros_like(a) + jnp.asarray(e, a.dtype), x, neutral)

    def one(step, state):
        source = count - 1 - step if backward else step
        return join(
            state,
            jax.tree.map(
                lambda a, own: lax.dynamic_index_in_dim(a, source, 0, False).astype(own.dtype),
                gathered,
                x,
            ),
        )

    return lax.fori_loop(0, ahead, one, state)


def contract_rows(left_side, right_side):
    return lax.dot_general(
        left_side, right_side, (((0,), (0,)), ((), ())), preferred_element_type=jnp.float32
    )


def contract_exact(left_side, right_side):
    return lax.dot_general(
        left_side,
        right_side,
        (((0,), (0,)), ((), ())),
        precision=highest,
        preferred_element_type=jnp.float32,
    )


def contract_cols(left_side, right_side):
    return lax.dot_general(
        left_side, right_side, (((1,), (1,)), ((), ())), preferred_element_type=jnp.float32
    )


def silu_slope(argument):
    sigmoid_value = jax.nn.sigmoid(argument)
    return sigmoid_value * (1.0 + argument * (1.0 - sigmoid_value))


def chain_combine(earlier, later):
    return (earlier[0] * later[0], later[0] * earlier[1] + later[1])


def filter_apply(padded, tap_weight, tap_bias, backward_time, length):
    rim_width = tap_weight.shape[0] - 1
    filtered = (
        jnp.zeros((padded.shape[0], length, padded.shape[2]), jnp.float32) + tap_bias[None, None, :]
    )
    for offset in range(tap_weight.shape[0]):
        start_row = 2 * rim_width - offset if backward_time else offset
        window = padded[:, start_row : start_row + length, :].astype(jnp.float32)
        filtered = filtered + tap_weight[offset][None, None, :] * window
    return filtered


def advance(hidden, step_now, input_now, into_now, decay_rate):
    decay = jnp.exp(step_now[:, None, :] * decay_rate[None])
    return (
        decay * hidden
        + (step_now * input_now.astype(jnp.float32))[:, None, :] * into_now[:, :, None]
    )


def block_plan(length, backward_time):
    block_size = math.gcd(length, 16)
    block_count = length // block_size
    forward_steps = list(range(block_size))[::-1] if backward_time else list(range(block_size))
    return (block_size, block_count, forward_steps)


def local_end(step_size, activated, state_in, decay_rate, backward_time):
    slot_count, length, inner_width = step_size.shape
    block_size, block_count, forward_steps = block_plan(length, backward_time)

    def block_step(block_turn, hidden):
        block_index = block_count - 1 - block_turn if backward_time else block_turn
        first_row = block_index * block_size
        step_block = lax.dynamic_slice_in_dim(step_size, first_row, block_size, 1)
        input_block = lax.dynamic_slice_in_dim(activated, first_row, block_size, 1)
        into_block = lax.dynamic_slice_in_dim(state_in, first_row, block_size, 1)
        for position in forward_steps:
            hidden = advance(
                hidden,
                step_block[:, position],
                input_block[:, position],
                into_block[:, position],
                decay_rate,
            )
        return hidden

    initial = jnp.zeros((slot_count, decay_rate.shape[0], inner_width), jnp.float32)
    return lax.fori_loop(0, block_count, block_step, initial)


def scan_outputs(step_size, activated, state_in, state_out, decay_rate, incoming, backward_time):
    slot_count, length, inner_width = step_size.shape
    block_size, block_count, forward_steps = block_plan(length, backward_time)

    def block_step(block_turn, carry):
        hidden, results, starts = carry
        block_index = block_count - 1 - block_turn if backward_time else block_turn
        first_row = block_index * block_size
        starts = lax.dynamic_update_index_in_dim(starts, hidden, block_index, 0)
        step_block = lax.dynamic_slice_in_dim(step_size, first_row, block_size, 1)
        input_block = lax.dynamic_slice_in_dim(activated, first_row, block_size, 1)
        into_block = lax.dynamic_slice_in_dim(state_in, first_row, block_size, 1)
        outof_block = lax.dynamic_slice_in_dim(state_out, first_row, block_size, 1)
        row_values = [None] * block_size
        for position in forward_steps:
            hidden = advance(
                hidden,
                step_block[:, position],
                input_block[:, position],
                into_block[:, position],
                decay_rate,
            )
            row_values[position] = jnp.sum(outof_block[:, position][:, :, None] * hidden, axis=1)
        results = lax.dynamic_update_slice_in_dim(results, jnp.stack(row_values, 1), first_row, 1)
        return (hidden, results, starts)

    results = jnp.zeros((slot_count, length, inner_width), jnp.float32)
    starts = jnp.zeros((block_count,) + incoming.shape, jnp.float32)
    final_state, results, starts = lax.fori_loop(
        0, block_count, block_step, (incoming, results, starts)
    )
    return (results, starts)


def adjoint_export(step_size, state_out, grad_scanned, decay_rate, backward_time):
    slot_count, length, inner_width = step_size.shape
    block_size, block_count, forward_steps = block_plan(length, backward_time)
    backward_steps = forward_steps[::-1]

    def block_step(block_turn, pending):
        block_index = block_turn if backward_time else block_count - 1 - block_turn
        first_row = block_index * block_size
        step_block = lax.dynamic_slice_in_dim(step_size, first_row, block_size, 1)
        outof_block = lax.dynamic_slice_in_dim(state_out, first_row, block_size, 1)
        grad_block = lax.dynamic_slice_in_dim(grad_scanned, first_row, block_size, 1)
        for position in backward_steps:
            adjoint = (
                outof_block[:, position][:, :, None] * grad_block[:, position][:, None, :] + pending
            )
            pending = jnp.exp(step_block[:, position][:, None, :] * decay_rate[None]) * adjoint
        return pending

    initial = jnp.zeros((slot_count, decay_rate.shape[0], inner_width), jnp.float32)
    return lax.fori_loop(0, block_count, block_step, initial)


def adjoint_grads(
    step_size,
    activated,
    state_in,
    state_out,
    grad_scanned,
    decay_rate,
    starts,
    pending,
    backward_time,
):
    slot_count, length, inner_width = step_size.shape
    states = decay_rate.shape[0]
    block_size, block_count, forward_steps = block_plan(length, backward_time)
    backward_steps = forward_steps[::-1]

    def block_step(block_turn, carry):
        pending, grad_step, grad_input, grad_into, grad_outof, grad_rate = carry
        block_index = block_turn if backward_time else block_count - 1 - block_turn
        first_row = block_index * block_size
        step_block = lax.dynamic_slice_in_dim(step_size, first_row, block_size, 1)
        input_block = lax.dynamic_slice_in_dim(activated, first_row, block_size, 1).astype(
            jnp.float32
        )
        into_block = lax.dynamic_slice_in_dim(state_in, first_row, block_size, 1)
        outof_block = lax.dynamic_slice_in_dim(state_out, first_row, block_size, 1)
        grad_block = lax.dynamic_slice_in_dim(grad_scanned, first_row, block_size, 1)
        hidden = lax.dynamic_index_in_dim(starts, block_index, 0, keepdims=False)
        before_list = [None] * block_size
        after_list = [None] * block_size
        for position in forward_steps:
            before_list[position] = hidden
            hidden = advance(
                hidden,
                step_block[:, position],
                input_block[:, position],
                into_block[:, position],
                decay_rate,
            )
            after_list[position] = hidden
        step_rows = [None] * block_size
        input_rows = [None] * block_size
        into_rows = [None] * block_size
        outof_rows = [None] * block_size
        for position in backward_steps:
            step_now = step_block[:, position]
            input_now = input_block[:, position]
            decay = jnp.exp(step_now[:, None, :] * decay_rate[None])
            adjoint = (
                outof_block[:, position][:, :, None] * grad_block[:, position][:, None, :] + pending
            )
            through = adjoint * before_list[position] * decay
            weighted = jnp.sum(adjoint * into_block[:, position][:, :, None], axis=1)
            step_rows[position] = jnp.sum(through * decay_rate[None], axis=1) + weighted * input_now
            input_rows[position] = weighted * step_now
            into_rows[position] = jnp.sum(adjoint * (step_now * input_now)[:, None, :], axis=2)
            outof_rows[position] = jnp.sum(
                grad_block[:, position][:, None, :] * after_list[position], axis=2
            )
            grad_rate = grad_rate + jnp.sum(through * step_now[:, None, :], axis=0)
            pending = decay * adjoint
        grad_step = lax.dynamic_update_slice_in_dim(
            grad_step, jnp.stack(step_rows, 1), first_row, 1
        )
        grad_input = lax.dynamic_update_slice_in_dim(
            grad_input, jnp.stack(input_rows, 1), first_row, 1
        )
        grad_into = lax.dynamic_update_slice_in_dim(
            grad_into, jnp.stack(into_rows, 1), first_row, 1
        )
        grad_outof = lax.dynamic_update_slice_in_dim(
            grad_outof, jnp.stack(outof_rows, 1), first_row, 1
        )
        return (pending, grad_step, grad_input, grad_into, grad_outof, grad_rate)

    wide_zero = jnp.zeros((slot_count, length, inner_width), jnp.float32)
    narrow_zero = jnp.zeros((slot_count, length, states), jnp.float32)
    initial = (
        pending,
        wide_zero,
        wide_zero,
        narrow_zero,
        narrow_zero,
        jnp.zeros(decay_rate.shape, jnp.float32),
    )
    result = lax.fori_loop(0, block_count, block_step, initial)
    return (result[1], result[2], result[3], result[4], result[5])


def per_device(
    tokens,
    timestep,
    slot_item,
    slot_valid,
    cotangent,
    in_weight,
    out_weight,
    select_weight,
    modulation_weight,
    delta_weight,
    filter_weight,
    filter_bias,
    delta_bias,
    decay_log,
    skip_gain,
    modulation_bias,
):
    slot_count, length, model_width = tokens.shape
    inner_width = delta_weight.shape[1] // 2
    rank_width = delta_weight.shape[0]
    states = decay_log.shape[0]
    select_width = select_weight.shape[1] // 2
    tap_count = filter_weight.shape[0]
    rim_width = tap_count - 1
    row_count = slot_count * length
    item_count = timestep.shape[0]
    shard_rows = modulation_weight.shape[0]
    first_slot = lax.axis_index("item") * slot_count
    my_items = lax.dynamic_slice_in_dim(slot_item, first_slot, slot_count)
    valid_mask = lax.dynamic_slice_in_dim(slot_valid, first_slot, slot_count).astype(jnp.float32)[
        :, None, None
    ]
    chooser = (my_items[:, None] == jnp.arange(item_count, dtype=jnp.int32)[None, :]).astype(
        jnp.bfloat16
    )
    embedded = jnp.dot(chooser, timestep, preferred_element_type=jnp.float32)
    condition = jax.nn.silu(embedded).astype(jnp.bfloat16)
    condition_rows = lax.dynamic_slice_in_dim(
        condition, lax.axis_index("seq") * shard_rows, shard_rows, 1
    )
    modulation = lax.psum(
        jnp.dot(condition_rows, modulation_weight, preferred_element_type=jnp.float32), "seq"
    )
    modulation = modulation + modulation_bias.astype(jnp.float32)[None, :]
    shift_mod = modulation[:, None, :model_width]
    scale_mod = modulation[:, None, model_width : 2 * model_width]
    gate_mod = modulation[:, None, 2 * model_width :]
    whole_in, whole_out, whole_select = (
        lax.all_gather(in_weight, "seq", axis=0, tiled=True),
        lax.all_gather(out_weight, "seq", axis=0, tiled=True),
        lax.all_gather(select_weight, "seq", axis=0, tiled=True),
    )
    source = tokens.astype(jnp.float32)
    centered = source - jnp.mean(source, axis=-1, keepdims=True)
    inv_spread = lax.rsqrt(jnp.mean(centered * centered, axis=-1, keepdims=True) + epsilon)
    normed = centered * inv_spread
    mixed_in = (
        (normed * (1.0 + scale_mod) + shift_mod)
        .astype(jnp.bfloat16)
        .reshape(row_count, model_width)
    )
    projected = jnp.dot(mixed_in, whole_in, preferred_element_type=jnp.float32).reshape(
        slot_count, length, 2 * inner_width
    )
    filter_input = projected[..., :inner_width].astype(jnp.bfloat16)
    gate_half = projected[..., inner_width:]
    padded = with_halo(filter_input, (("seq", 1),), rim_width)
    kept_values = []
    scanned_sum = jnp.zeros((slot_count, length, inner_width), jnp.float32)
    for direction in range(2):
        backward_time = direction == 1
        columns = slice(direction * inner_width, (direction + 1) * inner_width)
        tap_weight = filter_weight[:, columns].astype(jnp.float32)
        filtered = filter_apply(
            padded, tap_weight, filter_bias[columns].astype(jnp.float32), backward_time, length
        )
        activated = jax.nn.silu(filtered).astype(jnp.bfloat16)
        select_block = whole_select[:, direction * select_width : (direction + 1) * select_width]
        selection = jnp.dot(
            activated.reshape(row_count, inner_width),
            select_block,
            preferred_element_type=jnp.float32,
        )
        delta_rank = selection[:, :rank_width].astype(jnp.bfloat16)
        state_in = selection[:, rank_width : rank_width + states].reshape(
            slot_count, length, states
        )
        state_out = selection[:, rank_width + states :].reshape(slot_count, length, states)
        step_pre = (
            jnp.dot(delta_rank, delta_weight[:, columns], preferred_element_type=jnp.float32)
            + delta_bias[columns][None, :]
        )
        step_size = jax.nn.softplus(step_pre).reshape(slot_count, length, inner_width)
        decay_rate = -jnp.exp(decay_log[:, columns])
        local_state = local_end(step_size, activated, state_in, decay_rate, backward_time)
        total_decay = jnp.exp(decay_rate[None] * jnp.sum(step_size, axis=1)[:, None, :])
        identity = (jnp.ones_like(total_decay), jnp.zeros_like(local_state))
        if backward_time:
            incoming = entering((total_decay, local_state), "seq", chain_combine, identity, True)[1]
        else:
            incoming = entering((total_decay, local_state), "seq", chain_combine, identity, False)[
                1
            ]
        scanned, starts = scan_outputs(
            step_size, activated, state_in, state_out, decay_rate, incoming, backward_time
        )
        scanned_sum = scanned_sum + scanned + skip_gain[columns] * activated.astype(jnp.float32)
        kept_values.append(
            (
                filtered,
                activated,
                delta_rank,
                state_in,
                state_out,
                step_pre,
                step_size,
                decay_rate,
                total_decay,
                starts,
            )
        )
    silu_gate = jax.nn.silu(gate_half)
    mixed_out = (scanned_sum * silu_gate).astype(jnp.bfloat16).reshape(row_count, inner_width)
    branch = jnp.dot(mixed_out, whole_out, preferred_element_type=jnp.float32).reshape(
        slot_count, length, model_width
    )
    output = (source + valid_mask * gate_mod * branch).astype(jnp.bfloat16)
    whole_in, whole_out, whole_select = (
        lax.all_gather(in_weight, "seq", axis=0, tiled=True),
        lax.all_gather(out_weight, "seq", axis=0, tiled=True),
        lax.all_gather(select_weight, "seq", axis=0, tiled=True),
    )
    incoming_grad = cotangent.astype(jnp.float32)
    grad_branch = (
        (valid_mask * gate_mod * incoming_grad).astype(jnp.bfloat16).reshape(row_count, model_width)
    )
    grad_gate = jnp.sum(valid_mask * incoming_grad * branch, axis=1)
    grad_out_full = contract_rows(mixed_out, grad_branch)
    grad_mixed = contract_cols(grad_branch, whole_out).reshape(slot_count, length, inner_width)
    grad_scanned = grad_mixed * silu_gate
    grad_gate_half = grad_mixed * scanned_sum * silu_slope(gate_half)
    grad_padded = jnp.zeros((slot_count, length + 2 * rim_width, inner_width), jnp.float32)
    (
        delta_parts,
        filter_parts,
        filter_bias_parts,
        delta_bias_parts,
        decay_parts,
        skip_parts,
        select_parts,
    ) = ([], [], [], [], [], [], [])
    for direction in range(2):
        backward_time = direction == 1
        columns = slice(direction * inner_width, (direction + 1) * inner_width)
        (
            filtered,
            activated,
            delta_rank,
            state_in,
            state_out,
            step_pre,
            step_size,
            decay_rate,
            total_decay,
            starts,
        ) = kept_values[direction]
        select_block = whole_select[:, direction * select_width : (direction + 1) * select_width]
        export = adjoint_export(step_size, state_out, grad_scanned, decay_rate, backward_time)
        identity = (jnp.ones_like(total_decay), jnp.zeros_like(export))
        if backward_time:
            pending = entering_2((total_decay, export), "seq", chain_combine, identity, False)[1]
        else:
            pending = entering_2((total_decay, export), "seq", chain_combine, identity, True)[1]
        grad_step, grad_input, grad_into, grad_outof, grad_rate = adjoint_grads(
            step_size,
            activated,
            state_in,
            state_out,
            grad_scanned,
            decay_rate,
            starts,
            pending,
            backward_time,
        )
        activated_wide = activated.astype(jnp.float32)
        skip_parts.append(jnp.sum(grad_scanned * activated_wide, axis=(0, 1)))
        decay_parts.append(grad_rate * decay_rate)
        grad_pre = grad_step.reshape(row_count, inner_width) * jax.nn.sigmoid(step_pre)
        grad_pre_low = grad_pre.astype(jnp.bfloat16)
        delta_bias_parts.append(jnp.sum(grad_pre, axis=0))
        delta_parts.append(contract_rows(delta_rank, grad_pre_low))
        grad_rank = contract_cols(grad_pre_low, delta_weight[:, columns])
        grad_selection = jnp.concatenate(
            [
                grad_rank,
                grad_into.reshape(row_count, states),
                grad_outof.reshape(row_count, states),
            ],
            axis=1,
        ).astype(jnp.bfloat16)
        activated_rows = activated.reshape(row_count, inner_width)
        select_parts.append(contract_rows(activated_rows, grad_selection))
        grad_activated = grad_input + skip_gain[columns] * grad_scanned
        grad_activated = grad_activated + contract_cols(grad_selection, select_block).reshape(
            slot_count, length, inner_width
        )
        grad_filtered = grad_activated * silu_slope(filtered)
        filter_bias_parts.append(jnp.sum(grad_filtered, axis=(0, 1)))
        tap_weight = filter_weight[:, columns].astype(jnp.float32)
        tap_rows = []
        for offset in range(tap_count):
            start_row = 2 * rim_width - offset if backward_time else offset
            window = padded[:, start_row : start_row + length, :].astype(jnp.float32)
            tap_rows.append(jnp.sum(grad_filtered * window, axis=(0, 1)))
            grad_padded = grad_padded + jnp.pad(
                tap_weight[offset][None, None, :] * grad_filtered,
                ((0, 0), (start_row, 2 * rim_width - start_row), (0, 0)),
            )
        filter_parts.append(jnp.stack(tap_rows, 0))
    rim_rows = jnp.concatenate(
        [grad_padded[:, :rim_width], grad_padded[:, length + rim_width :]], axis=1
    )
    arrived = with_halo(rim_rows.astype(jnp.bfloat16), (("seq", 1),), rim_width).astype(
        rim_rows.dtype
    )
    grad_filter_input = grad_padded[:, rim_width : rim_width + length]
    grad_filter_input = grad_filter_input + jnp.pad(
        arrived[:, :rim_width], ((0, 0), (0, length - rim_width), (0, 0))
    )
    grad_filter_input = grad_filter_input + jnp.pad(
        arrived[:, 3 * rim_width :], ((0, 0), (length - rim_width, 0), (0, 0))
    )
    grad_projected = jnp.concatenate([grad_filter_input, grad_gate_half], axis=2).astype(
        jnp.bfloat16
    )
    grad_projected = grad_projected.reshape(row_count, 2 * inner_width)
    grad_in_full = contract_rows(mixed_in, grad_projected)
    grad_mixed_in = contract_cols(grad_projected, whole_in).reshape(slot_count, length, model_width)
    grad_shift = jnp.sum(grad_mixed_in, axis=1)
    grad_scale = jnp.sum(grad_mixed_in * normed, axis=1)
    grad_normed = grad_mixed_in * (1.0 + scale_mod)
    grad_source = inv_spread * (
        grad_normed
        - jnp.mean(grad_normed, axis=-1, keepdims=True)
        - normed * jnp.mean(grad_normed * normed, axis=-1, keepdims=True)
    )
    grad_tokens = (incoming_grad + grad_source).astype(jnp.bfloat16)
    grad_modulation = jnp.concatenate([grad_shift, grad_scale, grad_gate], axis=1)
    grad_select_full = jnp.concatenate(select_parts, axis=1)
    modulation_total = lax.psum(grad_modulation.astype(jnp.bfloat16), "seq").astype(jnp.float32)
    grad_modulation_rows = contract_exact(condition_rows.astype(jnp.float32), modulation_total)
    shards = (
        lax.psum_scatter(
            grad_in_full.astype(jnp.bfloat16), "seq", scatter_dimension=0, tiled=True
        ).astype(jnp.float32),
        lax.psum_scatter(
            grad_out_full.astype(jnp.bfloat16), "seq", scatter_dimension=0, tiled=True
        ).astype(jnp.float32),
        lax.psum_scatter(
            grad_select_full.astype(jnp.bfloat16), "seq", scatter_dimension=0, tiled=True
        ).astype(jnp.float32),
    )
    grad_in_weight, grad_out_weight, grad_select_weight, grad_modulation_weight = (
        lax.psum(shards[0].astype(jnp.bfloat16), "item").astype(jnp.float32),
        lax.psum(shards[1].astype(jnp.bfloat16), "item").astype(jnp.float32),
        lax.psum(shards[2].astype(jnp.bfloat16), "item").astype(jnp.float32),
        lax.psum(grad_modulation_rows.astype(jnp.bfloat16), "item").astype(jnp.float32),
    )
    small = lax.psum(
        (
            jnp.concatenate(delta_parts, axis=1),
            jnp.concatenate(filter_parts, axis=1),
            jnp.concatenate(filter_bias_parts, axis=0),
            jnp.concatenate(delta_bias_parts, axis=0),
            jnp.concatenate(decay_parts, axis=1),
            jnp.concatenate(skip_parts, axis=0),
            jnp.sum(grad_modulation, axis=0),
        ),
        ("item", "seq"),
    )
    return (
        output,
        grad_tokens,
        grad_in_weight,
        grad_out_weight,
        grad_select_weight,
        grad_modulation_weight,
        small[0],
        small[1],
        small[2],
        small[3],
        small[4],
        small[5],
        small[6],
    )


def solution(mesh):
    in_specs = (
        P("item", "seq", None),
        P(),
        P(),
        P(),
        P("item", "seq", None),
        P("seq", None),
        P("seq", None),
        P("seq", None),
        P("seq", None),
        P(),
        P(),
        P(),
        P(),
        P(),
        P(),
        P(),
    )
    out_specs = (
        P("item", "seq", None),
        P("item", "seq", None),
        P("seq", None),
        P("seq", None),
        P("seq", None),
        P("seq", None),
        P(),
        P(),
        P(),
        P(),
        P(),
        P(),
        P(),
    )
    return jax.shard_map(
        per_device, mesh=mesh, in_specs=in_specs, out_specs=out_specs, check_vma=False
    )
```

profile of v0, /device:TPU:0, one launch (start us, length us, event | category | flops | bytes accessed | tf_op | source)
XLA Modules:
  0.0 2235.6 jit_solution(15589922570228410675)
XLA Ops:
  10.8 31.6 %psum.91 = f32[2,4608]{1,0:T(2,128)S(1)} all-reduce(f32[2,4608]{1,0:T(2,128)S(1)} %fusion.483), channel_id=1, replica_groups=mesh['item'=4,'seq'=8] {'seq'}, use_global_device_ids=true, to_apply=%region_0.1 | all-reduce | flops 9216 | bytes 73728 | tf_op jit(solution)/shard_map/psum | solution.py:333
  43.6 137.9 %all-gather.16.cloned.1.call-done = bf16[1536,6144]{1,0:T(8,128)(2,1)} async-done(((bf16[192,6144]{1,0:T(8,128)(2,1)}), bf16[1536,6144]{1,0:T(8,128)(2,1)}) %all-gather.16.cloned.1.call-update) | async-done | bytes 18874384 | tf_op jit(solution)/shard_map/all_gather | solution.py:341
  181.5 13.6 fusion.502
  202.9 69.6 %all-gather.24.cloned.1.call-done = bf16[3072,1536]{1,0:T(8,128)(2,1)} async-done(((bf16[384,1536]{1,0:T(8,128)(2,1)}), bf16[3072,1536]{1,0:T(8,128)(2,1)}) %all-gather.24.cloned.1.call-update) | async-done | bytes 9437200 | tf_op jit(solution)/shard_map/all_gather | solution.py:342
  272.6 17.8 fusion.408
  290.4 7.3 all-gather.18.cloned.1.call-done
  299.6 3.3 bitcast_reduce_fusion.1
  304.6 4.0 copy.115
  308.6 4.2 copy.133
  312.9 25.0 %while.204 = (s32[]{:T(128)}, f32[2,16,3072]{2,1,0:T(8,128)S(1)}, f32[2,128,3072]{2,0,1:T(2,128)}, f32[16,3072]{1,0:T(8,128)S(1)}, f32[2,128,16]{2,0,1:T(2,128)S...) while((s32[]{:T(128)}, f32[2,16,3072]{2,1,0:T(8,128)S(1)}, ...), condition=%wide.region_50.51_spmd.clone, body=%wide.region_49.50_spmd.clone.sunk | while | flops 6389783 | bytes 3349085 | solution.py:200
  341.4 3.3 bitcast_reduce_fusion
  346.4 4.1 copy.123
  351.5 25.1 %while.206 = (s32[]{:T(128)}, f32[2,16,3072]{2,1,0:T(8,128)S(1)}, f32[2,128,3072]{2,0,1:T(2,128)}, f32[16,3072]{1,0:T(8,128)S(1)}, f32[2,128,16]{2,0,1:T(2,128)S...) while((s32[]{:T(128)}, f32[2,16,3072]{2,1,0:T(8,128)S(1)}, ...), condition=%wide.region_136.137_spmd.clone, body=%wide.region_135.136_spmd.clone.sunk | while | flops 6389782 | bytes 3349065 | solution.py:200
  381.4 35.7 %while.200 = (s32[]{:T(128)}, f32[2,16,3072]{2,1,0:T(8,128)}, f32[2,128,3072]{2,0,1:T(2,128)}, f32[16,3072]{1,0:T(8,128)S(1)}, bf16[2,128,3072]{2,0,1:T(2,128)(2...) while((s32[]{:T(128)}, f32[2,16,3072]{2,1,0:T(8,128)}, ...), condition=%wide.region_5.6_spmd.clone, body=%wide.region_4.5_spmd.clone.sunk | while | flops 6586390 | bytes 3152457 | solution.py:144
  386.6 3.2 multiply_add_fusion.125
  391.2 3.2 multiply_add_fusion.125
  409.4 3.2 multiply_add_fusion.125
  414.0 3.2 multiply_add_fusion.125
  420.3 35.8 %while.202 = (s32[]{:T(128)}, f32[2,16,3072]{2,1,0:T(8,128)}, f32[2,128,3072]{2,0,1:T(2,128)}, f32[16,3072]{1,0:T(8,128)S(1)}, bf16[2,128,3072]{2,0,1:T(2,128)(2...) while((s32[]{:T(128)}, f32[2,16,3072]{2,1,0:T(8,128)}, ...), condition=%wide.region_28.29_spmd.clone, body=%wide.region_27.28_spmd.clone.sunk | while | flops 6586391 | bytes 3152477 | solution.py:144
  434.5 3.2 multiply_add_fusion.126
  457.0 8.5 while.198
  465.6 16.4 all-gather.30.cloned.1.call-done
  482.0 39.4 %all-gather.20.cloned.1.call-done = f32[8,2,16,3072]{3,2,1,0:T(8,128)} async-done(((f32[1,2,16,3072]{3,2,1,0:T(8,128)}), f32[8,2,16,3072]{3,2,1,0:T(8,128)}) %all-gather.20.cloned.1.call-update) | async-done | bytes 3145744 | tf_op jit(solution)/shard_map/all_gather | solution.py:27
  521.4 10.4 while.201
  535.9 71.5 %while.196 = (s32[]{:T(128)}, f32[2,16,3072]{2,1,0:T(8,128)S(1)}, f32[2,128,3072]{2,1,0:T(8,128)}, f32[8,2,16,3072]{3,2,1,0:T(8,128)}, f32[2,128,3072]{2,0,1:T(2...) while((s32[]{:T(128)}, f32[2,16,3072]{2,1,0:T(8,128)S(1)}, ...), condition=%wide.region_25.26_spmd, body=%wide.region_8.25_spmd.sunk | while | flops 14254101 | bytes 10828379 | solution.py:175
  612.7 407.2 %while.205 = (s32[]{:T(128)}, f32[2,16,3072]{2,1,0:T(8,128)S(1)}, f32[2,128,3072]{2,1,0:T(8,128)}, f32[2,128,3072]{2,1,0:T(8,128)}, bf16[2,128,16]{2,0,1:T(2,128...) while((s32[]{:T(128)}, f32[2,16,3072]{2,1,0:T(8,128)S(1)}, ...), condition=%wide.region_134.135_spmd.clone, body=%wide.region_53.134_spmd.clone.sunk | while | flops 37010456 | bytes 35972848 | solution.py:288
  635.1 3.4 multiply_reduce_fusion.237
  685.8 3.4 multiply_reduce_fusion.237
  736.6 3.4 multiply_reduce_fusion.237
  787.4 3.4 multiply_reduce_fusion.237
  838.3 3.4 multiply_reduce_fusion.237
  889.1 3.4 multiply_reduce_fusion.237
  940.0 3.4 multiply_reduce_fusion.237
  990.8 3.4 multiply_reduce_fusion.237
  1022.3 3.8 rev.7
  1026.2 3.9 rev.6
  1030.1 10.3 while.203
  1044.4 70.7 %while.197 = (s32[]{:T(128)}, f32[2,16,3072]{2,1,0:T(8,128)S(1)}, f32[2,128,3072]{2,1,0:T(8,128)}, f32[8,2,16,3072]{3,2,1,0:T(8,128)}, f32[2,128,3072]{2,0,1:T(2...) while((s32[]{:T(128)}, f32[2,16,3072]{2,1,0:T(8,128)S(1)}, ...), condition=%wide.region_48.49_spmd, body=%wide.region_31.48_spmd.sunk | while | flops 14254105 | bytes 10827933 | solution.py:175
  1120.5 361.9 %while.207 = (s32[]{:T(128)}, f32[2,16,3072]{2,1,0:T(8,128)S(1)}, f32[2,128,3072]{2,1,0:T(8,128)}, f32[2,128,3072]{2,1,0:T(8,128)}, bf16[2,128,16]{2,0,1:T(2,128...) while((s32[]{:T(128)}, f32[2,16,3072]{2,1,0:T(8,128)S(1)}, ...), condition=%wide.region_220.221_spmd.clone, body=%wide.region_139.220_spmd.clone.sunk | while | flops 37993488 | bytes 34530480 | solution.py:288
  1127.3 4.8 multiply_reduce_fusion.239
  1172.4 4.8 multiply_reduce_fusion.239
  1217.5 4.8 multiply_reduce_fusion.239
  1262.7 4.8 multiply_reduce_fusion.239
  1307.9 4.8 multiply_reduce_fusion.239
  1353.1 4.8 multiply_reduce_fusion.239
  1398.3 4.8 multiply_reduce_fusion.239
  1443.4 4.8 multiply_reduce_fusion.239
  1482.4 6.2 fusion.490
  1496.0 6.6 multiply_convert_fusion
  1505.6 5.2 bitcast_convert_fusion.1
  1515.4 12.6 fusion.488
  1529.6 3.9 broadcast_multiply_fusion.3
  1533.5 6.1 fusion.492
  1547.9 9.6 bitcast_convert_fusion
  1557.6 10.5 fusion.433
  1568.2 8.0 fusion.443
  1576.2 32.0 %psum.95 = bf16[2,4608]{1,0:T(2,128)(2,1)S(1)} all-reduce(bf16[2,4608]{1,0:T(2,128)(2,1)S(1)} %fusion.482), channel_id=1, replica_groups=mesh['item'=4,'seq'=8] {'seq'}, use_global_device_ids=true, to_apply=%region_232.233 | all-reduce | flops 9216 | bytes 36864 | tf_op jit(solution)/shard_map/psum | solution.py:542
  1612.8 17.3 reduce-scatter.8.cloned.1.call-done
  1630.2 188.6 %reduce-scatter.6.cloned.1.call-done = bf16[192,6144]{1,0:T(8,128)(2,1)} async-done(((bf16[1536,6144]{1,0:T(8,128)(2,1)}), bf16[192,6144]{1,0:T(8,128)(2,1)}) %reduce-scatter.6.cloned.1.call-update) | async-done | bytes 2359312 | tf_op jit(solution)/shard_map/reduce_scatter | solution.py:545
  1826.9 120.9 %all-reduce.21.cloned.1.call-done = (bf16[384,256]{0,1:T(8,128)(2,1)}, bf16[192,6144]{1,0:T(8,128)(2,1)}, bf16[384,1536]{1,0:T(8,128)(2,1)}, bf16[192,4608]{1,0:T(8,128)(2,1)}) async-done(((bf16[384,256]{0,1:T(8,128)(2,1)}, bf16[192,6144]{1,0:T(8,128)(2,1)}, bf16[384,1536]{1,0:T(8,128)(2,1)}, bf16[192,4608]{1,0:T(8,128)(2,1)}), (bf16[384,256]{0,1:T(8,128)(2,1)}, bf16[192,6144]{1,0:T(8,128)(2,1)}, ...) | async-done | bytes 5505040 | tf_op jit(solution)/shard_map/psum | solution.py:558
  1947.9 4.5 convert_element_type.829
  1957.2 119.5 %all-reduce.17.cloned.1.call-done = (f32[6144]{0:T(1024)}, f32[6144]{0:T(1024)}, f32[6144]{0:T(1024)}, f32[4608]{0:T(1024)}) async-done(((f32[6144]{0:T(1024)}, f32[6144]{0:T(1024)}, f32[6144]{0:T(1024)}, f32[4608]{0:T(1024)}), (f32[6144]{0:T(1024)}, f32[6144]{0:T(1024)}, f32[6144]{0:T(1024)}, f32[4608]{0:T(1024)})) %all-reduce.17.cloned.1.call-update) | async-done | bytes 92176 | tf_op jit(solution)/shard_map/psum | solution.py:561
  2076.7 145.1 %all-reduce.19.cloned.1.call-done = (f32[96,6144]{1,0:T(8,128)}, f32[4,6144]{1,0:T(4,128)}, f32[16,6144]{1,0:T(8,128)}) async-done(((f32[96,6144]{1,0:T(8,128)}, f32[4,6144]{1,0:T(4,128)}, f32[16,6144]{1,0:T(8,128)}), (f32[96,6144]{1,0:T(8,128)}, f32[4,6144]{1,0:T(4,128)}, f32[16,6144]{1,0:T(8,128)})) %all-reduce.19.cloned.1.call-update) | async-done | bytes 2850832 | tf_op jit(solution)/shard_map/psum | solution.py:561
  2221.8 3.3 copy.477
  (4715 shorter events, 1052.9 us)
Async XLA Ops:
  7.2 35.3 %copy-start.269 = (bf16[4608]{0:T(1024)(128)(2,1)S(1)}, bf16[4608]{0:T(1024)(128)(2,1)}, u32[]{:S(2)}) copy-start(bf16[4608]{0:T(1024)(128)(2,1)} %param.55) | copy-start | bytes 27652
  7.2 35.3 %copy-start.276 = (s32[8]{0:T(128)S(1)}, s32[8]{0:T(128)}, u32[]{:S(2)}) copy-start(s32[8]{0:T(128)} %param.43) | copy-start | bytes 100
  7.2 35.3 %copy-start.38 = (bf16[2,128,1536]{2,1,0:T(8,128)(2,1)S(1)}, bf16[2,128,1536]{2,1,0:T(8,128)(2,1)}, u32[]{:S(2)}) copy-start(bf16[2,128,1536]{2,1,0:T(8,128)(2,1)} %param.40) | copy-start | bytes 2359300
  7.2 35.9 %copy-start.204 = (bf16[4,6144]{1,0:T(4,128)(2,1)S(1)}, bf16[4,6144]{1,0:T(4,128)(2,1)}, u32[]{:S(2)}) copy-start(bf16[4,6144]{1,0:T(4,128)(2,1)} %param.50) | copy-start | bytes 147460
  7.3 174.2 %all-gather.16.cloned.1.call-start = ((), (), s32[]{:S(2)}) async-start(), calls=%async_computation.3 | async-start | bytes 21233664 | tf_op jit(solution)/shard_map/all_gather | solution.py:341
  8.0 35.3 %copy-start.212 = (f32[6144]{0:T(1024)S(1)}, f32[6144]{0:T(1024)}, u32[]{:S(2)}) copy-start(f32[6144]{0:T(1024)} %param.52) | copy-start | bytes 73732
  8.0 35.4 %copy-start.126 = (f32[16,6144]{1,0:T(8,128)S(1)}, f32[16,6144]{1,0:T(8,128)}, u32[]{:S(2)}) copy-start(f32[16,6144]{1,0:T(8,128)} %param.53) | copy-start | bytes 1179652
  8.0 264.5 %all-gather.24.cloned.1.call-start = ((), (), s32[]{:S(2)}) async-start(), calls=%async_computation.7 | async-start | bytes 10616832 | tf_op jit(solution)/shard_map/all_gather | solution.py:342
  8.8 289.0 %all-gather.18.cloned.1.call-start = ((), (), s32[]{:S(2)}) async-start(), calls=%async_computation.4 | async-start | bytes 1769472 | tf_op jit(solution)/shard_map/all_gather | solution.py:343
  9.5 447.4 %all-gather.34.cloned.1.call-start = ((), (), s32[]{:S(2)}) async-start(), calls=%async_computation.14 | async-start | bytes 1769472 | tf_op jit(solution)/shard_map/all_gather | solution.py:47
  42.6 152.5 %copy-start.271 = (f32[2]{0:T(128)}, f32[2]{0:T(128)S(1)}, u32[]{:S(2)}) copy-start(f32[2]{0:T(128)S(1)} %dynamic-slice_convert_fusion.2) | copy-start | bytes 28
  42.8 152.3 %copy-start.207 = (f32[2,128]{1,0:T(2,128)}, f32[2,128]{1,0:T(2,128)S(1)}, u32[]{:S(2)}) copy-start(f32[2,128]{1,0:T(2,128)S(1)} %broadcast_multiply_fusion.10) | copy-start | bytes 3076
  43.2 151.9 %copy-start.210 = (f32[2,128]{1,0:T(2,128)}, f32[2,128]{1,0:T(2,128)S(1)}, u32[]{:S(2)}) copy-start(f32[2,128]{1,0:T(2,128)S(1)} %add_rsqrt_fusion) | copy-start | bytes 3076
  43.2 229.3 %copy-start.173 = (f32[1,3072]{1,0:T(1,128)}, f32[1,3072]{1,0:T(1,128)S(1)}, u32[]{:S(2)}) copy-start(f32[1,3072]{1,0:T(1,128)S(1)} %get-tuple-element.3357) | copy-start | bytes 36868
  43.2 229.3 %copy-start.175 = (f32[1,3072]{1,0:T(1,128)}, f32[1,3072]{1,0:T(1,128)S(1)}, u32[]{:S(2)}) copy-start(f32[1,3072]{1,0:T(1,128)S(1)} %get-tuple-element.3358) | copy-start | bytes 36868
  43.3 229.3 %copy-start.177 = (f32[1,3072]{1,0:T(1,128)}, f32[1,3072]{1,0:T(1,128)S(1)}, u32[]{:S(2)}) copy-start(f32[1,3072]{1,0:T(1,128)S(1)} %get-tuple-element.3359) | copy-start | bytes 36868
  43.3 229.3 %copy-start.179 = (f32[1,3072]{1,0:T(1,128)}, f32[1,3072]{1,0:T(1,128)S(1)}, u32[]{:S(2)}) copy-start(f32[1,3072]{1,0:T(1,128)S(1)} %get-tuple-element.3360) | copy-start | bytes 36868
  43.3 229.2 %copy-start.165 = (f32[1,3072]{1,0:T(1,128)}, f32[1,3072]{1,0:T(1,128)S(1)}, u32[]{:S(2)}) copy-start(f32[1,3072]{1,0:T(1,128)S(1)} %get-tuple-element.3351) | copy-start | bytes 36868
  43.3 229.2 %copy-start.167 = (f32[1,3072]{1,0:T(1,128)}, f32[1,3072]{1,0:T(1,128)S(1)}, u32[]{:S(2)}) copy-start(f32[1,3072]{1,0:T(1,128)S(1)} %get-tuple-element.3352) | copy-start | bytes 36868
  43.3 229.2 %copy-start.169 = (f32[1,3072]{1,0:T(1,128)}, f32[1,3072]{1,0:T(1,128)S(1)}, u32[]{:S(2)}) copy-start(f32[1,3072]{1,0:T(1,128)S(1)} %get-tuple-element.3353) | copy-start | bytes 36868
  43.4 229.2 %copy-start.171 = (f32[1,3072]{1,0:T(1,128)}, f32[1,3072]{1,0:T(1,128)S(1)}, u32[]{:S(2)}) copy-start(f32[1,3072]{1,0:T(1,128)S(1)} %get-tuple-element.3354) | copy-start | bytes 36868
  43.6 137.9 %copy-start.182 = (f32[2,1536]{1,0:T(2,128)}, f32[2,1536]{1,0:T(2,128)S(1)}, u32[]{:S(2)}) copy-start(f32[2,1536]{1,0:T(2,128)S(1)} %get-tuple-element.3361) | copy-start | bytes 36868
  43.6 137.9 %copy-start.186 = (f32[2,1536]{1,0:T(2,128)}, f32[2,1536]{1,0:T(2,128)S(1)}, u32[]{:S(2)}) copy-start(f32[2,1536]{1,0:T(2,128)S(1)} %get-tuple-element.3362) | copy-start | bytes 36868
  43.6 229.0 %copy-start.184 = (f32[2,1536]{1,0:T(2,128)}, f32[2,1536]{1,0:T(2,128)S(1)}, u32[]{:S(2)}) copy-start(f32[2,1536]{1,0:T(2,128)S(1)} %get-tuple-element.3363) | copy-start | bytes 36868
  195.1 77.6 %copy-start.134 = (bf16[2,128,1536]{2,1,0:T(8,128)(2,1)S(1)}, bf16[2,128,1536]{2,1,0:T(8,128)(2,1)}, u32[]{:S(2)}) copy-start(bf16[2,128,1536]{2,1,0:T(8,128)(2,1)} %param.44) | copy-start | bytes 2359300
  196.8 75.8 %collective-permute-start = (bf16[2,3,3072]{2,1,0:T(4,128)(2,1)S(1)}, bf16[2,3,3072]{2,1,0:T(4,128)(2,1)S(1)}, u32[]{:S(2)}, u32[]{:S(2)}) collective-permute-start(bf16[2,3,3072]{2,1,0:T(4,128)(2,1)S(1)} %get-tuple-element.3331), channel_id=1, source_target_pairs={{0,1},{1,2},{2,3},{3,4},{4,5},{5,6},{6,7},{8,9},{9,10},{10,11},{11... | collective-permute-start | bytes 110600 | tf_op jit(solution)/shard_map/ppermute | solution.py:19
  198.9 73.6 %collective-permute-start.1 = (bf16[2,3,3072]{2,1,0:T(4,128)(2,1)S(1)}, bf16[2,3,3072]{2,1,0:T(4,128)(2,1)S(1)}, u32[]{:S(2)}, u32[]{:S(2)}) collective-permute-start(bf16[2,3,3072]{2,1,0:T(4,128)(2,1)S(1)} %get-tuple-element.3330), channel_id=1, source_target_pairs={{1,0},{2,1},{3,2},{4,3},{5,4},{6,5},{7,6},{9,8},{10,9},{11,10},{12... | collective-permute-start | bytes 110600 | tf_op jit(solution)/shard_map/ppermute | solution.py:20
  200.2 90.1 %copy-start.190 = (f32[3072]{0:T(1024)}, f32[3072]{0:T(1024)S(1)}, u32[]{:S(2)}) copy-start(f32[3072]{0:T(1024)S(1)} %get-tuple-element.3368) | copy-start | bytes 36868
  200.2 90.1 %copy-start.192 = (f32[3072]{0:T(1024)}, f32[3072]{0:T(1024)S(1)}, u32[]{:S(2)}) copy-start(f32[3072]{0:T(1024)S(1)} %get-tuple-element.3369) | copy-start | bytes 36868
  290.4 87.0 %copy-start.2 = (bf16[2,128,3072]{2,1,0:T(8,128)(2,1)}, bf16[2,128,3072]{2,1,0:T(8,128)(2,1)S(1)}, u32[]{:S(2)}) copy-start(bf16[2,128,3072]{2,1,0:T(8,128)(2,1)S(1)} %get-tuple-element.2691) | copy-start | bytes 4718596
  338.7 118.3 %all-gather.26.cloned.1.call-start = ((), (), s32[]{:S(2)}) async-start(), calls=%async_computation.8 | async-start | bytes 1769472 | tf_op jit(solution)/shard_map/all_gather | solution.py:47
  351.4 114.1 %all-gather.36.cloned.1.call-start = ((), (), s32[]{:S(2)}) async-start(), calls=%async_computation.15 | async-start | bytes 1769472 | tf_op jit(solution)/shard_map/all_gather | solution.py:47
  377.3 88.2 %all-gather.28.cloned.1.call-start = ((), (), s32[]{:S(2)}) async-start(), calls=%async_computation.9 | async-start | bytes 1769472 | tf_op jit(solution)/shard_map/all_gather | solution.py:47
  381.2 100.8 %all-gather.30.cloned.1.call-start = ((), (), s32[]{:S(2)}) async-start(), calls=%async_computation.12 | async-start | bytes 3538944 | tf_op jit(solution)/shard_map/all_gather | solution.py:27
  381.4 35.8 %copy-start.4 = (bf16[2,128,3072]{2,1,0:T(8,128)(2,1)S(1)}, bf16[2,128,3072]{2,1,0:T(8,128)(2,1)}, u32[]{:S(2)}) copy-start(bf16[2,128,3072]{2,1,0:T(8,128)(2,1)} %get-tuple-element.2692) | copy-start | bytes 4718596
  417.2 104.2 %all-gather.20.cloned.1.call-start = ((), (), s32[]{:S(2)}) async-start(), calls=%async_computation.5 | async-start | bytes 3538944 | tf_op jit(solution)/shard_map/all_gather | solution.py:27
  420.2 602.1 %all-gather.32.cloned.1.call-start = ((), (), s32[]{:S(2)}) async-start(), calls=%async_computation.13 | async-start | bytes 3538944 | tf_op jit(solution)/shard_map/all_gather | solution.py:27
  456.1 570.1 %all-gather.22.cloned.1.call-start = ((), (), s32[]{:S(2)}) async-start(), calls=%async_computation.6 | async-start | bytes 3538944 | tf_op jit(solution)/shard_map/all_gather | solution.py:27
  456.8 1154.1 %reduce-scatter.10.cloned.1.call-start = ((), (), s32[]{:S(2)}) async-start(), calls=%async_computation.16 | async-start | bytes 1769472
  689.4 22.8 %copy-start.103 = (f32[2,3072]{1,0:T(2,128)S(1)}, f32[2,3072]{1,0:T(2,128)}, u32[]{:S(2)}) copy-start(f32[2,3072]{1,0:T(2,128)} %get-tuple-element.5159) | copy-start | bytes 73732 | tf_op jit(solution)/shard_map/while
  791.1 22.8 %copy-start.103 = (f32[2,3072]{1,0:T(2,128)S(1)}, f32[2,3072]{1,0:T(2,128)}, u32[]{:S(2)}) copy-start(f32[2,3072]{1,0:T(2,128)} %get-tuple-element.5159) | copy-start | bytes 73732 | tf_op jit(solution)/shard_map/while
  841.9 22.8 %copy-start.103 = (f32[2,3072]{1,0:T(2,128)S(1)}, f32[2,3072]{1,0:T(2,128)}, u32[]{:S(2)}) copy-start(f32[2,3072]{1,0:T(2,128)} %get-tuple-element.5159) | copy-start | bytes 73732 | tf_op jit(solution)/shard_map/while
  943.6 22.8 %copy-start.103 = (f32[2,3072]{1,0:T(2,128)S(1)}, f32[2,3072]{1,0:T(2,128)}, u32[]{:S(2)}) copy-start(f32[2,3072]{1,0:T(2,128)} %get-tuple-element.5159) | copy-start | bytes 73732 | tf_op jit(solution)/shard_map/while
  994.4 22.8 %copy-start.103 = (f32[2,3072]{1,0:T(2,128)S(1)}, f32[2,3072]{1,0:T(2,128)}, u32[]{:S(2)}) copy-start(f32[2,3072]{1,0:T(2,128)} %get-tuple-element.5159) | copy-start | bytes 73732 | tf_op jit(solution)/shard_map/while
  1496.0 134.2 %reduce-scatter.8.cloned.1.call-start = ((), (), s32[]{:S(2)}) async-start(), calls=%async_computation.11 | async-start | bytes 10616832 | tf_op jit(solution)/shard_map/reduce_scatter | solution.py:548
  1510.9 307.8 %reduce-scatter.6.cloned.1.call-start = ((), (), s32[]{:S(2)}) async-start(), calls=%async_computation.10 | async-start | bytes 21233664 | tf_op jit(solution)/shard_map/reduce_scatter | solution.py:545
  1540.8 3.6 collective-permute-start.2
  1543.1 3.1 collective-permute-start.3
  1557.5 390.3 %all-reduce.21.cloned.1.call-start = ((), (), s32[]{:S(2)}) async-start(), calls=%async_computation.19 | async-start | bytes 11010048 | tf_op jit(solution)/shard_map/psum | solution.py:558
  1576.2 32.1 %copy-start.202 = (f32[2,1536]{1,0:T(2,128)}, f32[2,1536]{1,0:T(2,128)S(1)}, u32[]{:S(2)}) copy-start(f32[2,1536]{1,0:T(2,128)S(1)} %get-tuple-element.3334) | copy-start | bytes 36868
  1610.9 207.9 %copy-start.267 = (f32[3072]{0:T(1024)S(1)}, f32[3072]{0:T(1024)}, u32[]{:S(2)}) copy-start(f32[3072]{0:T(1024)} %get-tuple-element.2449) | copy-start | bytes 36868
  1610.9 208.0 %copy-start.268 = (f32[3072]{0:T(1024)S(1)}, f32[3072]{0:T(1024)}, u32[]{:S(2)}) copy-start(f32[3072]{0:T(1024)} %get-tuple-element.2450) | copy-start | bytes 36868
  1610.9 208.6 %copy-start.194 = (f32[3072]{0:T(1024)S(1)}, f32[3072]{0:T(1024)}, u32[]{:S(2)}) copy-start(f32[3072]{0:T(1024)} %get-tuple-element.2693) | copy-start | bytes 36868
  1610.9 208.6 %copy-start.195 = (f32[3072]{0:T(1024)S(1)}, f32[3072]{0:T(1024)}, u32[]{:S(2)}) copy-start(f32[3072]{0:T(1024)} %get-tuple-element.3378) | copy-start | bytes 36868
  1610.9 209.2 %copy-start.196 = (f32[3072]{0:T(1024)S(1)}, f32[3072]{0:T(1024)}, u32[]{:S(2)}) copy-start(f32[3072]{0:T(1024)} %get-tuple-element.2451) | copy-start | bytes 36868
  1610.9 209.2 %copy-start.197 = (f32[3072]{0:T(1024)S(1)}, f32[3072]{0:T(1024)}, u32[]{:S(2)}) copy-start(f32[3072]{0:T(1024)} %get-tuple-element.2454) | copy-start | bytes 36868
  1610.9 209.8 %copy-start.140 = (f32[256,128]{0,1:T(8,128)S(1)}, f32[256,128]{0,1:T(8,128)}, u32[]{:S(2)}) copy-start(f32[256,128]{0,1:T(8,128)} %copy-done.139) | copy-start | bytes 393220
  1818.8 257.9 %all-reduce.17.cloned.1.call-start = ((), (), s32[]{:S(2)}) async-start(), calls=%async_computation.17 | async-start | bytes 188416 | tf_op jit(solution)/shard_map/psum | solution.py:561
  1826.1 395.7 %all-reduce.19.cloned.1.call-start = ((), (), s32[]{:S(2)}) async-start(), calls=%async_computation.18 | async-start | bytes 5701632 | tf_op jit(solution)/shard_map/psum | solution.py:561
  1956.3 272.6 %copy-start.1 = (bf16[192,4608]{1,0:T(8,128)(2,1)S(1)}, bf16[192,4608]{1,0:T(8,128)(2,1)}, u32[]{:S(2)}) copy-start(bf16[192,4608]{1,0:T(8,128)(2,1)} %param.48) | copy-start | bytes 5308420
  2076.7 149.0 %copy-start.216 = (f32[6144]{0:T(1024)S(1)}, f32[6144]{0:T(1024)}, u32[]{:S(2)}) copy-start(f32[6144]{0:T(1024)} %get-tuple-element.6273) | copy-start | bytes 73732
  2076.7 149.6 %copy-start.215 = (f32[6144]{0:T(1024)S(1)}, f32[6144]{0:T(1024)}, u32[]{:S(2)}) copy-start(f32[6144]{0:T(1024)} %get-tuple-element.6274) | copy-start | bytes 73732
  2076.7 151.0 %copy-start.214 = (f32[6144]{0:T(1024)S(1)}, f32[6144]{0:T(1024)}, u32[]{:S(2)}) copy-start(f32[6144]{0:T(1024)} %get-tuple-element.6276) | copy-start | bytes 73732
  2076.7 151.6 %copy-start.217 = (f32[4608]{0:T(1024)S(1)}, f32[4608]{0:T(1024)}, u32[]{:S(2)}) copy-start(f32[4608]{0:T(1024)} %get-tuple-element.6277) | copy-start | bytes 55300
  (1445 other events, 12190.4 us)
Sparse Core Ops, SparseCore 0:
  9.7 171.6 all-gather.15
  183.1 89.3 all-gather.23
  274.2 23.5 all-gather.17
  338.8 24.5 all-gather.33
  364.9 24.5 all-gather.25
  391.0 24.5 all-gather.35
  417.3 24.5 all-gather.27
  444.1 37.8 all-gather.29
  484.2 37.1 all-gather.19
  523.4 37.1 all-gather.31
  562.8 37.1 all-gather.21
  1496.1 33.0 reduce-scatter.9
  1531.5 98.6 reduce-scatter.7
  1632.4 186.3 reduce-scatter.5
  1823.0 124.8 all-reduce.20
  1954.5 122.1 all-reduce.16
  2083.6 138.2 all-reduce.18
where the time goes:
time: 2270 us; the launch traced here: 2240 us
  waiting for transfers between devices  867 us (38%)
  other arithmetic  863 us (38%)
  local copies, waits for them, and re-layouts  306 us (13%)
  matrix products  86.9 us (4%)
  blocking collectives  63.7 us (3%)
  loops' own time  25.5 us (1%)
    psum x2, waiting for transfers between devices, per_device(): lax.psum((jnp.concatenate(delta_parts, axis=1), jnp.concatenate(filter_pa...  265 us
    reduce_sum x80, other arithmetic, block_step(): grad_rate = grad_rate + jnp.sum(through * step_now[:, None, :], axis=0)  214 us
    while x240, other arithmetic  192 us
    reduce_scatter x1, waiting for transfers between devices, per_device(): lax.psum_scatter(grad_in_full.astype(jnp.bfloat16), 'seq', scatter_dimens...  189 us
    all_gather x1, waiting for transfers between devices, per_device(): lax.all_gather(in_weight, 'seq', axis=0, tiled=True)  138 us
    psum x1, waiting for transfers between devices, per_device(): lax.psum(shards[2].astype(jnp.bfloat16), 'item').astype(jnp.float32)  121 us
    while x3256, local copies, waits for them, and re-layouts  72.5 us
    all_gather x1, waiting for transfers between devices, per_device(): lax.all_gather(out_weight, 'seq', axis=0, tiled=True)  69.6 us

commit v1 on v0

v1 whole, which is shorter than its diff:
```python
import functools
import math

import jax
import jax.numpy as jnp
from jax import lax
from jax.experimental import pallas as pl
from jax.experimental.pallas import tpu as pltpu
from jax.sharding import PartitionSpec as P

epsilon = 1e-06
log2e = 1.4426950408889634
ln2 = 0.6931471805599453
chunk = 16
lanes = 128
f32 = jnp.float32
bf16 = jnp.bfloat16


def silu_slope(v):
    s = jax.nn.sigmoid(v)
    return s * (1.0 + v * (1.0 - s))


def dot_rows(a, b):
    return lax.dot_general(a, b, (((0,), (0,)), ((), ())), preferred_element_type=f32)


def dot_cols(a, b):
    return lax.dot_general(a, b, (((1,), (1,)), ((), ())), preferred_element_type=f32)


def fold_sublanes(parts):
    outs = []
    for first in range(0, len(parts), 8):
        cur = parts[first : first + 8]
        row = lax.broadcasted_iota(jnp.int32, cur[0].shape, 0)
        for hop in (4, 2, 1):
            keep = (row // hop) % 2 == 0
            half = len(cur) // 2
            merged = []
            for j in range(half):
                a, b = cur[j], cur[j + half]
                x, y = jnp.where(keep, a, b), jnp.where(keep, b, a)
                if hop == 4:
                    moved = pltpu.roll(y, 4, 0)
                else:
                    moved = jnp.where(keep, pltpu.roll(y, 8 - hop, 0), pltpu.roll(y, hop, 0))
                merged.append(x + moved)
            cur = merged
        outs.append(cur[0])
    return jnp.concatenate(outs, axis=0)


def wide(v, groups):
    return v if groups == 1 else jnp.concatenate([v] * groups, axis=1)


def spread_matrix():
    rows = lax.broadcasted_iota(jnp.int32, (2 * chunk, 2 * lanes), 0) // chunk
    cols = lax.broadcasted_iota(jnp.int32, (2 * chunk, 2 * lanes), 1) // lanes
    return (rows == cols).astype(f32).astype(bf16)


def chunk_sweep(count, body, spread, first, second):
    spread(0, first)
    if count == 1:
        body(0, first)
        return

    def pair(k, carry):
        spread(2 * k + 1, second)
        body(2 * k, first)
        spread(jnp.minimum(2 * k + 2, count - 1), first)
        body(2 * k + 1, second)
        return carry

    lax.fori_loop(0, count // 2, pair, 0)


def states_kernel(count, dt_ref, x_ref, bc_ref, r_ref, y_ref, h_ref, state, even, odd):
    slots, width = dt_ref.shape[1], dt_ref.shape[3]
    groups = width // lanes
    states = r_ref.shape[1]

    @pl.when(pl.program_id(1) == 0)
    def _():
        state[...] = jnp.zeros_like(state)

    def one_direction(reverse):
        mix = spread_matrix()

        def place(i):
            return (count - 1 - i) if reverse else i

        def spread(i, into):
            start = pl.multiple_of(place(i) * chunk, chunk)
            for s in range(slots):
                both = bc_ref[0, s, pl.ds(start, chunk), :]
                span = both.shape[1] // 2
                into[s] = dot_rows(jnp.concatenate([both[:, :span], both[:, span:]], axis=0), mix)

        def body(i, held):
            start = pl.multiple_of(place(i) * chunk, chunk)
            order = range(chunk - 1, -1, -1) if reverse else range(chunk)
            for s in range(slots):
                h = state[s]
                rate = r_ref[0]
                dt = dt_ref[0, s, pl.ds(start, chunk), :]
                u = dt * x_ref[0, s, pl.ds(start, chunk), :].astype(f32)
                kept, sums = [None] * chunk, [None] * chunk
                for t in order:
                    rows = slice(t * states, (t + 1) * states)
                    b = wide(held[s, rows, :lanes], groups)
                    c = wide(held[s, rows, lanes:], groups)
                    h = jnp.exp2(dt[t : t + 1] * rate) * h + u[t : t + 1] * b
                    kept[t] = h.astype(bf16)
                    p = h * c
                    sums[t] = p[:8] + p[8:]
                size = chunk * states
                h_ref[0, s, pl.ds(pl.multiple_of(start * states, size), size), :] = jnp.concatenate(
                    kept, axis=0
                )
                y_ref[0, s, pl.ds(start, chunk), :] = fold_sublanes(sums)
                state[s] = h

        chunk_sweep(count, body, spread, even, odd)

    for d in range(2):

        @pl.when(pl.program_id(0) == d)
        def _():
            one_direction(d == 1)


def adjoint_kernel(
    count,
    dt_ref,
    x_ref,
    bc_ref,
    r_ref,
    g_ref,
    h_ref,
    edge_ref,
    step_ref,
    input_ref,
    coef_ref,
    decay_ref,
    pending,
    even,
    odd,
):
    slots, width = dt_ref.shape[1], dt_ref.shape[3]
    groups = width // lanes
    states = r_ref.shape[1]
    last_block = pl.program_id(1) == pl.num_programs(1) - 1

    @pl.when(pl.program_id(1) == 0)
    def _():
        pending[...] = jnp.zeros_like(pending)
        decay_ref[...] = jnp.zeros_like(decay_ref)

    def one_direction(reverse):
        mix = spread_matrix()
        picks = (
            lax.broadcasted_iota(jnp.int32, (8, 2 * lanes), 0)
            == lax.broadcasted_iota(jnp.int32, (8, 2 * lanes), 1) // lanes
        ).astype(f32).astype(bf16)

        def place(i):
            return i if reverse else (count - 1 - i)

        def spread(i, into):
            start = pl.multiple_of(place(i) * chunk, chunk)
            for s in range(slots):
                both = bc_ref[0, s, pl.ds(start, chunk), :]
                span = both.shape[1] // 2
                into[s] = dot_rows(jnp.concatenate([both[:, :span], both[:, span:]], axis=0), mix)

        def body(i, held):
            here = place(i)
            start = pl.multiple_of(here * chunk, chunk)
            order = range(chunk) if reverse else range(chunk - 1, -1, -1)
            size = chunk * states
            base = pl.multiple_of(start * states, size)
            at_end = here == (count - 1 if reverse else 0)
            outer = jnp.where(last_block, 0.0, 1.0)
            near = pl.multiple_of(
                jnp.clip(start + (chunk if reverse else -1), 0, count * chunk - 1) * states, states
            )
            for s in range(slots):
                pend = pending[s]
                rate = r_ref[0]
                dt = dt_ref[0, s, pl.ds(start, chunk), :]
                x = x_ref[0, s, pl.ds(start, chunk), :].astype(f32)
                g = g_ref[s, pl.ds(start, chunk), :].astype(f32)
                u = dt * x
                before = jnp.where(
                    at_end,
                    edge_ref[0, s].astype(f32) * outer,
                    h_ref[0, s, pl.ds(near, states), :].astype(f32),
                )
                total = decay_ref[0, s]
                rate_sums, into_sums = [None] * chunk, [None] * chunk
                coef = [None] * chunk
                hidden = h_ref[0, s, pl.ds(base, size), :]
                now = hidden[order[0] * states : (order[0] + 1) * states].astype(f32)
                for k, t in enumerate(order):
                    rows = slice(t * states, (t + 1) * states)
                    b = wide(held[s, rows, :lanes], groups)
                    c = wide(held[s, rows, lanes:], groups)
                    if k + 1 < chunk:
                        q = order[k + 1]
                        prev = hidden[q * states : (q + 1) * states].astype(f32)
                    else:
                        prev = before
                    gt = g[t : t + 1]
                    adj = c * gt + pend
                    pend = jnp.exp2(dt[t : t + 1] * rate) * adj
                    through = pend * prev * rate
                    total = total + through * dt[t : t + 1]
                    rate_sums[t] = through[:8] + through[8:]
                    w = adj * b
                    into_sums[t] = w[:8] + w[8:]
                    cb, cc = adj * u[t : t + 1], now * gt
                    sb, sc = cb[:, :lanes], cc[:, :lanes]
                    for j in range(1, groups):
                        sb = sb + cb[:, j * lanes : (j + 1) * lanes]
                        sc = sc + cc[:, j * lanes : (j + 1) * lanes]
                    coef[t] = jnp.concatenate([sb, sc], axis=1).astype(bf16)
                    now = prev
                pending[s] = pend
                decay_ref[0, s] = total
                weighted = fold_sublanes(into_sums)
                step_ref[0, s, pl.ds(start, chunk), :] = (
                    fold_sublanes(rate_sums) * ln2 + weighted * x
                )
                input_ref[0, s, pl.ds(start, chunk), :] = weighted * dt
                coef_ref[0, s, pl.ds(pl.multiple_of(here * 8, 8), 8), :] = dot_cols(
                    picks, jnp.concatenate(coef, axis=0)
                )

        chunk_sweep(count, body, spread, even, odd)

    for d in range(2):

        @pl.when(pl.program_id(0) == d)
        def _():
            one_direction(d == 1)


def block_of(length):
    return math.gcd(length, 128)


def scan_states(dt, x, bc, rate):
    two, slots, length, width = dt.shape
    states = rate.shape[1]
    hidden_size = two * slots * length * states * width
    block = block_of(length)
    blocks = length // block

    def where(d, i):
        return (d, 0, jnp.where(d == 1, blocks - 1 - i, i), 0)

    return pl.pallas_call(
        functools.partial(states_kernel, block // chunk),
        grid=(two, blocks),
        in_specs=[
            pl.BlockSpec((1, slots, block, width), where),
            pl.BlockSpec((1, slots, block, width), where),
            pl.BlockSpec((1, slots, block, 2 * chunk * states), where),
            pl.BlockSpec((1, states, width), lambda d, i: (d, 0, 0)),
        ],
        out_specs=[
            pl.BlockSpec((1, slots, block, width), where),
            pl.BlockSpec((1, slots, block * states, width), where),
        ],
        out_shape=[
            jax.ShapeDtypeStruct((two, slots, length, width), f32),
            jax.ShapeDtypeStruct((two, slots, length * states, width), bf16),
        ],
        scratch_shapes=[
            pltpu.VMEM((slots, states, width), f32),
            pltpu.VMEM((slots, chunk * states, 2 * lanes), f32),
            pltpu.VMEM((slots, chunk * states, 2 * lanes), f32),
        ],
        compiler_params=pltpu.CompilerParams(vmem_limit_bytes=48 * 2**20),
        cost_estimate=pl.CostEstimate(
            flops=64 * 10**9, bytes_accessed=80 * 2**20, transcendentals=hidden_size
        ),
        name="scan_states",
    )(dt, x, bc, rate)


def scan_adjoint(dt, x, bc, rate, g, h):
    two, slots, length, width = dt.shape
    states = rate.shape[1]
    hidden_size = two * slots * length * states * width
    block = block_of(length)
    blocks = length // block

    def at(d, i):
        return jnp.where(d == 1, i, blocks - 1 - i)

    def where(d, i):
        return (d, 0, at(d, i), 0)

    def edge(d, i):
        mine = at(d, i) * block
        return (d, 0, jnp.clip(jnp.where(d == 1, mine + block, mine - 1), 0, length - 1), 0)

    return pl.pallas_call(
        functools.partial(adjoint_kernel, block // chunk),
        grid=(two, blocks),
        in_specs=[
            pl.BlockSpec((1, slots, block, width), where),
            pl.BlockSpec((1, slots, block, width), where),
            pl.BlockSpec((1, slots, block, 2 * chunk * states), where),
            pl.BlockSpec((1, states, width), lambda d, i: (d, 0, 0)),
            pl.BlockSpec((slots, block, width), lambda d, i: (0, at(d, i), 0)),
            pl.BlockSpec((1, slots, block * states, width), where),
            pl.BlockSpec((1, slots, states, width), edge),
        ],
        out_specs=[
            pl.BlockSpec((1, slots, block, width), where),
            pl.BlockSpec((1, slots, block, width), where),
            pl.BlockSpec((1, slots, block // chunk * 8, chunk * states), where),
            pl.BlockSpec((1, slots, states, width), lambda d, i: (d, 0, 0, 0)),
        ],
        out_shape=[
            jax.ShapeDtypeStruct((two, slots, length, width), f32),
            jax.ShapeDtypeStruct((two, slots, length, width), f32),
            jax.ShapeDtypeStruct((two, slots, length // chunk * 8, chunk * states), f32),
            jax.ShapeDtypeStruct((two, slots, states, width), f32),
        ],
        scratch_shapes=[
            pltpu.VMEM((slots, states, width), f32),
            pltpu.VMEM((slots, chunk * states, 2 * lanes), f32),
            pltpu.VMEM((slots, chunk * states, 2 * lanes), f32),
        ],
        compiler_params=pltpu.CompilerParams(vmem_limit_bytes=48 * 2**20),
        cost_estimate=pl.CostEstimate(
            flops=100 * 10**9, bytes_accessed=100 * 2**20, transcendentals=hidden_size
        ),
        name="scan_adjoint",
    )(dt, x, bc, rate, g, h, h)


def coefficient_rows(selection, rank, states):
    rows, width = selection.shape[1:]
    span = chunk * states
    col = jnp.arange(2 * span)
    origin = rank + (col // span) * states + col % states
    copies = (jnp.arange(width)[:, None] == origin[None, :]).astype(bf16)
    own = (jnp.arange(rows) % chunk)[:, None] == ((col % span) // states)[None, :]
    placed = jnp.einsum("drk,kc->drc", selection, copies, preferred_element_type=f32)
    return jnp.where(own, placed, 0.0).astype(bf16)


def widen(v, width):
    short = width - v.shape[-1]
    return v if short == 0 else jnp.pad(v, ((0, 0),) * (v.ndim - 1) + ((0, short),))


def remote(src, dst, sends, recvs, slot, axis, to):
    return pltpu.make_async_remote_copy(
        src_ref=src,
        dst_ref=dst,
        send_sem=sends.at[slot],
        recv_sem=recvs.at[slot],
        device_id={axis: to},
        device_id_type=pl.DeviceIdType.MESH,
    )


def each(first, last, body):
    def run(k, carry):
        body(k)
        return carry

    lax.fori_loop(first, last, run, 0)


def greet(peers):
    barrier = pltpu.get_barrier_semaphore()
    total = 0
    for axis, me, count in peers:

        def hello(k):
            pl.semaphore_signal(
                barrier,
                inc=1,
                device_id={axis: lax.rem(me + k, count)},
                device_id_type=pl.DeviceIdType.MESH,
            )

        each(1, count, hello)
        total += count - 1
    pl.semaphore_wait(barrier, total)


def total_kernel(line, v_ref, o_ref, pairbox, stage, inbox, *sems):
    pair_send, pair_recv, sum_send, sum_recv, out_send, out_recv, fwd_send, fwd_recv = sems
    me = lax.axis_index("seq")
    pos, core = me // 2, lax.rem(me, 2)
    partner = me + 1 - 2 * core
    barrier = pltpu.get_barrier_semaphore()

    def hello(to):
        pl.semaphore_signal(
            barrier, inc=1, device_id={"seq": to}, device_id_type=pl.DeviceIdType.MESH
        )

    hello(partner)
    each(1, line, lambda k: hello(lax.rem(pos + k, line) * 2 + core))
    pl.semaphore_wait(barrier, line)

    pair = remote(v_ref.at[:, :, 1 - core], pairbox, pair_send, pair_recv, 0, "seq", partner)
    pair.start()
    pair.wait_recv()

    def own(q):
        return v_ref[:, q, core].astype(f32) + pairbox[:, q].astype(f32)

    def summand(k):
        q = lax.rem(pos + k, line)
        return remote(
            stage.at[q], inbox.at[pos], sum_send, sum_recv, k - 1, "seq", q * 2 + core
        )

    def send(k):
        q = lax.rem(pos + k, line)
        stage[q] = own(q).astype(bf16)
        summand(k).start()

    each(1, line, send)

    def source(k):
        return lax.rem(pos - k + line, line)

    def arrived(k, total):
        q = source(k)
        remote(stage.at[q], inbox.at[q], sum_send, sum_recv, k - 1, "seq", partner).wait_recv()
        return total + inbox[q].astype(f32)

    total = lax.fori_loop(1, line, arrived, own(pos))
    o_ref[:, pos, core] = total.astype(bf16)

    def result(k):
        mine = o_ref.at[:, pos, core]
        return remote(
            mine, mine, out_send, out_recv, k - 1, "seq", lax.rem(pos + k, line) * 2 + core
        )

    def forward(k):
        block = o_ref.at[:, source(k), core]
        return remote(block, block, fwd_send, fwd_recv, k, "seq", partner)

    each(1, line, lambda k: result(k).start())
    forward(0).start()

    def pass_on(k):
        block = o_ref.at[:, source(k), core]
        remote(block, block, out_send, out_recv, k - 1, "seq", partner).wait_recv()
        forward(k).start()

    each(1, line, pass_on)

    def finish(k):
        block = o_ref.at[:, source(k), 1 - core]
        remote(block, block, fwd_send, fwd_recv, k, "seq", partner).wait_recv()
        forward(k).wait_send()

    each(0, line, finish)
    pair.wait_send()

    def drain(k):
        summand(k).wait_send()
        result(k).wait_send()

    each(1, line, drain)


def summed_everywhere(v, call):
    batch, length, width = v.shape
    shares = lax.axis_size("seq")
    line, rows = shares // 2, length // shares
    vmem = pl.BlockSpec(memory_space=pltpu.VMEM)
    dma = pltpu.SemaphoreType.DMA
    blocks = v.reshape(batch, line, 2, rows, width)
    out = pl.pallas_call(
        functools.partial(total_kernel, line),
        in_specs=[vmem],
        out_specs=vmem,
        out_shape=jax.ShapeDtypeStruct(blocks.shape, bf16),
        scratch_shapes=[
            pltpu.VMEM((batch, line, rows, width), bf16),
            pltpu.VMEM((line, batch, rows, width), bf16),
            pltpu.VMEM((line, batch, rows, width), bf16),
            dma((1,)),
            dma((1,)),
            dma((line,)),
            dma((line,)),
            dma((line,)),
            dma((line,)),
            dma((line,)),
            dma((line,)),
        ],
        compiler_params=pltpu.CompilerParams(
            collective_id=call, has_side_effects=True, vmem_limit_bytes=40 * 2**20
        ),
        cost_estimate=pl.CostEstimate(flops=25 * 10**9, bytes_accessed=2**20, transcendentals=0),
        name="sum_" + str(call),
    )(blocks)
    return out.reshape(v.shape)


def head_kernel(w_ref, mod_ref, box_ref, out_ref, parts, *sems):
    keep, w_send, w_recv, f_send, f_recv, m_send, m_recv = sems
    shares, peers = box_ref.shape[0], box_ref.shape[1]
    me, item = lax.axis_index("seq"), lax.axis_index("item")
    greet((("seq", me, shares), ("item", item, peers)))

    def modulation(k):
        return remote(
            mod_ref, parts.at[k - 1], m_send, m_recv, k - 1, "seq", lax.rem(me + k, shares)
        )

    def weight(k):
        to = lax.rem(me + k, shares)
        return remote(w_ref.at[to], box_ref.at[me, item], w_send, w_recv, k, "seq", to)

    each(1, shares, lambda k: weight(k).start())
    each(1, shares, lambda k: modulation(k).start())
    own = pltpu.make_async_copy(w_ref.at[me], box_ref.at[me, item], keep)
    own.start()

    def forward(k, t):
        block = box_ref.at[lax.rem(me - k + shares, shares), item]
        return remote(
            block, block, f_send, f_recv, k * (peers - 1) + t - 1, "item", lax.rem(item + t, peers)
        )

    own.wait()
    each(1, peers, lambda t: forward(0, t).start())

    def pass_on(k):
        source = lax.rem(me - k + shares, shares)
        block = box_ref.at[source, item]
        remote(block, block, w_send, w_recv, k, "seq", source).wait_recv()
        each(1, peers, lambda t: forward(k, t).start())

    each(1, shares, pass_on)

    def add(k, total):
        modulation(k).wait_recv()
        return total + parts[k - 1]

    out_ref[...] = lax.fori_loop(1, shares, add, mod_ref[...])

    def finish(k):
        def one(t):
            source = lax.rem(item - t + peers, peers)
            block = box_ref.at[lax.rem(me - k + shares, shares), source]
            remote(
                block, block, f_send, f_recv, k * (peers - 1) + t - 1, "item", source
            ).wait_recv()
            forward(k, t).wait_send()

        each(1, peers, one)

    each(0, shares, finish)

    def drain(k):
        weight(k).wait_send()
        modulation(k).wait_send()

    each(1, shares, drain)


def input_columns(blocks, modulation):
    shares, peers = lax.axis_size("seq"), lax.axis_size("item")
    vmem, anywhere = pl.BlockSpec(memory_space=pltpu.VMEM), pl.BlockSpec(memory_space=pl.ANY)
    dma = pltpu.SemaphoreType.DMA
    return pl.pallas_call(
        head_kernel,
        in_specs=[anywhere, vmem],
        out_specs=[anywhere, vmem],
        out_shape=[
            jax.ShapeDtypeStruct((shares, peers) + blocks.shape[1:], bf16),
            jax.ShapeDtypeStruct(modulation.shape, f32),
        ],
        scratch_shapes=[
            pltpu.VMEM((shares - 1,) + modulation.shape, f32),
            dma,
            dma((shares,)),
            dma((shares,)),
            dma((shares * (peers - 1),)),
            dma((shares * (peers - 1),)),
            dma((shares,)),
            dma((shares,)),
        ],
        compiler_params=pltpu.CompilerParams(collective_id=1, has_side_effects=True),
        cost_estimate=pl.CostEstimate(flops=40 * 10**9, bytes_accessed=2**20, transcendentals=0),
        name="input_columns",
    )(blocks, modulation)


def tail_kernel(
    g_ref, small_ref, select_ref, g_out, small_out, select_out, g_box, small_box, select_box, g_stage, *sems
):
    (a_send, a_recv, s_send, s_recv, c_send, c_recv, z_send, z_recv, y_send, y_recv) = sems[:10]
    f_send, f_recv, h_send, h_recv, e_send, e_recv = sems[10:]
    shares, peers = g_ref.shape[0], g_ref.shape[1]
    me, item = lax.axis_index("seq"), lax.axis_index("item")
    greet((("seq", me, shares), ("item", item, peers)))

    def other(t):
        return lax.rem(item + t, peers)

    def origin(t):
        return lax.rem(item - t + peers, peers)

    def ahead(k):
        return lax.rem(me + k, shares)

    def behind(k):
        return lax.rem(me - k + shares, shares)

    def flat(k, t):
        return k * (peers - 1) + t - 1

    def share_small(t):
        return remote(
            small_ref.at[other(t)], small_box.at[t - 1], s_send, s_recv, t - 1, "item", other(t)
        )

    def share_select(t):
        return remote(
            select_ref.at[other(t)], select_box.at[t - 1], c_send, c_recv, t - 1, "item", other(t)
        )

    def share_in(k, t):
        p = ahead(k)
        return remote(
            g_ref.at[p, other(t)], g_box.at[t - 1, p], a_send, a_recv, flat(k, t), "item", other(t)
        )

    each(1, peers, lambda t: share_small(t).start())
    each(1, shares, lambda k: each(1, peers, lambda t: share_in(k, t).start()))
    each(1, peers, lambda t: share_in(0, t).start())
    each(1, peers, lambda t: share_select(t).start())

    def add_small(t, total):
        share_small(t).wait_recv()
        return total + small_box[t - 1].astype(f32)

    small_out[item, me] = lax.fori_loop(
        1, peers, add_small, small_ref[item].astype(f32)
    ).astype(bf16)

    def spread_small(k):
        block = small_out.at[item, me]
        return remote(block, block, y_send, y_recv, k, "seq", ahead(k))

    each(1, shares, lambda k: spread_small(k).start())

    def sum_in(k):
        p = ahead(k)

        def add(t, total):
            share_in(k, t).wait_recv()
            return total + g_box[t - 1, p].astype(f32)

        return lax.fori_loop(1, peers, add, g_ref[p, item].astype(f32)).astype(bf16)

    def place_in(k):
        return remote(
            g_stage.at[k], g_out.at[item, me], z_send, z_recv, k, "seq", ahead(k)
        )

    def turn(k):
        g_stage[k] = sum_in(k)
        place_in(k).start()

    each(1, shares, turn)
    g_out[item, me] = sum_in(0)

    def forward_in(k, t):
        block = g_out.at[item, behind(k)]
        return remote(block, block, f_send, f_recv, flat(k, t), "item", other(t))

    def forward_small(k, t):
        block = small_out.at[item, behind(k)]
        return remote(block, block, h_send, h_recv, flat(k, t), "item", other(t))

    each(1, peers, lambda t: forward_in(0, t).start())
    each(1, peers, lambda t: forward_small(0, t).start())

    def add_select(t, total):
        share_select(t).wait_recv()
        return total + select_box[t - 1].astype(f32)

    select_out[item] = lax.fori_loop(
        1, peers, add_select, select_ref[item].astype(f32)
    ).astype(bf16)

    def forward_select(t):
        block = select_out.at[item]
        return remote(block, block, e_send, e_recv, t - 1, "item", other(t))

    each(1, peers, lambda t: forward_select(t).start())

    def pass_on(k):
        block = g_out.at[item, behind(k)]
        remote(block, block, z_send, z_recv, k, "seq", behind(k)).wait_recv()
        each(1, peers, lambda t: forward_in(k, t).start())
        little = small_out.at[item, behind(k)]
        remote(little, little, y_send, y_recv, k, "seq", behind(k)).wait_recv()
        each(1, peers, lambda t: forward_small(k, t).start())

    each(1, shares, pass_on)

    def finish(k):
        def one(t):
            block = g_out.at[origin(t), behind(k)]
            remote(block, block, f_send, f_recv, flat(k, t), "item", other(t)).wait_recv()
            little = small_out.at[origin(t), behind(k)]
            remote(little, little, h_send, h_recv, flat(k, t), "item", other(t)).wait_recv()
            forward_in(k, t).wait_send()
            forward_small(k, t).wait_send()
            share_in(k, t).wait_send()

        each(1, peers, one)

    each(0, shares, finish)

    def finish_item(t):
        block = select_out.at[origin(t)]
        remote(block, block, e_send, e_recv, t - 1, "item", other(t)).wait_recv()
        forward_select(t).wait_send()
        share_small(t).wait_send()
        share_select(t).wait_send()

    each(1, peers, finish_item)

    def finish_seq(k):
        spread_small(k).wait_send()
        place_in(k).wait_send()

    each(1, shares, finish_seq)


def weight_sums(g, small, select):
    shares, peers = g.shape[:2]
    vmem = pl.BlockSpec(memory_space=pltpu.VMEM)
    dma = pltpu.SemaphoreType.DMA
    some = peers - 1
    sizes = [shares * some] * 2 + [some] * 4 + [shares] * 4 + [shares * some] * 4 + [some] * 2
    return pl.pallas_call(
        tail_kernel,
        in_specs=[vmem] * 3,
        out_specs=[vmem] * 3,
        out_shape=[
            jax.ShapeDtypeStruct((peers, shares) + g.shape[2:], bf16),
            jax.ShapeDtypeStruct((peers, shares) + small.shape[1:], bf16),
            jax.ShapeDtypeStruct(select.shape, bf16),
        ],
        scratch_shapes=[
            pltpu.VMEM((some, shares) + g.shape[2:], bf16),
            pltpu.VMEM((some,) + small.shape[1:], bf16),
            pltpu.VMEM((some,) + select.shape[1:], bf16),
            pltpu.VMEM((shares,) + g.shape[2:], bf16),
        ]
        + [dma((size,)) for size in sizes],
        compiler_params=pltpu.CompilerParams(
            collective_id=2, has_side_effects=True, vmem_limit_bytes=40 * 2**20
        ),
        cost_estimate=pl.CostEstimate(flops=60 * 10**9, bytes_accessed=2**20, transcendentals=0),
        name="weight_sums",
    )(g, small, select)


def modulation_kernel(v_ref, out_ref, parts, m_send, m_recv, f_send, f_recv):
    shares = parts.shape[0] + 1
    peers = out_ref.shape[0]
    me, item = lax.axis_index("seq"), lax.axis_index("item")
    greet((("seq", me, shares), ("item", item, peers)))

    def part(k):
        return remote(v_ref, parts.at[k - 1], m_send, m_recv, k - 1, "seq", lax.rem(me + k, shares))

    each(1, shares, lambda k: part(k).start())

    def add(k, total):
        part(k).wait_recv()
        return total + parts[k - 1]

    out_ref[item] = lax.fori_loop(1, shares, add, v_ref[...])

    def forward(t):
        block = out_ref.at[item]
        return remote(block, block, f_send, f_recv, t - 1, "item", lax.rem(item + t, peers))

    each(1, peers, lambda t: forward(t).start())

    def finish(t):
        source = lax.rem(item - t + peers, peers)
        block = out_ref.at[source]
        remote(block, block, f_send, f_recv, t - 1, "item", source).wait_recv()
        forward(t).wait_send()

    each(1, peers, finish)
    each(1, shares, lambda k: part(k).wait_send())


def modulation_sums(v):
    shares, peers = lax.axis_size("seq"), lax.axis_size("item")
    vmem = pl.BlockSpec(memory_space=pltpu.VMEM)
    dma = pltpu.SemaphoreType.DMA
    return pl.pallas_call(
        modulation_kernel,
        in_specs=[vmem],
        out_specs=vmem,
        out_shape=jax.ShapeDtypeStruct((peers,) + v.shape, f32),
        scratch_shapes=[
            pltpu.VMEM((shares - 1,) + v.shape, f32),
            dma((shares,)),
            dma((shares,)),
            dma((peers,)),
            dma((peers,)),
        ],
        compiler_params=pltpu.CompilerParams(collective_id=3, has_side_effects=True),
        cost_estimate=pl.CostEstimate(flops=10 * 10**9, bytes_accessed=2**20, transcendentals=0),
        name="modulation_sums",
    )(v)


def filter_windows(x, taps, reverse):
    rim = taps - 1
    length = x.shape[1]
    padded = jnp.pad(x, ((0, 0), (rim, rim), (0, 0)))
    starts = [2 * rim - j if reverse else j for j in range(taps)]
    return [padded[:, s : s + length] for s in starts]


def per_device(
    tokens,
    timestep,
    slot_item,
    slot_valid,
    cotangent,
    in_weight,
    out_weight,
    select_weight,
    modulation_weight,
    delta_weight,
    filter_weight,
    filter_bias,
    delta_bias,
    decay_log,
    skip_gain,
    modulation_bias,
):
    slots, local, model = tokens.shape
    shares = lax.axis_size("seq")
    place = lax.axis_index("seq")
    rank, inner = delta_weight.shape[0], delta_weight.shape[1] // 2
    states = decay_log.shape[0]
    select = select_weight.shape[1] // 2
    taps = filter_weight.shape[0]
    rim = taps - 1
    length = local * shares
    rows = slots * length
    mine = inner // shares
    padded_width = -(-mine // lanes) * lanes
    shard_rows = modulation_weight.shape[0]
    items = timestep.shape[0]

    def own_columns(v):
        split = v.reshape(v.shape[:-1] + (2, shares, mine))
        return lax.dynamic_index_in_dim(split, place, split.ndim - 2, False)

    first_slot = lax.axis_index("item") * slots
    valid = lax.dynamic_slice_in_dim(slot_valid, first_slot, slots).astype(f32)[:, None, None]
    chooser = (slot_item[:, None] == jnp.arange(items, dtype=jnp.int32)[None, :]).astype(bf16)
    embedded = jnp.dot(chooser, timestep, preferred_element_type=f32)
    condition = jax.nn.silu(embedded).astype(bf16)
    own_features = lax.dynamic_slice_in_dim(condition, place * shard_rows, shard_rows, 1)
    own_condition = lax.dynamic_slice_in_dim(own_features, first_slot, slots, 0)
    modulation_part = jnp.dot(own_condition, modulation_weight, preferred_element_type=f32)
    peers = lax.axis_size("item")
    share_rows = in_weight.shape[0] // peers
    own_rows = lax.dynamic_slice_in_dim(
        in_weight, lax.axis_index("item") * share_rows, share_rows, 0
    )
    own_rows = jnp.moveaxis(own_rows.reshape(share_rows, 2, shares, mine), 2, 0)
    own_in, modulation = input_columns(
        own_rows.reshape(shares, share_rows, 2 * mine), modulation_part
    )
    own_in = own_in.reshape(model, 2 * mine)
    modulation = modulation + modulation_bias.astype(f32)[None, :]
    shift = modulation[:, None, :model]
    scale = modulation[:, None, model : 2 * model]
    gate = modulation[:, None, 2 * model :]

    all_tokens = lax.all_gather(tokens, "seq", axis=1, tiled=True)
    source = all_tokens.astype(f32)
    centered = source - jnp.mean(source, axis=-1, keepdims=True)
    spread = lax.rsqrt(jnp.mean(centered * centered, axis=-1, keepdims=True) + epsilon)
    mixed_in = (centered * spread * (1.0 + scale) + shift).astype(bf16).reshape(rows, model)
    projected = jnp.dot(mixed_in, own_in, preferred_element_type=f32).reshape(
        slots, length, 2 * mine
    )
    x_half = projected[..., :mine].astype(bf16)
    gate_half = projected[..., mine:]

    tap_weight = own_columns(filter_weight).astype(f32)
    tap_bias = own_columns(filter_bias).astype(f32)
    step_weight = own_columns(delta_weight)
    step_bias = own_columns(delta_bias)
    rate = -jnp.exp(own_columns(decay_log))
    skip = own_columns(skip_gain)

    filtered, activated, partial = [], [], []
    for d in range(2):
        f = tap_bias[d]
        for j, window in enumerate(filter_windows(x_half, taps, d == 1)):
            f = f + tap_weight[j, d] * window.astype(f32)
        a = jax.nn.silu(f).astype(bf16)
        filtered.append(f)
        activated.append(a)
        partial.append(
            jnp.dot(
                a.reshape(rows, mine),
                select_weight[:, d * select : (d + 1) * select],
                preferred_element_type=f32,
            )
        )
    selection = summed_everywhere(
        jnp.stack(partial).astype(bf16).reshape(2 * slots, length, select), 4
    ).reshape(2, rows, select)
    selection, late_cotangent = lax.optimization_barrier((selection, cotangent))
    all_cotangent = lax.all_gather(late_cotangent, "seq", axis=1, tiled=True)
    delta_rank = selection[:, :, :rank]
    bc = coefficient_rows(selection, rank, states).reshape(2, slots, length, -1)
    step_pre = [
        jnp.dot(delta_rank[d], step_weight[:, d], preferred_element_type=f32) + step_bias[d]
        for d in range(2)
    ]
    step = jnp.stack([jax.nn.softplus(p) for p in step_pre]).reshape(2, slots, length, mine)
    active = jnp.stack(activated)
    wide_step = widen(step, padded_width)
    wide_active = widen(active, padded_width)
    wide_rate = widen(jnp.swapaxes(rate, 0, 1) * log2e, padded_width)
    scanned, hidden = scan_states(wide_step, wide_active, bc, wide_rate)
    scanned = scanned[..., :mine]
    scanned_sum = scanned[0] + scanned[1]
    for d in range(2):
        scanned_sum = scanned_sum + skip[d] * activated[d].astype(f32)
    silu_gate = jax.nn.silu(gate_half)
    mixed_out = (scanned_sum * silu_gate).astype(bf16).reshape(rows, mine)
    own_cotangent = cotangent.astype(f32)

    grad_branch = (
        (valid * gate * all_cotangent.astype(f32)).astype(bf16).reshape(rows, model)
    )
    grad_mixed = dot_cols(grad_branch, out_weight).reshape(slots, length, mine)
    grad_scanned = grad_mixed * silu_gate
    grad_gate_half = grad_mixed * scanned_sum * silu_slope(gate_half)
    grad_out = dot_rows(mixed_out, grad_branch).astype(bf16)
    branch_part = (
        jnp.dot(mixed_out, out_weight, preferred_element_type=f32)
        .astype(bf16)
        .reshape(slots, length, model)
    )
    branch_part, grad_out, scan_grad = lax.optimization_barrier(
        (branch_part, grad_out, grad_scanned)
    )
    branch_part = lax.psum_scatter(branch_part, "seq", scatter_dimension=1, tiled=True)
    grad_out, branch_part = lax.optimization_barrier((grad_out, branch_part))
    grad_out = lax.psum(grad_out, "item")
    grad_step, grad_input, grad_coef, grad_rate = scan_adjoint(
        wide_step, wide_active, bc, wide_rate, widen(scan_grad, padded_width), hidden
    )
    grad_decay = jnp.sum(grad_rate, axis=1)[..., :mine] * ln2
    grad_coef = grad_coef.reshape(2, slots, length // chunk, 8, chunk, states)[:, :, :, :2]
    grad_coef = jnp.moveaxis(grad_coef, 3, 4).reshape(2, rows, 2 * states)
    parts = []
    grad_skip, grad_step_bias, grad_delta = [], [], []
    for d in range(2):
        grad_skip.append(jnp.sum(grad_scanned * activated[d].astype(f32), axis=(0, 1)))
        grad_pre = grad_step[d, ..., :mine].reshape(rows, mine) * jax.nn.sigmoid(step_pre[d])
        low = grad_pre.astype(bf16)
        grad_step_bias.append(jnp.sum(grad_pre, axis=0))
        grad_delta.append(dot_rows(delta_rank[d], low))
        parts.append(jnp.concatenate([dot_cols(low, step_weight[:, d]), grad_coef[d]], axis=1))
    parts[1], grad_out, branch_part = lax.optimization_barrier((parts[1], grad_out, branch_part))
    grad_selection = summed_everywhere(
        jnp.stack(parts).astype(bf16).reshape(2 * slots, length, select), 5
    ).reshape(2, rows, select)
    grad_x = jnp.zeros((slots, length, mine), f32)
    grad_select, grad_taps, grad_tap_bias = [], [], []
    for d in range(2):
        block = select_weight[:, d * select : (d + 1) * select]
        grad_select.append(dot_rows(activated[d].reshape(rows, mine), grad_selection[d]))
        grad_active = (
            grad_input[d, ..., :mine]
            + skip[d] * grad_scanned
            + dot_cols(grad_selection[d], block).reshape(slots, length, mine)
        )
        grad_filtered = grad_active * silu_slope(filtered[d])
        grad_tap_bias.append(jnp.sum(grad_filtered, axis=(0, 1)))
        windows = filter_windows(x_half, taps, d == 1)
        grad_taps.append(
            jnp.stack([jnp.sum(grad_filtered * w.astype(f32), axis=(0, 1)) for w in windows])
        )
        for j, window in enumerate(filter_windows(grad_filtered, taps, d == 0)):
            grad_x = grad_x + tap_weight[j, d] * window
    grad_projected = (
        jnp.concatenate([grad_x, grad_gate_half], axis=2).astype(bf16).reshape(rows, 2 * mine)
    )
    grad_mixed_in = lax.psum_scatter(
        dot_cols(grad_projected, own_in).astype(bf16).reshape(slots, length, model),
        "seq",
        scatter_dimension=1,
        tiled=True,
    ).astype(f32)
    grad_in = dot_rows(mixed_in, grad_projected).astype(bf16)
    own_source = tokens.astype(f32)
    own_centered = own_source - jnp.mean(own_source, axis=-1, keepdims=True)
    own_spread = lax.rsqrt(
        jnp.mean(own_centered * own_centered, axis=-1, keepdims=True) + epsilon
    )
    normed = own_centered * own_spread
    grad_normed = grad_mixed_in * (1.0 + scale)
    grad_source = own_spread * (
        grad_normed
        - jnp.mean(grad_normed, axis=-1, keepdims=True)
        - normed * jnp.mean(grad_normed * normed, axis=-1, keepdims=True)
    )
    grad_tokens = (own_cotangent + grad_source).astype(bf16)
    branch = branch_part.astype(f32)
    output = (tokens.astype(f32) + valid * gate * branch).astype(bf16)
    grad_gate = jnp.sum(valid * own_cotangent * branch, axis=1)
    grad_modulation = jnp.concatenate(
        [jnp.sum(grad_mixed_in, axis=1), jnp.sum(grad_mixed_in * normed, axis=1), grad_gate], axis=1
    )
    grad_modulation = modulation_sums(grad_modulation).reshape(-1, 3 * model)
    grad_modulation_weight = lax.dot_general(
        own_features.astype(f32),
        grad_modulation,
        (((0,), (0,)), ((), ())),
        precision=lax.Precision.HIGHEST,
        preferred_element_type=f32,
    )
    small = jnp.concatenate(
        [
            jnp.stack(grad_delta, 1),
            jnp.stack(grad_taps, 1),
            jnp.stack(grad_tap_bias)[None],
            jnp.stack(grad_step_bias)[None],
            jnp.swapaxes(grad_decay, 0, 1),
            jnp.stack(grad_skip)[None],
        ],
        axis=0,
    )
    small_rows = small.shape[0]
    share = -(-small_rows // (16 * peers)) * 16
    small = jnp.pad(
        small.astype(bf16).reshape(small_rows, 2 * mine), ((0, peers * share - small_rows), (0, 0))
    )
    grad_select = jnp.concatenate(grad_select, axis=1).astype(bf16)
    grad_in, small, grad_select = weight_sums(
        grad_in.reshape(shares, peers, share_rows, 2 * mine),
        small.reshape(peers, share, 2 * mine),
        grad_select.reshape(peers, mine // peers, 2 * select),
    )
    grad_in = grad_in.reshape(peers, shares, share_rows, 2, mine)
    grad_in = jnp.transpose(grad_in, (0, 2, 3, 1, 4)).reshape(peers * share_rows, 2 * inner)
    grad_select = grad_select.reshape(mine, 2 * select)
    small = small.reshape(peers, shares, share, 2, mine)
    small = jnp.transpose(small, (0, 2, 3, 1, 4)).reshape(peers * share, 2 * inner).astype(f32)
    cuts = [rank, rank + taps, rank + taps + 1, rank + taps + 2, rank + taps + 2 + states]
    return (
        output,
        grad_tokens,
        grad_in.astype(f32),
        grad_out.astype(f32),
        grad_select.astype(f32),
        grad_modulation_weight,
        small[: cuts[0]],
        small[cuts[0] : cuts[1]],
        small[cuts[1]],
        small[cuts[2]],
        small[cuts[3] : cuts[4]],
        small[cuts[4]],
        jnp.sum(grad_modulation, axis=0),
    )


def solution(mesh):
    tokens, rows, same = P("item", "seq", None), P("seq", None), P()
    return jax.shard_map(
        per_device,
        mesh=mesh,
        in_specs=(tokens, same, same, same, tokens, rows, rows, rows, rows) + (same,) * 7,
        out_specs=(tokens, tokens, rows, rows, rows, rows) + (same,) * 7,
        check_vma=False,
    )
```

time: 2270 us -> 666 us (0.29); the launches traced: 2240 us -> 655 us
  other arithmetic: 863 us -> 41.8 us
  waiting for transfers between devices: 867 us -> 79.5 us
  Pallas kernels: 0 us -> 346 us
  local copies, waits for them, and re-layouts: 306 us -> 90.7 us
  blocking collectives: 63.7 us -> 0 us
  loops' own time: 25.5 us -> 0 us
    reduce_sum x218 -> x7, other arithmetic: 370 us -> 10.1 us  [the longest x2 4.04 us: per_device(): grad_step_bias.append(jnp.sum(grad_pre, axis=0))]
    pallas_call x0 -> x7, Pallas kernels: none -> 346 us  [the longest x1 90.6 us: scan_adjoint(): pl.pallas_call(functools.partial(adjoint_kernel, block // chunk), grid=(t...]
    psum x3 -> x1, waiting for transfers between devices: 386 us -> 45.4 us  [per_device(): grad_out = lax.psum(grad_out, 'item')]
    all_gather x11 -> x2, waiting for transfers between devices: 271 us -> 33.4 us  [the longest x1 33.4 us: per_device(): all_tokens = lax.all_gather(tokens, 'seq', axis=1, tiled=True)]
    reduce_scatter x2, waiting for transfers between devices: 206 us -> 0.01 us  [the longest x1 0.01 us: per_device(): lax.psum_scatter(branch_part, 'seq', scatter_dimension=1, tiled=True)]
    while x240 -> x0, other arithmetic: 192 us -> none
    mul x91 -> x2, other arithmetic: 110 us -> 0.09 us  [the longest x1 0.08 us: per_device(): output = (tokens.astype(f32) + valid * gate * branch).astype(bf16)]
    add x49 -> x1, other arithmetic: 101 us -> 0.79 us  [per_device(): modulation = modulation + modulation_bias.astype(f32)[None, :]]
where the time goes in v1:
time: 666 us; the launch traced here: 655 us
  Pallas kernels  346 us (52%)
  local copies, waits for them, and re-layouts  90.7 us (14%)
  matrix products  81.3 us (12%)
  waiting for transfers between devices  79.5 us (12%)
  other arithmetic  41.8 us (6%)
  between operations  15.9 us (2%)
    pallas_call x1, Pallas kernels, scan_adjoint(): pl.pallas_call(functools.partial(adjoint_kernel, block // chunk), grid=(t...  90.6 us
    pallas_call x1, Pallas kernels, weight_sums(): pl.pallas_call(tail_kernel, in_specs=[vmem] * 3, out_specs=[vmem] * 3, ou...  85.8 us
    pallas_call x1, Pallas kernels, scan_states(): pl.pallas_call(functools.partial(states_kernel, block // chunk), grid=(tw...  55.9 us
    pallas_call x2, Pallas kernels, summed_everywhere(): pl.pallas_call(functools.partial(total_kernel, line), in_specs=[vmem], ou...  54.2 us
    psum x1, waiting for transfers between devices, per_device(): grad_out = lax.psum(grad_out, 'item')  45.4 us
    pallas_call x1, Pallas kernels, input_columns(): pl.pallas_call(head_kernel, in_specs=[anywhere, vmem], out_specs=[anywher...  44.9 us
    dot_general x6, matrix products, dot_cols(): lax.dot_general(a, b, (((1,), (1,)), ((), ())), preferred_element_type=f32)  33.7 us
    all_gather x1, waiting for transfers between devices, per_device(): all_tokens = lax.all_gather(tokens, 'seq', axis=1, tiled=True)  33.4 us
  transfers between devices with their start and end apart: 5, of which 2 were waited for; matrix products, arithmetic and copies ran while one was open for 19% of the time, Pallas kernels for 42%

profile of v1, /device:TPU:0, one launch (start us, length us, event | category | flops | bytes accessed | tf_op | source)
XLA Modules:
  0.0 655.2 jit_solution(4542578695535973577)
XLA Ops:
  9.5 1.2 reshape.280.w_ref
  12.3 44.9 %input_columns.1 = (bf16[8,4,48,768]{3,2,1,0:T(8,128)(2,1)}, f32[2,4608]{1,0:T(2,128)}) custom-call(bf16[8,48,768]{2,1,0:T(8,128)(2,1)} %reshape.280.w_ref, f32[2,4608]{1,0:T(2,128)} %fusion.121.mod_ref), custom_call_target="tpu_custom_call" | custom-call | flops 40000000000 | bytes 1048576 | tf_op jit(solution)/shard_map/input_columns/pallas_call | solution.py:586
  58.0 33.4 %all-gather.3.cloned.1.call-done = bf16[2,1024,1536]{2,1,0:T(8,128)(2,1)} async-done(((bf16[2,128,1536]{2,1,0:T(8,128)(2,1)}), bf16[2,1024,1536]{2,1,0:T(8,128)(2,1)}) %all-gather.3.cloned.1.call-update) | async-done | bytes 6291472 | tf_op jit(solution)/shard_map/all_gather | solution.py:908
  91.4 3.8 convert_reduce_fusion
  96.0 1.8 fusion.2
  97.9 6.2 fusion.9
  104.4 4.4 multiply_convert_fusion.6
  110.1 26.8 %sum_4.1 = bf16[4,4,2,128,128]{4,3,2,1,0:T(8,128)(2,1)S(1)} custom-call(bf16[4,4,2,128,128]{4,3,2,1,0:T(8,128)(2,1)S(1)} %bitcast.217), custom_call_target="tpu_custom_call" | custom-call | flops 24999999488 | bytes 1048576 | tf_op jit(solution)/shard_map/sum_4/pallas_call | solution.py:492
  140.4 2.3 pad_maximum_fusion.1.x_ref
  142.7 3.5 compare_select_fusion.1
  146.3 3.5 compare_select_fusion
  149.8 3.1 pad_maximum_fusion.dt_ref
  152.8 3.5 select_convert_fusion
  156.3 55.9 %scan_states.1 = (f32[2,2,1024,384]{3,2,1,0:T(8,128)}, bf16[2,2,16384,384]{3,2,1,0:T(8,128)(2,1)}) custom-call(f32[2,2,1024,384]{3,2,1,0:T(8,128)} %pad_maximum_fusion.dt_ref, bf16[2,2,1024,384]{3,2,1,0:T(8,128)(2,1)S(1)} %pad_maximum_fusion.1.x_ref, bf16[2,2,1024,512]{3,2,1,0:T(8,128)(2,1)} %bitcast.272, f32[2,16,384]{2,1,0:T(8,128)S(1)} %fusion.91.r_ref), custom_call_target="tpu_custom_call" | custom-call | flops 64000000000 | bytes 83886080 | tf_op jit(solution)/shard_map/scan_states/pallas_call | solution.py:266
  212.3 13.3 %fusion.27 = (bf16[384]{0:T(512)(128)(2,1)}, bf16[384]{0:T(512)(128)(2,1)}, f32[2,1024,384]{2,1,0:T(8,128)}, bf16[2,1024,384]{2,1,0:T(8,128)(2,1)}, f32[2,1024,384]{2,1,0:T(8,128)S(1)}) fusion(bf16[2,1024,384]{2,1,0:T(8,128)(2,1)} %copy-done.8, bf16[2,1024,384]{2,1,0:T(8,128)(2,1)} %copy-done.10, f32[2,1024,768]{2,1,0:T(8,128)} %copy-done.20, ...), kind=kOutput, calls=%fused_computation.56 | convolution fusion | flops 2443443200 | bytes 27935232 | tf_op jit(solution)/shard_map/dot_general | solution.py:30
  225.6 3.0 multiply_convert_fusion.4
  228.6 5.6 convolution_convert_fusion.1
  234.2 3.8 fusion.46
  238.0 90.6 %scan_adjoint.1 = (f32[2,2,1024,384]{3,2,1,0:T(8,128)}, f32[2,2,1024,384]{3,2,1,0:T(8,128)}, f32[2,2,512,256]{3,2,1,0:T(8,128)S(1)}, f32[2,2,16,384]{3,2,1,0:T(8,128)S(1)}) custom-call(f32[2,2,1024,384]{3,2,1,0:T(8,128)} %pad_maximum_fusion.dt_ref, bf16[2,2,1024,384]{3,2,1,0:T(8,128)(2,1)S(1)} %pad_maximum_fusion.1.x_ref, ...), custom_call_target="tpu_custom_call" | custom-call | flops 99999997952 | bytes 104857600 | tf_op jit(solution)/shard_map/scan_adjoint/pallas_call | solution.py:313
  328.7 1.3 copy-done.2
  330.0 10.1 %reshape.293 = bf16[2,2,64,8,16,16]{5,4,3,2,1,0:T(8,128)(2,1)} reshape(f32[2,2,512,256]{3,2,1,0:T(8,128)} %copy-done.2) | data formatting | bytes 3145728 | tf_op jit(solution)/shard_map/reshape | solution.py:988
  340.1 2.0 slice_bitcast_fusion
  342.1 1.4 fusion.131
  343.5 2.0 copy.85
  345.5 1.8 squeeze.68
  347.3 3.4 fusion.129
  351.9 1.1 copy-done.14
  353.0 1.4 convolution_convert_fusion.4
  354.5 1.8 maximum_bitcast_fusion
  356.3 3.7 copy.84
  360.0 2.9 squeeze.66
  363.0 3.2 fusion.127
  367.9 45.4 %all-reduce.6.cloned.1.call-done = bf16[384,1536]{1,0:T(8,128)(2,1)} async-done(((bf16[384,1536]{1,0:T(8,128)(2,1)}), bf16[384,1536]{1,0:T(8,128)(2,1)}) %all-reduce.6.cloned.1.call-update) | async-done | bytes 1179664 | tf_op jit(solution)/shard_map/psum | solution.py:983
  414.2 27.5 %sum_5.1 = bf16[4,4,2,128,128]{4,3,2,1,0:T(8,128)(2,1)S(1)} custom-call(bf16[4,4,2,128,128]{4,3,2,1,0:T(8,128)(2,1)S(1)} %bitcast.218), custom_call_target="tpu_custom_call" | custom-call | flops 24999999488 | bytes 1048576 | tf_op jit(solution)/shard_map/sum_5/pallas_call | solution.py:492
  441.9 5.3 fusion.40
  447.4 5.9 fusion.22
  453.3 2.9 add_convert_fusion
  456.2 7.1 %convolution_convert_fusion = bf16[2048,1536]{1,0:T(8,128)(2,1)} fusion(bf16[1536,768]{1,0:T(8,128)(2,1)S(1)} %bitcast.275, bf16[2048,384]{1,0:T(8,128)(2,1)S(1)} %bitcast.276, bf16[2048,384]{1,0:T(8,128)(2,1)S(1)} %bitcast.249), kind=kOutput, calls=%fused_computation.12 | convolution fusion | flops 4841275392 | bytes 11796480 | tf_op jit(solution)/shard_map/dot_general | solution.py:30
  465.1 2.7 copy.91
  467.8 1.8 copy.90
  469.7 1.9 fusion.64
  471.6 2.0 fusion.65
  474.2 2.2 convolution_convert_fusion.5
  477.2 8.5 %bitcast_convert_fusion = bf16[1536,768]{1,0:T(8,128)(2,1)S(1)} fusion(bf16[2,1024,1536]{2,1,0:T(8,128)(2,1)} %all-gather.3.cloned.1.call-done, f32[2,1536]{1,0:T(2,128)S(1)} %copy-done.61, f32[2,1536]{1,0:T(2,128)S(1)} %copy-done.36, f32[2,1024]{1,0:T(2,128)S(1)} %copy-done.69, f32[2,1024]{1,0:T(2,128)S(1)} %copy-done.41, ...), kind=kOutput, calls=%fused_computation.21 | convolution fusion | flops 4858183680 | bytes 11837440 | tf_op jit(solution)/shard_map/dot_general | solution.py:26
  485.7 85.8 %weight_sums.1 = (bf16[4,8,48,768]{3,2,1,0:T(8,128)(2,1)S(1)}, bf16[4,8,32,768]{3,2,1,0:T(8,128)(2,1)S(1)}, bf16[4,96,256]{2,1,0:T(8,128)(2,1)S(1)}) custom-call(bf16[8,4,48,768]{3,2,1,0:T(8,128)(2,1)S(1)} %bitcast.225, bf16[4,32,768]{2,1,0:T(8,128)(2,1)S(1)} %bitcast.224, bf16[4,96,256]{2,1,0:T(8,128)(2,1)S(1)} %pad_maximum_fusion.5.select_ref), custom_call_target="tpu_custom_call" | custom-call | flops 60000002048 | bytes 1048576 | tf_op jit(solution)/shard_map/weight_sums/pallas_call | solution.py:761
  571.5 1.1 copy-done.3
  572.6 4.9 reshape.301
  577.6 4.4 slice.285
  582.0 3.5 copy.94
  585.5 4.2 convert_element_type.228
  589.7 1.8 slice.289
  591.6 1.6 slice.286
  593.1 3.9 reshape.302
  597.1 7.3 %copy.92 = f32[4,48,2,8,384]{4,3,2,1,0:T(8,128)} copy(f32[4,48,2,8,384]{4,2,1,3,0:T(2,128)} %bitcast.234) | data formatting | bytes 9437184 | tf_op jit(solution)/shard_map/convert_element_type | solution.py:1089
  604.4 5.3 reshape.299
  609.7 2.8 copy.93
  612.5 2.9 slice.259
  615.4 3.1 convert_element_type.222
  619.3 1.8 fusion.130
  621.1 2.1 fusion.62
  623.2 3.5 fusion.58
  627.3 14.2 %modulation_sums.1 = f32[4,2,4608]{2,1,0:T(2,128)} custom-call(f32[2,4608]{1,0:T(2,128)} %pad_maximum_fusion.6.v_ref), custom_call_target="tpu_custom_call" | custom-call | flops 10000000000 | bytes 1048576 | tf_op jit(solution)/shard_map/modulation_sums/pallas_call | solution.py:822
  642.5 1.6 reduce_sum.249
  644.1 4.1 fusion.96
  (277 shorter events, 19.5 us)
Async XLA Ops:
  7.3 84.2 %all-gather.3.cloned.1.call-start = ((), (), s32[]{:S(2)}) async-start(), calls=%async_computation.2 | async-start | bytes 7077888 | tf_op jit(solution)/shard_map/all_gather | solution.py:908
  8.0 204.3 %all-gather.5.cloned.1.call-start = ((), (), s32[]{:S(2)}) async-start(), calls=%async_computation.3 | async-start | bytes 7077888 | tf_op jit(solution)/shard_map/all_gather | solution.py:945
  10.8 47.1 %copy-start.70 = (f32[2]{0:T(128)}, f32[2]{0:T(128)S(1)}, u32[]{:S(2)}) copy-start(f32[2]{0:T(128)S(1)} %dynamic-slice_convert_fusion.2) | copy-start | bytes 28
  10.9 93.4 %copy-start.44 = (f32[384]{0:T(512)}, f32[384]{0:T(512)S(1)}, u32[]{:S(2)}) copy-start(f32[384]{0:T(512)S(1)} %get-tuple-element.80) | copy-start | bytes 4612
  10.9 93.4 %copy-start.46 = (f32[384]{0:T(512)}, f32[384]{0:T(512)S(1)}, u32[]{:S(2)}) copy-start(f32[384]{0:T(512)S(1)} %get-tuple-element.81) | copy-start | bytes 4612
  11.0 93.4 %copy-start.48 = (f32[384]{0:T(512)}, f32[384]{0:T(512)S(1)}, u32[]{:S(2)}) copy-start(f32[384]{0:T(512)S(1)} %get-tuple-element.82) | copy-start | bytes 4612
  11.0 93.4 %copy-start.50 = (f32[384]{0:T(512)}, f32[384]{0:T(512)S(1)}, u32[]{:S(2)}) copy-start(f32[384]{0:T(512)S(1)} %get-tuple-element.83) | copy-start | bytes 4612
  11.0 93.4 %copy-start.52 = (f32[384]{0:T(512)}, f32[384]{0:T(512)S(1)}, u32[]{:S(2)}) copy-start(f32[384]{0:T(512)S(1)} %get-tuple-element.84) | copy-start | bytes 4612
  11.0 93.4 %copy-start.54 = (f32[384]{0:T(512)}, f32[384]{0:T(512)S(1)}, u32[]{:S(2)}) copy-start(f32[384]{0:T(512)S(1)} %get-tuple-element.85) | copy-start | bytes 4612
  11.0 93.4 %copy-start.56 = (f32[384]{0:T(512)}, f32[384]{0:T(512)S(1)}, u32[]{:S(2)}) copy-start(f32[384]{0:T(512)S(1)} %get-tuple-element.86) | copy-start | bytes 4612
  11.0 93.4 %copy-start.58 = (f32[384]{0:T(512)}, f32[384]{0:T(512)S(1)}, u32[]{:S(2)}) copy-start(f32[384]{0:T(512)S(1)} %get-tuple-element.87) | copy-start | bytes 4612
  11.0 93.4 %copy-start.64 = (f32[384]{0:T(512)}, f32[384]{0:T(512)S(1)}, u32[]{:S(2)}) copy-start(f32[384]{0:T(512)S(1)} %get-tuple-element.123) | copy-start | bytes 4612
  11.0 93.4 %copy-start.66 = (f32[384]{0:T(512)}, f32[384]{0:T(512)S(1)}, u32[]{:S(2)}) copy-start(f32[384]{0:T(512)S(1)} %get-tuple-element.124) | copy-start | bytes 4612
  11.3 45.9 %copy-start.76 = (bf16[8,1536]{1,0:T(8,128)(2,1)}, bf16[8,1536]{1,0:T(8,128)(2,1)S(1)}, u32[]{:S(2)}) copy-start(bf16[8,1536]{1,0:T(8,128)(2,1)S(1)} %multiply_convert_fusion.12) | copy-start | bytes 73732
  58.0 39.8 %copy-start.35 = (f32[2,1536]{1,0:T(2,128)}, f32[2,1536]{1,0:T(2,128)S(1)}, u32[]{:S(2)}) copy-start(f32[2,1536]{1,0:T(2,128)S(1)} %get-tuple-element.115) | copy-start | bytes 36868
  58.0 39.8 %copy-start.60 = (f32[2,1536]{1,0:T(2,128)}, f32[2,1536]{1,0:T(2,128)S(1)}, u32[]{:S(2)}) copy-start(f32[2,1536]{1,0:T(2,128)S(1)} %get-tuple-element.114) | copy-start | bytes 36868
  58.0 176.1 %copy-start.37 = (f32[2,1536]{1,0:T(2,128)}, f32[2,1536]{1,0:T(2,128)S(1)}, u32[]{:S(2)}) copy-start(f32[2,1536]{1,0:T(2,128)S(1)} %get-tuple-element.113) | copy-start | bytes 36868
  91.4 4.6 copy-start.7
  97.9 6.3 copy-start.68
  104.1 4.7 copy-start.20
  104.3 5.1 copy-start.18
  104.3 4.5 copy-start.33
  108.8 28.1 %copy-start.8 = (bf16[2,1024,384]{2,1,0:T(8,128)(2,1)}, bf16[2,1024,384]{2,1,0:T(8,128)(2,1)S(1)}, u32[]{:S(2)}) copy-start(bf16[2,1024,384]{2,1,0:T(8,128)(2,1)S(1)} %get-tuple-element.106) | copy-start | bytes 4718596
  110.1 27.9 %copy-start.28 = (bf16[96,6144]{1,0:T(8,128)(2,1)S(1)}, bf16[96,6144]{1,0:T(8,128)(2,1)}, u32[]{:S(2)}) copy-start(bf16[96,6144]{1,0:T(8,128)(2,1)} %param.25) | copy-start | bytes 3538948
  138.0 216.4 %reduce-scatter.3.cloned.1.call-start = ((), (), s32[]{:S(2)}) async-start(), calls=%async_computation.4 | async-start | bytes 7077888 | tf_op jit(solution)/shard_map/reduce_scatter | solution.py:981
  138.6 7.6 %copy-start.30 = (bf16[96,2,1,384]{3,0,2,1:T(8,128)(2,1)}, bf16[96,2,1,384]{3,0,2,1:T(8,128)(2,1)S(1)}, u32[]{:S(2)}) copy-start(bf16[96,2,1,384]{3,0,2,1:T(8,128)(2,1)S(1)} %copy.118) | copy-start | bytes 442372
  139.2 73.1 %copy-start.72 = (f32[384]{0:T(512)}, f32[384]{0:T(512)S(1)}, u32[]{:S(2)}) copy-start(f32[384]{0:T(512)S(1)} %get-tuple-element.77) | copy-start | bytes 4612
  139.2 73.1 %copy-start.74 = (f32[384]{0:T(512)}, f32[384]{0:T(512)S(1)}, u32[]{:S(2)}) copy-start(f32[384]{0:T(512)S(1)} %get-tuple-element.76) | copy-start | bytes 4612
  225.6 8.6 %slice-start = ((s8[6291456]{0:T(1024)(128)(4,1)}), s8[4194304]{0:T(1024)(128)(4,1)S(1)}, s32[]{:S(2)}) async-start(s8[6291456]{0:T(1024)(128)(4,1)} %bitcast.270), calls=%async_computation.7 | async-start | bytes 8388608
  228.6 5.6 slice-start.1
  238.0 175.4 %all-reduce.6.cloned.1.call-start = ((), (), s32[]{:S(2)}) async-start(), calls=%async_computation.5 | async-start | bytes 2359296 | tf_op jit(solution)/shard_map/psum | solution.py:983
  354.4 266.6 %reduce-scatter.5.cloned.1.call-start = ((), (), s32[]{:S(2)}) async-start(), calls=%async_computation.6 | async-start | bytes 7077888 | tf_op jit(solution)/shard_map/reduce_scatter | solution.py:1024
  366.1 47.2 %copy-start.23 = (bf16[1,2048,128]{1,2,0:T(8,128)(2,1)S(1)}, bf16[1,2048,128]{1,2,0:T(8,128)(2,1)}, u32[]{:S(2)}) copy-start(bf16[1,2048,128]{1,2,0:T(8,128)(2,1)} %maximum_bitcast_fusion) | copy-start | bytes 1572868
  414.1 27.7 %copy-start.19 = (bf16[2,1024,384]{2,1,0:T(8,128)(2,1)S(1)}, bf16[2,1024,384]{2,1,0:T(8,128)(2,1)}, u32[]{:S(2)}) copy-start(bf16[2,1024,384]{2,1,0:T(8,128)(2,1)} %copy-done.18) | copy-start | bytes 4718596
  414.1 27.7 %copy-start.34 = (bf16[384,256]{1,0:T(8,128)(2,1)S(1)}, bf16[384,256]{1,0:T(8,128)(2,1)}, u32[]{:S(2)}) copy-start(bf16[384,256]{1,0:T(8,128)(2,1)} %param.23) | copy-start | bytes 589828
  414.1 27.7 %copy-start.45 = (f32[384]{0:T(512)S(1)}, f32[384]{0:T(512)}, u32[]{:S(2)}) copy-start(f32[384]{0:T(512)} %copy-done.44) | copy-start | bytes 4612
  414.1 27.7 %copy-start.55 = (f32[384]{0:T(512)S(1)}, f32[384]{0:T(512)}, u32[]{:S(2)}) copy-start(f32[384]{0:T(512)} %copy-done.54) | copy-start | bytes 4612
  414.1 27.7 %copy-start.57 = (f32[384]{0:T(512)S(1)}, f32[384]{0:T(512)}, u32[]{:S(2)}) copy-start(f32[384]{0:T(512)} %copy-done.56) | copy-start | bytes 4612
  414.1 27.7 %copy-start.59 = (f32[384]{0:T(512)S(1)}, f32[384]{0:T(512)}, u32[]{:S(2)}) copy-start(f32[384]{0:T(512)} %copy-done.58) | copy-start | bytes 4612
  414.2 27.7 %copy-start.67 = (f32[384]{0:T(512)S(1)}, f32[384]{0:T(512)}, u32[]{:S(2)}) copy-start(f32[384]{0:T(512)} %copy-done.66) | copy-start | bytes 4612
  414.2 27.7 %copy-start.75 = (f32[384]{0:T(512)S(1)}, f32[384]{0:T(512)}, u32[]{:S(2)}) copy-start(f32[384]{0:T(512)} %copy-done.74) | copy-start | bytes 4612
  414.2 27.7 %copy-start.87 = (f32[2,1024,384]{2,1,0:T(8,128)S(1)}, f32[2,1024,384]{2,1,0:T(8,128)}, u32[]{:S(2)}) copy-start(f32[2,1024,384]{2,1,0:T(8,128)} %get-tuple-element.39.g_ref) | copy-start | bytes 9437188
  441.7 5.6 slice-start.2
  441.8 5.5 copy-start.24
  441.9 5.4 copy-start.47
  441.9 5.4 copy-start.49
  441.9 5.4 copy-start.51
  441.9 5.4 copy-start.53
  441.9 5.4 copy-start.65
  441.9 5.4 copy-start.73
  441.9 5.4 slice-start.3
  456.2 7.2 %copy-start.26 = (bf16[2,1024,384]{2,1,0:T(8,128)(2,1)}, bf16[2,1024,384]{2,1,0:T(8,128)(2,1)S(1)}, u32[]{:S(2)}) copy-start(bf16[2,1024,384]{2,1,0:T(8,128)(2,1)S(1)} %add_convert_fusion) | copy-start | bytes 4718596
  465.0 4.5 copy-start.78
  465.1 4.5 copy-start.77
  465.1 4.6 copy-start.6
  471.6 4.9 copy-start.17
  577.5 4.5 copy-start.11
  604.4 5.4 copy-start.16
  615.3 5.7 copy-start.13
  615.3 7.8 %copy-start.21 = (bf16[2,128,1536]{2,1,0:T(8,128)(2,1)S(1)}, bf16[2,128,1536]{2,1,0:T(8,128)(2,1)}, u32[]{:S(2)}) copy-start(bf16[2,128,1536]{2,1,0:T(8,128)(2,1)} %param.20) | copy-start | bytes 2359300
  615.3 7.8 %copy-start.29 = (bf16[2,128,1536]{2,1,0:T(8,128)(2,1)S(1)}, bf16[2,128,1536]{2,1,0:T(8,128)(2,1)}, u32[]{:S(2)}) copy-start(bf16[2,128,1536]{2,1,0:T(8,128)(2,1)} %reduce-scatter.3.cloned.1.call-done) | copy-start | bytes 2359300
  615.3 7.8 %copy-start.38 = (f32[2,1536]{1,0:T(2,128)S(1)}, f32[2,1536]{1,0:T(2,128)}, u32[]{:S(2)}) copy-start(f32[2,1536]{1,0:T(2,128)} %copy-done.37) | copy-start | bytes 36868
  615.4 7.8 %copy-start.71 = (f32[2]{0:T(128)S(1)}, f32[2]{0:T(128)}, u32[]{:S(2)}) copy-start(f32[2]{0:T(128)} %copy-done.70) | copy-start | bytes 28
  627.3 20.9 %copy-start.1 = (bf16[192,6144]{1,0:T(8,128)(2,1)S(1)}, bf16[192,6144]{1,0:T(8,128)(2,1)}, u32[]{:S(2)}) copy-start(bf16[192,6144]{1,0:T(8,128)(2,1)} %param.21) | copy-start | bytes 7077892
  (33 other events, 80.4 us)
Sparse Core Ops, SparseCore 0:
  9.7 81.6 all-gather.2
  138.1 69.0 all-gather.4
  238.1 74.0 reduce-scatter.2
  354.5 58.7 all-reduce.5
  463.5 89.4 reduce-scatter.4

commit v2 on v1

--- a/solution.py
+++ b/solution.py
@@ -78,7 +78,34 @@
     lax.fori_loop(0, count // 2, pair, 0)
 
 
-def states_kernel(count, dt_ref, x_ref, bc_ref, r_ref, y_ref, h_ref, state, even, odd):
+def place_coefficients(selection, copies):
+    placed = jnp.dot(selection, copies, preferred_element_type=f32)
+    row = lax.rem(lax.broadcasted_iota(jnp.int32, placed.shape, 0), chunk)
+    span = placed.shape[1] // 2
+    col = lax.rem(lax.broadcasted_iota(jnp.int32, placed.shape, 1), span) // (span // chunk)
+    return jnp.where(row == col, placed, 0.0).astype(bf16)
+
+
+def softplus(v):
+    return jnp.maximum(v, 0.0) + jnp.log1p(jnp.exp(-jnp.abs(v)))
+
+
+def states_kernel(
+    count,
+    sel_ref,
+    x_ref,
+    w_ref,
+    bias_ref,
+    r_ref,
+    copies_ref,
+    y_ref,
+    h_ref,
+    dt_ref,
+    state,
+    bc,
+    even,
+    odd,
+):
     slots, width = dt_ref.shape[1], dt_ref.shape[3]
     groups = width // lanes
     states = r_ref.shape[1]
@@ -87,6 +114,13 @@
     def _():
         state[...] = jnp.zeros_like(state)
 
+    for s in range(slots):
+        selection = sel_ref[0, s]
+        dt_ref[0, s] = softplus(
+            jnp.dot(selection, w_ref[0], preferred_element_type=f32) + bias_ref[0]
+        )
+        bc[s] = place_coefficients(selection, copies_ref[...])
+
     def one_direction(reverse):
         mix = spread_matrix()
 
@@ -96,7 +130,7 @@
         def spread(i, into):
             start = pl.multiple_of(place(i) * chunk, chunk)
             for s in range(slots):
-                both = bc_ref[0, s, pl.ds(start, chunk), :]
+                both = bc[s, pl.ds(start, chunk), :]
                 span = both.shape[1] // 2
                 into[s] = dot_rows(jnp.concatenate([both[:, :span], both[:, span:]], axis=0), mix)
 
@@ -135,18 +169,24 @@
 
 def adjoint_kernel(
     count,
+    sel_ref,
+    x_ref,
+    w_ref,
+    r_ref,
+    copies_ref,
+    skip_ref,
     dt_ref,
-    x_ref,
-    bc_ref,
-    r_ref,
     g_ref,
     h_ref,
     edge_ref,
-    step_ref,
+    low_ref,
     input_ref,
-    coef_ref,
+    gsel_ref,
     decay_ref,
+    sums_ref,
     pending,
+    bc,
+    coefs,
     even,
     odd,
 ):
@@ -159,6 +199,10 @@
     def _():
         pending[...] = jnp.zeros_like(pending)
         decay_ref[...] = jnp.zeros_like(decay_ref)
+        sums_ref[...] = jnp.zeros_like(sums_ref)
+
+    for s in range(slots):
+        bc[s] = place_coefficients(sel_ref[0, s], copies_ref[...])
 
     def one_direction(reverse):
         mix = spread_matrix()
@@ -173,7 +217,7 @@
         def spread(i, into):
             start = pl.multiple_of(place(i) * chunk, chunk)
             for s in range(slots):
-                both = bc_ref[0, s, pl.ds(start, chunk), :]
+                both = bc[s, pl.ds(start, chunk), :]
                 span = both.shape[1] // 2
                 into[s] = dot_rows(jnp.concatenate([both[:, :span], both[:, span:]], axis=0), mix)
 
@@ -232,11 +276,16 @@
                 pending[s] = pend
                 decay_ref[0, s] = total
                 weighted = fold_sublanes(into_sums)
-                step_ref[0, s, pl.ds(start, chunk), :] = (
-                    fold_sublanes(rate_sums) * ln2 + weighted * x
+                few = dt * (1.0 - dt * (0.5 - dt * (1.0 / 6.0 - dt * (1.0 / 24.0))))
+                slope = jnp.where(dt < 0.03, few, 1.0 - jnp.exp(-dt))
+                grad_pre = (fold_sublanes(rate_sums) * ln2 + weighted * x) * slope
+                low_ref[0, s, pl.ds(start, chunk), :] = grad_pre.astype(bf16)
+                input_ref[0, s, pl.ds(start, chunk), :] = weighted * dt + skip_ref[0] * g
+                gx = g * x
+                sums_ref[0] += jnp.concatenate(
+                    [grad_pre[:8] + grad_pre[8:], gx[:8] + gx[8:]], axis=0
                 )
-                input_ref[0, s, pl.ds(start, chunk), :] = weighted * dt
-                coef_ref[0, s, pl.ds(pl.multiple_of(here * 8, 8), 8), :] = dot_cols(
+                coefs[s, pl.ds(pl.multiple_of(here * 8, 8), 8), :] = dot_cols(
                     picks, jnp.concatenate(coef, axis=0)
                 )
 
@@ -249,39 +298,70 @@
             one_direction(d == 1)
 
 
+    own = lax.broadcasted_iota(jnp.int32, (chunk, chunk * states), 0) == (
+        lax.broadcasted_iota(jnp.int32, (chunk, chunk * states), 1) // states
+    )
+    for s in range(slots):
+        placed = []
+        for c in range(count):
+            placed.append(
+                jnp.concatenate(
+                    [
+                        jnp.where(own, coefs[s, c * 8 + k : c * 8 + k + 1, :], 0.0)
+                        for k in range(2)
+                    ],
+                    axis=1,
+                )
+            )
+        placed = jnp.concatenate(placed, axis=0).astype(bf16)
+        gsel_ref[0, s] = (
+            dot_cols(low_ref[0, s], w_ref[0]) + dot_cols(placed, copies_ref[...])
+        ).astype(bf16)
+
+
 def block_of(length):
     return math.gcd(length, 128)
 
 
-def scan_states(dt, x, bc, rate):
-    two, slots, length, width = dt.shape
+def scan_states(selection, x, weight, bias, rate, copies):
+    two, slots, length, width = x.shape
+    select = selection.shape[3]
     states = rate.shape[1]
     hidden_size = two * slots * length * states * width
     block = block_of(length)
     blocks = length // block
+    spread = copies.shape[1]
 
     def where(d, i):
         return (d, 0, jnp.where(d == 1, blocks - 1 - i, i), 0)
+
+    def by_direction(d, i):
+        return (d, 0, 0)
 
     return pl.pallas_call(
         functools.partial(states_kernel, block // chunk),
         grid=(two, blocks),
         in_specs=[
+            pl.BlockSpec((1, slots, block, select), where),
             pl.BlockSpec((1, slots, block, width), where),
-            pl.BlockSpec((1, slots, block, width), where),
-            pl.BlockSpec((1, slots, block, 2 * chunk * states), where),
-            pl.BlockSpec((1, states, width), lambda d, i: (d, 0, 0)),
+            pl.BlockSpec((1, select, width), by_direction),
+            pl.BlockSpec((1, 1, width), by_direction),
+            pl.BlockSpec((1, states, width), by_direction),
+            pl.BlockSpec((select, spread), lambda d, i: (0, 0)),
         ],
         out_specs=[
             pl.BlockSpec((1, slots, block, width), where),
             pl.BlockSpec((1, slots, block * states, width), where),
+            pl.BlockSpec((1, slots, block, width), where),
         ],
         out_shape=[
             jax.ShapeDtypeStruct((two, slots, length, width), f32),
             jax.ShapeDtypeStruct((two, slots, length * states, width), bf16),
+            jax.ShapeDtypeStruct((two, slots, length, width), f32),
         ],
         scratch_shapes=[
             pltpu.VMEM((slots, states, width), f32),
+            pltpu.VMEM((slots, block, spread), bf16),
             pltpu.VMEM((slots, chunk * states, 2 * lanes), f32),
             pltpu.VMEM((slots, chunk * states, 2 * lanes), f32),
         ],
@@ -290,15 +370,17 @@
             flops=64 * 10**9, bytes_accessed=80 * 2**20, transcendentals=hidden_size
         ),
         name="scan_states",
-    )(dt, x, bc, rate)
-
-
-def scan_adjoint(dt, x, bc, rate, g, h):
+    )(selection, x, weight, bias, rate, copies)
+
+
+def scan_adjoint(selection, x, weight, rate, copies, skip, dt, g, h):
     two, slots, length, width = dt.shape
+    select = selection.shape[3]
     states = rate.shape[1]
     hidden_size = two * slots * length * states * width
     block = block_of(length)
     blocks = length // block
+    spread = copies.shape[1]
 
     def at(d, i):
         return jnp.where(d == 1, i, blocks - 1 - i)
@@ -309,15 +391,21 @@
     def edge(d, i):
         mine = at(d, i) * block
         return (d, 0, jnp.clip(jnp.where(d == 1, mine + block, mine - 1), 0, length - 1), 0)
+
+    def by_direction(d, i):
+        return (d, 0, 0)
 
     return pl.pallas_call(
         functools.partial(adjoint_kernel, block // chunk),
         grid=(two, blocks),
         in_specs=[
+            pl.BlockSpec((1, slots, block, select), where),
             pl.BlockSpec((1, slots, block, width), where),
+            pl.BlockSpec((1, select, width), by_direction),
+            pl.BlockSpec((1, states, width), by_direction),
+            pl.BlockSpec((select, spread), lambda d, i: (0, 0)),
+            pl.BlockSpec((1, 1, width), by_direction),
             pl.BlockSpec((1, slots, block, width), where),
-            pl.BlockSpec((1, slots, block, 2 * chunk * states), where),
-            pl.BlockSpec((1, states, width), lambda d, i: (d, 0, 0)),
             pl.BlockSpec((slots, block, width), lambda d, i: (0, at(d, i), 0)),
             pl.BlockSpec((1, slots, block * states, width), where),
             pl.BlockSpec((1, slots, states, width), edge),
@@ -325,17 +413,21 @@
         out_specs=[
             pl.BlockSpec((1, slots, block, width), where),
             pl.BlockSpec((1, slots, block, width), where),
-            pl.BlockSpec((1, slots, block // chunk * 8, chunk * states), where),
+            pl.BlockSpec((1, slots, block, select), where),
             pl.BlockSpec((1, slots, states, width), lambda d, i: (d, 0, 0, 0)),
+            pl.BlockSpec((1, 16, width), by_direction),
         ],
         out_shape=[
+            jax.ShapeDtypeStruct((two, slots, length, width), bf16),
             jax.ShapeDtypeStruct((two, slots, length, width), f32),
-            jax.ShapeDtypeStruct((two, slots, length, width), f32),
-            jax.ShapeDtypeStruct((two, slots, length // chunk * 8, chunk * states), f32),
+            jax.ShapeDtypeStruct((two, slots, length, select), bf16),
             jax.ShapeDtypeStruct((two, slots, states, width), f32),
+            jax.ShapeDtypeStruct((two, 16, width), f32),
         ],
         scratch_shapes=[
             pltpu.VMEM((slots, states, width), f32),
+            pltpu.VMEM((slots, block, spread), bf16),
+            pltpu.VMEM((slots, block // chunk * 8, chunk * states), f32),
             pltpu.VMEM((slots, chunk * states, 2 * lanes), f32),
             pltpu.VMEM((slots, chunk * states, 2 * lanes), f32),
         ],
@@ -344,18 +436,14 @@
             flops=100 * 10**9, bytes_accessed=100 * 2**20, transcendentals=hidden_size
         ),
         name="scan_adjoint",
-    )(dt, x, bc, rate, g, h, h)
-
-
-def coefficient_rows(selection, rank, states):
-    rows, width = selection.shape[1:]
+    )(selection, x, weight, rate, copies, skip, dt, g, h, h)
+
+
+def coefficient_copies(width, rank, states):
     span = chunk * states
     col = jnp.arange(2 * span)
     origin = rank + (col // span) * states + col % states
-    copies = (jnp.arange(width)[:, None] == origin[None, :]).astype(bf16)
-    own = (jnp.arange(rows) % chunk)[:, None] == ((col % span) // states)[None, :]
-    placed = jnp.einsum("drk,kc->drc", selection, copies, preferred_element_type=f32)
-    return jnp.where(own, placed, 0.0).astype(bf16)
+    return (jnp.arange(width)[:, None] == origin[None, :]).astype(bf16)
 
 
 def widen(v, width):
@@ -607,9 +695,14 @@
     )(blocks, modulation)
 
 
-def tail_kernel(
-    g_ref, small_ref, select_ref, g_out, small_out, select_out, g_box, small_box, select_box, g_stage, *sems
-):
+def tail_kernel(cuts, g_ref, small_ref, select_ref, *refs):
+    if cuts is None:
+        g_out, small_out, select_out, *refs = refs
+    else:
+        in_final, select_final, *refs = refs
+        finals, refs = refs[: len(cuts)], refs[len(cuts) :]
+        g_out, small_out, select_out, *refs = refs
+    g_box, small_box, select_box, g_stage, *sems = refs
     (a_send, a_recv, s_send, s_recv, c_send, c_recv, z_send, z_recv, y_send, y_recv) = sems[:10]
     f_send, f_recv, h_send, h_recv, e_send, e_recv = sems[10:]
     shares, peers = g_ref.shape[0], g_ref.shape[1]
@@ -722,12 +815,26 @@
 
     each(1, shares, pass_on)
 
+    def widen_in(j, s):
+        if cuts is None:
+            return
+        rows, mine = g_ref.shape[2], g_ref.shape[3] // 2
+        inner = in_final.shape[1] // 2
+        block = g_out[j, s].astype(f32)
+        place = pl.ds(pl.multiple_of(j * rows, rows), rows)
+        for half in range(2):
+            first = pl.multiple_of(s * mine + half * inner, lanes)
+            in_final[place, pl.ds(first, mine)] = block[:, half * mine : (half + 1) * mine]
+
+    each(0, shares, lambda k: widen_in(item, behind(k)))
+
     def finish(k):
         def one(t):
             block = g_out.at[origin(t), behind(k)]
             remote(block, block, f_send, f_recv, flat(k, t), "item", other(t)).wait_recv()
             little = small_out.at[origin(t), behind(k)]
             remote(little, little, h_send, h_recv, flat(k, t), "item", other(t)).wait_recv()
+            widen_in(origin(t), behind(k))
             forward_in(k, t).wait_send()
             forward_small(k, t).wait_send()
             share_in(k, t).wait_send()
@@ -750,24 +857,47 @@
         place_in(k).wait_send()
 
     each(1, shares, finish_seq)
-
-
-def weight_sums(g, small, select):
+    if cuts is None:
+        return
+    for j in range(peers):
+        rows = select_ref.shape[1]
+        select_final[j * rows : (j + 1) * rows] = select_out[j].astype(f32)
+    inner = in_final.shape[1] // 2
+    mine, share = small_ref.shape[2] // 2, small_ref.shape[1]
+    for s in range(shares):
+        whole = jnp.concatenate([small_out[j, s].astype(f32) for j in range(peers)], axis=0)
+        for half in range(2):
+            columns = slice(half * inner + s * mine, half * inner + (s + 1) * mine)
+            first = 0
+            for cut, final in zip(cuts, finals):
+                final[:, columns] = whole[first : first + cut, half * mine : (half + 1) * mine]
+                first += cut
+
+
+def weight_sums(g, small, select, cuts):
     shares, peers = g.shape[:2]
     vmem = pl.BlockSpec(memory_space=pltpu.VMEM)
     dma = pltpu.SemaphoreType.DMA
     some = peers - 1
     sizes = [shares * some] * 2 + [some] * 4 + [shares] * 4 + [shares * some] * 4 + [some] * 2
+    kept = [
+        ((peers, shares) + g.shape[2:], bf16),
+        ((peers, shares) + small.shape[1:], bf16),
+        (select.shape, bf16),
+    ]
+    inner2 = shares * g.shape[3]
+    direct = (g.shape[3] // 2) % lanes == 0
+    outs = kept
+    if direct:
+        outs = [((peers * g.shape[2], inner2), f32), ((peers * select.shape[1], select.shape[2]), f32)]
+        outs += [((cut, inner2), f32) for cut in cuts]
     return pl.pallas_call(
-        tail_kernel,
+        functools.partial(tail_kernel, cuts if direct else None),
         in_specs=[vmem] * 3,
-        out_specs=[vmem] * 3,
-        out_shape=[
-            jax.ShapeDtypeStruct((peers, shares) + g.shape[2:], bf16),
-            jax.ShapeDtypeStruct((peers, shares) + small.shape[1:], bf16),
-            jax.ShapeDtypeStruct(select.shape, bf16),
-        ],
-        scratch_shapes=[
+        out_specs=[vmem] * len(outs),
+        out_shape=[jax.ShapeDtypeStruct(shape, kind) for shape, kind in outs],
+        scratch_shapes=[pltpu.VMEM(shape, kind) for shape, kind in kept if direct]
+        + [
             pltpu.VMEM((some, shares) + g.shape[2:], bf16),
             pltpu.VMEM((some,) + small.shape[1:], bf16),
             pltpu.VMEM((some,) + select.shape[1:], bf16),
@@ -944,17 +1074,19 @@
     selection, late_cotangent = lax.optimization_barrier((selection, cotangent))
     all_cotangent = lax.all_gather(late_cotangent, "seq", axis=1, tiled=True)
     delta_rank = selection[:, :, :rank]
-    bc = coefficient_rows(selection, rank, states).reshape(2, slots, length, -1)
-    step_pre = [
-        jnp.dot(delta_rank[d], step_weight[:, d], preferred_element_type=f32) + step_bias[d]
-        for d in range(2)
-    ]
-    step = jnp.stack([jax.nn.softplus(p) for p in step_pre]).reshape(2, slots, length, mine)
-    active = jnp.stack(activated)
-    wide_step = widen(step, padded_width)
-    wide_active = widen(active, padded_width)
+    selection = selection.reshape(2, slots, length, select)
+    copies = coefficient_copies(select, rank, states)
+    wide_active = widen(jnp.stack(activated), padded_width)
     wide_rate = widen(jnp.swapaxes(rate, 0, 1) * log2e, padded_width)
-    scanned, hidden = scan_states(wide_step, wide_active, bc, wide_rate)
+    wide_weight = widen(
+        jnp.pad(jnp.swapaxes(step_weight, 0, 1), ((0, 0), (0, select - rank), (0, 0))),
+        padded_width,
+    )
+    wide_bias = widen(step_bias[:, None, :], padded_width)
+    wide_skip = widen(skip[:, None, :], padded_width)
+    scanned, hidden, step = scan_states(
+        selection, wide_active, wide_weight, wide_bias, wide_rate, copies
+    )
     scanned = scanned[..., :mine]
     scanned_sum = scanned[0] + scanned[1]
     for d in range(2):
@@ -979,27 +1111,31 @@
         (branch_part, grad_out, grad_scanned)
     )
     branch_part = lax.psum_scatter(branch_part, "seq", scatter_dimension=1, tiled=True)
-    grad_out, branch_part = lax.optimization_barrier((grad_out, branch_part))
-    grad_out = lax.psum(grad_out, "item")
-    grad_step, grad_input, grad_coef, grad_rate = scan_adjoint(
-        wide_step, wide_active, bc, wide_rate, widen(scan_grad, padded_width), hidden
+    grad_low, grad_input, grad_parts, grad_rate, grad_sums = scan_adjoint(
+        selection,
+        wide_active,
+        wide_weight,
+        wide_rate,
+        copies,
+        wide_skip,
+        step,
+        widen(scan_grad, padded_width),
+        hidden,
     )
     grad_decay = jnp.sum(grad_rate, axis=1)[..., :mine] * ln2
-    grad_coef = grad_coef.reshape(2, slots, length // chunk, 8, chunk, states)[:, :, :, :2]
-    grad_coef = jnp.moveaxis(grad_coef, 3, 4).reshape(2, rows, 2 * states)
-    parts = []
-    grad_skip, grad_step_bias, grad_delta = [], [], []
-    for d in range(2):
-        grad_skip.append(jnp.sum(grad_scanned * activated[d].astype(f32), axis=(0, 1)))
-        grad_pre = grad_step[d, ..., :mine].reshape(rows, mine) * jax.nn.sigmoid(step_pre[d])
-        low = grad_pre.astype(bf16)
-        grad_step_bias.append(jnp.sum(grad_pre, axis=0))
-        grad_delta.append(dot_rows(delta_rank[d], low))
-        parts.append(jnp.concatenate([dot_cols(low, step_weight[:, d]), grad_coef[d]], axis=1))
-    parts[1], grad_out, branch_part = lax.optimization_barrier((parts[1], grad_out, branch_part))
+    grad_step_bias = jnp.sum(grad_sums[:, :8, :mine], axis=1)
+    grad_skip = jnp.sum(grad_sums[:, 8:, :mine], axis=1)
+    grad_parts, grad_out, branch_part = lax.optimization_barrier(
+        (grad_parts, grad_out, branch_part)
+    )
+    grad_out = lax.psum_scatter(grad_out, "item", scatter_dimension=0, tiled=True)
+    grad_out = lax.all_gather(grad_out, "item", axis=0, tiled=True)
     grad_selection = summed_everywhere(
-        jnp.stack(parts).astype(bf16).reshape(2 * slots, length, select), 5
+        grad_parts.reshape(2 * slots, length, select), 5
     ).reshape(2, rows, select)
+    grad_delta = [
+        dot_rows(delta_rank[d], grad_low[d, ..., :mine].reshape(rows, mine)) for d in range(2)
+    ]
     grad_x = jnp.zeros((slots, length, mine), f32)
     grad_select, grad_taps, grad_tap_bias = [], [], []
     for d in range(2):
@@ -1007,7 +1143,6 @@
         grad_select.append(dot_rows(activated[d].reshape(rows, mine), grad_selection[d]))
         grad_active = (
             grad_input[d, ..., :mine]
-            + skip[d] * grad_scanned
             + dot_cols(grad_selection[d], block).reshape(slots, length, mine)
         )
         grad_filtered = grad_active * silu_slope(filtered[d])
@@ -1058,11 +1193,11 @@
     small = jnp.concatenate(
         [
             jnp.stack(grad_delta, 1),
+            jnp.swapaxes(grad_decay, 0, 1),
             jnp.stack(grad_taps, 1),
             jnp.stack(grad_tap_bias)[None],
-            jnp.stack(grad_step_bias)[None],
-            jnp.swapaxes(grad_decay, 0, 1),
-            jnp.stack(grad_skip)[None],
+            grad_step_bias[None],
+            grad_skip[None],
         ],
         axis=0,
     )
@@ -1072,30 +1207,38 @@
         small.astype(bf16).reshape(small_rows, 2 * mine), ((0, peers * share - small_rows), (0, 0))
     )
     grad_select = jnp.concatenate(grad_select, axis=1).astype(bf16)
-    grad_in, small, grad_select = weight_sums(
+    cuts = [rank, states, taps, 1, 1, 1]
+    results = weight_sums(
         grad_in.reshape(shares, peers, share_rows, 2 * mine),
         small.reshape(peers, share, 2 * mine),
         grad_select.reshape(peers, mine // peers, 2 * select),
-    )
-    grad_in = grad_in.reshape(peers, shares, share_rows, 2, mine)
-    grad_in = jnp.transpose(grad_in, (0, 2, 3, 1, 4)).reshape(peers * share_rows, 2 * inner)
-    grad_select = grad_select.reshape(mine, 2 * select)
-    small = small.reshape(peers, shares, share, 2, mine)
-    small = jnp.transpose(small, (0, 2, 3, 1, 4)).reshape(peers * share, 2 * inner).astype(f32)
-    cuts = [rank, rank + taps, rank + taps + 1, rank + taps + 2, rank + taps + 2 + states]
+        cuts,
+    )
+    if mine % lanes == 0:
+        grad_in, grad_select, *small = results
+    else:
+        grad_in, small, grad_select = results
+        grad_in = grad_in.reshape(peers, shares, share_rows, 2, mine)
+        grad_in = jnp.transpose(grad_in, (0, 2, 3, 1, 4)).reshape(peers * share_rows, 2 * inner)
+        grad_in = grad_in.astype(f32)
+        small = small.reshape(peers, shares, share, 2, mine)
+        small = jnp.transpose(small, (0, 2, 3, 1, 4)).reshape(peers * share, 2 * inner).astype(f32)
+        ends = [sum(cuts[: i + 1]) for i in range(len(cuts))]
+        small = [small[end - cut : end] for cut, end in zip(cuts, ends)]
+        grad_select = grad_select.reshape(mine, 2 * select).astype(f32)
     return (
         output,
         grad_tokens,
-        grad_in.astype(f32),
+        grad_in,
         grad_out.astype(f32),
-        grad_select.astype(f32),
+        grad_select,
         grad_modulation_weight,
-        small[: cuts[0]],
-        small[cuts[0] : cuts[1]],
-        small[cuts[1]],
-        small[cuts[2]],
-        small[cuts[3] : cuts[4]],
-        small[cuts[4]],
+        small[0],
+        small[2],
+        small[3].reshape(-1),
+        small[4].reshape(-1),
+        small[1],
+        small[5].reshape(-1),
         jnp.sum(grad_modulation, axis=0),
     )
 

time: 666 us -> 581 us (0.87)
  local copies, waits for them, and re-layouts: 90.7 us -> 35.7 us
  waiting for transfers between devices: 79.5 us -> 35.4 us
  Pallas kernels: 346 us -> 366 us
  other arithmetic: 41.8 us -> 31 us
  starting transfers between devices: 0.2 us -> 10.9 us
    psum x1 -> x0, waiting for transfers between devices: 45.4 us -> none  [per_device(): grad_out = lax.psum(grad_out, 'item')]
    convert_element_type x6 -> x0, local copies, waits for them, and re-layouts: 29.2 us -> none  [the longest x3 16.6 us: per_device(): grad_in.astype(f32)]
    slice x11 -> x1, local copies, waits for them, and re-layouts: 25.8 us -> 2.2 us  [per_device(): grad_low[d, ..., :mine].reshape(rows, mine)]
    unnamed x192 -> x161, local copies, waits for them, and re-layouts: 9.91 us -> 24.5 us
    pallas_call x1, Pallas kernels: 90.6 us -> 102 us  [scan_adjoint(): pl.pallas_call(functools.partial(adjoint_kernel, block // chunk), grid=(t...]
    dot_general x3 -> x0, matrix products: 10.5 us -> none  [the longest x2 7.04 us: per_device(): jnp.dot(delta_rank[d], step_weight[:, d], preferred_element_type=f32)]
    reduce_scatter x0 -> x1, starting transfers between devices: none -> 10.4 us  [per_device(): lax.psum_scatter(grad_out, 'item', scatter_dimension=0, tiled=True)]
    reshape x1 -> x0, local copies, waits for them, and re-layouts: 10.1 us -> none  [per_device(): grad_coef.reshape(2, slots, length // chunk, 8, chunk, states)[:, :, :, :2]]
  transfers between devices with their start and end apart: 5 -> 6, of which waited for: 2 -> 2; matrix products, arithmetic and copies ran while one was open for 19% -> 11% of each run, Pallas kernels for 42% -> 57%
where the time goes in v2:
time: 581 us; the launch traced here: 571 us
  Pallas kernels  366 us (63%)
  matrix products  76.7 us (13%)
  local copies, waits for them, and re-layouts  35.7 us (6%)
  waiting for transfers between devices  35.4 us (6%)
  other arithmetic  31 us (5%)
  between operations  15.9 us (3%)
  starting transfers between devices  10.9 us (2%)
    pallas_call x1, Pallas kernels, scan_adjoint(): pl.pallas_call(functools.partial(adjoint_kernel, block // chunk), grid=(t...  102 us
    pallas_call x1, Pallas kernels, weight_sums(): pl.pallas_call(functools.partial(tail_kernel, cuts if direct else None),...  85.7 us
    pallas_call x1, Pallas kernels, scan_states(): pl.pallas_call(functools.partial(states_kernel, block // chunk), grid=(tw...  61.8 us
    pallas_call x2, Pallas kernels, summed_everywhere(): pl.pallas_call(functools.partial(total_kernel, line), in_specs=[vmem], ou...  56.5 us
    pallas_call x1, Pallas kernels, input_columns(): pl.pallas_call(head_kernel, in_specs=[anywhere, vmem], out_specs=[anywher...  44.9 us
    dot_general x4, matrix products, dot_cols(): lax.dot_general(a, b, (((1,), (1,)), ((), ())), preferred_element_type=f32)  39.4 us
    all_gather x1, waiting for transfers between devices, per_device(): all_tokens = lax.all_gather(tokens, 'seq', axis=1, tiled=True)  33.4 us
    unnamed x161, local copies, waits for them, and re-layouts  24.5 us
  transfers between devices with their start and end apart: 6, of which 2 were waited for; matrix products, arithmetic and copies ran while one was open for 11% of the time, Pallas kernels for 57%

profile of v2, /device:TPU:0, one launch (start us, length us, event | category | flops | bytes accessed | tf_op | source)
XLA Modules:
  0.0 571.2 jit_solution(750251425981821269)
XLA Ops:
  7.3 0.7 all-gather.4.cloned.1.call-update
  8.0 0.8 copy-done
  9.0 0.5 copy.50
  9.4 1.2 reshape.222.w_ref
  11.2 2.5 fusion.95.mod_ref
  13.7 44.9 %input_columns.1 = (bf16[8,4,48,768]{3,2,1,0:T(8,128)(2,1)}, f32[2,4608]{1,0:T(2,128)}) custom-call(bf16[8,48,768]{2,1,0:T(8,128)(2,1)} %reshape.222.w_ref, f32[2,4608]{1,0:T(2,128)} %fusion.95.mod_ref), custom_call_target="tpu_custom_call" | custom-call | flops 40000000000 | bytes 1048576 | tf_op jit(solution)/shard_map/input_columns/pallas_call | solution.py:674
  58.6 0.8 broadcast_add_fusion
  59.5 33.4 %all-gather.4.cloned.1.call-done = bf16[2,1024,1536]{2,1,0:T(8,128)(2,1)} async-done(((bf16[2,128,1536]{2,1,0:T(8,128)(2,1)}), bf16[2,1024,1536]{2,1,0:T(8,128)(2,1)}) %all-gather.4.cloned.1.call-update) | async-done | bytes 6291472 | tf_op jit(solution)/shard_map/all_gather | solution.py:1038
  92.9 3.8 convert_reduce_fusion
  96.7 0.8 copy-done.9
  97.5 1.8 fusion.2
  99.4 6.2 %fusion.9 = f32[2,1024,768]{2,1,0:T(8,128)S(1)} fusion(bf16[1536,768,1]{1,0,2:T(8,128)(2,1)S(1)} %bitcast.204, bf16[2,1024,1536]{2,1,0:T(8,128)(2,1)S(1)} %copy-done.9, f32[2,1536]{1,0:T(2,128)S(1)} %get-tuple-element.111, f32[2,1536]{1,0:T(2,128)S(1)} %get-tuple-element.112, f32[2,1024]{1,0:T(2,128)S(1)} %add_rsqrt_fusion, ...), kind=kOutput, calls=%fused_computation.30 | convolution fusion | flops 4850712576 | bytes 14983168 | tf_op jit(solution)/shard_map/dot_general | solution.py:1043
  105.9 4.4 multiply_convert_fusion.6
  110.3 0.6 fusion.43
  110.9 0.5 copy-done.10
  111.4 0.6 fusion.42
  112.1 26.8 %sum_4.1 = bf16[4,4,2,128,128]{4,3,2,1,0:T(8,128)(2,1)S(1)} custom-call(bf16[4,4,2,128,128]{4,3,2,1,0:T(8,128)(2,1)S(1)} %bitcast.155), custom_call_target="tpu_custom_call" | custom-call | flops 24999999488 | bytes 1048576 | tf_op jit(solution)/shard_map/sum_4/pallas_call | solution.py:580
  139.8 1.1 copy.69
  141.1 2.2 pad_maximum_fusion.x_ref
  143.3 61.8 %scan_states.1 = (f32[2,2,1024,384]{3,2,1,0:T(8,128)}, bf16[2,2,16384,384]{3,2,1,0:T(8,128)(2,1)}, f32[2,2,1024,384]{3,2,1,0:T(8,128)}) custom-call(bf16[2,2,1024,128]{3,2,1,0:T(8,128)(2,1)S(1)} %bitcast.156, bf16[2,2,1024,384]{3,2,1,0:T(8,128)(2,1)S(1)} %pad_maximum_fusion.x_ref, bf16[2,128,384]{2,1,0:T(8,128)(2,1)S(1)} %pad.23.w_ref, ...), custom_call_target="tpu_custom_call" | custom-call | flops 64000000000 | bytes 83886080 | tf_op jit(solution)/shard_map/scan_states/pallas_call | solution.py:341
  205.2 1.7 copy-done.4
  206.8 1.3 all-gather.6.cloned.1.call-done
  208.1 13.2 %multiply_convert_fusion.3 = (bf16[2,1024,384]{2,1,0:T(8,128)(2,1)}, f32[2,1024,384]{2,1,0:T(8,128)S(1)}, f32[2,1024,384]{2,1,0:T(8,128)}) fusion(f32[2,1024,768]{2,1,0:T(8,128)} %copy-done.15, bf16[2,1024,384]{2,1,0:T(8,128)(2,1)} %copy-done.11, f32[384]{0:T(512)S(1)} %get-tuple-element.87, bf16[2,1024,384]{2,1,0:T(8,128)(2,1)} %copy-done.10, ...), kind=kOutput, calls=%fused_computation.61 | convolution fusion | flops 2440298496 | bytes 27933696 | tf_op jit(solution)/shard_map/dot_general | solution.py:30
  221.3 3.0 multiply_convert_fusion.4
  224.3 5.2 convolution_convert_fusion.1
  229.5 3.8 fusion.41
  233.3 10.4 %reduce-scatter.8.cloned.1.call-start = ((), (), s32[]{:S(2)}) async-start(), calls=%async_computation.7 | async-start | bytes 1474560 | tf_op jit(solution)/shard_map/reduce_scatter | solution.py:1131
  243.8 102.5 %scan_adjoint.1 = (bf16[2,2,1024,384]{3,2,1,0:T(8,128)(2,1)S(1)}, f32[2,2,1024,384]{3,2,1,0:T(8,128)}, bf16[2,2,1024,128]{3,2,1,0:T(8,128)(2,1)S(1)}, f32[2,2,16,384]{3,2,1,0:T(8,128)S(1)}, f32[2,16,384]{2,1,0:T(8,128)S(1)}) custom-call(bf16[2,2,1024,128]{3,2,1,0:T(8,128)(2,1)S(1)} %bitcast.157, bf16[2,2,1024,384]{3,2,1,0:T(8,128)(2,1)} %copy-done.4, ...), custom_call_target="tpu_custom_call" | custom-call | flops 99999997952 | bytes 104857600 | tf_op jit(solution)/shard_map/scan_adjoint/pallas_call | solution.py:398
  346.2 1.7 copy-done.3
  348.0 0.9 copy-done.7
  348.9 1.2 copy-done.8
  350.2 29.7 %sum_5.1 = bf16[4,4,2,128,128]{4,3,2,1,0:T(8,128)(2,1)S(1)} custom-call(bf16[4,4,2,128,128]{4,3,2,1,0:T(8,128)(2,1)S(1)} %bitcast.165), custom_call_target="tpu_custom_call" | custom-call | flops 24999999488 | bytes 1048576 | tf_op jit(solution)/shard_map/sum_5/pallas_call | solution.py:580
  380.1 4.1 fusion.34
  384.4 15.0 %fusion.22 = (bf16[384]{0:T(512)(128)(2,1)S(1)}, bf16[384]{0:T(512)(128)(2,1)S(1)}, bf16[384]{0:T(512)(128)(2,1)S(1)}, bf16[384]{0:T(512)(128)(2,1)S(1)}, bf16[3...) fusion(bf16[2,1024,384]{2,1,0:T(8,128)(2,1)} %copy-done.13, ...), kind=kOutput, calls=%fused_computation.42 | convolution fusion | flops 236712192 | bytes 11650560 | tf_op jit(solution)/shard_map/dot_general | solution.py:30
  399.4 2.9 add_convert_fusion
  402.4 7.0 %convolution_convert_fusion = bf16[2048,1536]{1,0:T(8,128)(2,1)} fusion(bf16[1536,768]{1,0:T(8,128)(2,1)S(1)} %bitcast.205, bf16[2048,384]{1,0:T(8,128)(2,1)S(1)} %bitcast.206, bf16[2048,384]{1,0:T(8,128)(2,1)S(1)} %bitcast.185), kind=kOutput, calls=%fused_computation.9 | convolution fusion | flops 4841275392 | bytes 11796480 | tf_op jit(solution)/shard_map/dot_general | solution.py:30
  409.4 1.1 copy-done.12
  411.1 2.6 copy.58
  413.7 2.6 copy.57
  416.3 2.2 fusion.100
  418.5 0.5 fusion.60
  419.0 0.5 fusion.59
  420.2 2.1 convolution_convert_fusion.4
  422.3 2.0 convolution_convert_fusion.5
  424.4 9.1 %bitcast_convert_fusion = bf16[1536,768]{1,0:T(8,128)(2,1)S(1)} fusion(bf16[2,1024,1536]{2,1,0:T(8,128)(2,1)} %all-gather.4.cloned.1.call-done, f32[2,1536]{1,0:T(2,128)S(1)} %copy-done.49, f32[2,1536]{1,0:T(2,128)S(1)} %copy-done.24, f32[2,1024]{1,0:T(2,128)S(1)} %copy-done.57, f32[2,1024]{1,0:T(2,128)S(1)} %copy-done.29, ...), kind=kOutput, calls=%fused_computation.17 | convolution fusion | flops 4858183680 | bytes 11837440 | tf_op jit(solution)/shard_map/dot_general | solution.py:26
  433.5 85.7 %weight_sums.1 = (f32[192,6144]{1,0:T(8,128)S(1)}, f32[384,256]{1,0:T(8,128)S(1)}, f32[96,6144]{1,0:T(8,128)S(1)}, f32[16,6144]{1,0:T(8,128)S(1)}, f32[4,6144]{1...) custom-call(bf16[8,4,48,768]{3,2,1,0:T(8,128)(2,1)S(1)} %bitcast.164, ...), custom_call_target="tpu_custom_call" | custom-call | flops 60000002048 | bytes 1048576 | tf_op jit(solution)/shard_map/weight_sums/pallas_call | solution.py:894
  519.2 2.2 copy-done.2
  521.5 1.4 copy-done.5
  522.9 3.0 convert_element_type.175
  525.9 2.1 fusion.57
  528.0 3.7 fusion.53
  531.8 0.6 pad_maximum_fusion.3.v_ref
  532.4 14.3 %modulation_sums.1 = f32[4,2,4608]{2,1,0:T(2,128)} custom-call(f32[2,4608]{1,0:T(2,128)} %pad_maximum_fusion.3.v_ref), custom_call_target="tpu_custom_call" | custom-call | flops 10000000000 | bytes 1048576 | tf_op jit(solution)/shard_map/modulation_sums/pallas_call | solution.py:952
  546.7 1.0 reshape.238
  547.7 1.6 reduce_sum.229
  549.3 4.1 fusion.81
  553.5 5.1 copy.94
  558.6 0.7 copy.95
  559.4 1.4 copy.96
  560.8 0.6 copy.97
  561.4 0.6 copy.98
  562.0 0.6 copy.99
  562.6 0.7 copy.100
  563.4 0.6 copy.101
  (210 shorter events, 3.7 us)
Async XLA Ops:
  7.2 3.4 copy-start.51
  7.2 3.4 copy-start.27
  7.2 3.5 copy-start.50
  7.2 3.5 copy-start.63
  7.2 3.7 copy-start.62
  7.2 3.7 copy-start.64
  7.3 85.6 %all-gather.4.cloned.1.call-start = ((), (), s32[]{:S(2)}) async-start(), calls=%async_computation.3 | async-start | bytes 7077888 | tf_op jit(solution)/shard_map/all_gather | solution.py:1038
  8.0 200.1 %all-gather.6.cloned.1.call-start = ((), (), s32[]{:S(2)}) async-start(), calls=%async_computation.4 | async-start | bytes 7077888 | tf_op jit(solution)/shard_map/all_gather | solution.py:1075
  10.8 48.6 %copy-start.58 = (f32[2]{0:T(128)}, f32[2]{0:T(128)S(1)}, u32[]{:S(2)}) copy-start(f32[2]{0:T(128)S(1)} %dynamic-slice_convert_fusion.2) | copy-start | bytes 28
  10.9 94.9 %copy-start.32 = (f32[384]{0:T(512)}, f32[384]{0:T(512)S(1)}, u32[]{:S(2)}) copy-start(f32[384]{0:T(512)S(1)} %get-tuple-element.88) | copy-start | bytes 4612
  10.9 94.9 %copy-start.34 = (f32[384]{0:T(512)}, f32[384]{0:T(512)S(1)}, u32[]{:S(2)}) copy-start(f32[384]{0:T(512)S(1)} %get-tuple-element.89) | copy-start | bytes 4612
  10.9 94.9 %copy-start.36 = (f32[384]{0:T(512)}, f32[384]{0:T(512)S(1)}, u32[]{:S(2)}) copy-start(f32[384]{0:T(512)S(1)} %get-tuple-element.90) | copy-start | bytes 4612
  10.9 94.9 %copy-start.38 = (f32[384]{0:T(512)}, f32[384]{0:T(512)S(1)}, u32[]{:S(2)}) copy-start(f32[384]{0:T(512)S(1)} %get-tuple-element.91) | copy-start | bytes 4612
  11.0 94.9 %copy-start.40 = (f32[384]{0:T(512)}, f32[384]{0:T(512)S(1)}, u32[]{:S(2)}) copy-start(f32[384]{0:T(512)S(1)} %get-tuple-element.92) | copy-start | bytes 4612
  11.0 94.9 %copy-start.42 = (f32[384]{0:T(512)}, f32[384]{0:T(512)S(1)}, u32[]{:S(2)}) copy-start(f32[384]{0:T(512)S(1)} %get-tuple-element.93) | copy-start | bytes 4612
  11.0 94.9 %copy-start.44 = (f32[384]{0:T(512)}, f32[384]{0:T(512)S(1)}, u32[]{:S(2)}) copy-start(f32[384]{0:T(512)S(1)} %get-tuple-element.94) | copy-start | bytes 4612
  11.0 94.8 %copy-start.46 = (f32[384]{0:T(512)}, f32[384]{0:T(512)S(1)}, u32[]{:S(2)}) copy-start(f32[384]{0:T(512)S(1)} %get-tuple-element.95) | copy-start | bytes 4612
  11.0 94.8 %copy-start.52 = (f32[384]{0:T(512)}, f32[384]{0:T(512)S(1)}, u32[]{:S(2)}) copy-start(f32[384]{0:T(512)S(1)} %get-tuple-element.116) | copy-start | bytes 4612
  11.0 94.8 %copy-start.54 = (f32[384]{0:T(512)}, f32[384]{0:T(512)S(1)}, u32[]{:S(2)}) copy-start(f32[384]{0:T(512)S(1)} %get-tuple-element.117) | copy-start | bytes 4612
  11.2 47.4 %copy-start.60 = (bf16[8,1536]{1,0:T(8,128)(2,1)}, bf16[8,1536]{1,0:T(8,128)(2,1)S(1)}, u32[]{:S(2)}) copy-start(bf16[8,1536]{1,0:T(8,128)(2,1)S(1)} %multiply_convert_fusion.12) | copy-start | bytes 73732
  59.5 39.8 %copy-start.23 = (f32[2,1536]{1,0:T(2,128)}, f32[2,1536]{1,0:T(2,128)S(1)}, u32[]{:S(2)}) copy-start(f32[2,1536]{1,0:T(2,128)S(1)} %get-tuple-element.112) | copy-start | bytes 36868
  59.5 39.8 %copy-start.48 = (f32[2,1536]{1,0:T(2,128)}, f32[2,1536]{1,0:T(2,128)S(1)}, u32[]{:S(2)}) copy-start(f32[2,1536]{1,0:T(2,128)S(1)} %get-tuple-element.111) | copy-start | bytes 36868
  59.5 170.0 %copy-start.25 = (f32[2,1536]{1,0:T(2,128)}, f32[2,1536]{1,0:T(2,128)S(1)}, u32[]{:S(2)}) copy-start(f32[2,1536]{1,0:T(2,128)S(1)} %get-tuple-element.110) | copy-start | bytes 36868
  92.9 4.6 copy-start.9
  99.3 6.2 %copy-start.56 = (f32[2,1024]{1,0:T(2,128)}, f32[2,1024]{1,0:T(2,128)S(1)}, u32[]{:S(2)}) copy-start(f32[2,1024]{1,0:T(2,128)S(1)} %add_rsqrt_fusion) | copy-start | bytes 24580
  105.6 4.7 copy-start.15
  105.7 5.1 copy-start.13
  105.8 4.5 copy-start.20
  112.1 27.1 %copy-start.19 = (bf16[96,6144]{1,0:T(8,128)(2,1)S(1)}, bf16[96,6144]{1,0:T(8,128)(2,1)}, u32[]{:S(2)}) copy-start(bf16[96,6144]{1,0:T(8,128)(2,1)} %param.25) | copy-start | bytes 3538948
  138.9 209.0 %reduce-scatter.4.cloned.1.call-start = ((), (), s32[]{:S(2)}) async-start(), calls=%async_computation.5 | async-start | bytes 7077888 | tf_op jit(solution)/shard_map/reduce_scatter | solution.py:1113
  143.3 64.7 %copy-start.61 = (bf16[384,1536]{1,0:T(8,128)(2,1)S(1)}, bf16[384,1536]{1,0:T(8,128)(2,1)}, u32[]{:S(2)}) copy-start(bf16[384,1536]{1,0:T(8,128)(2,1)} %param.22) | copy-start | bytes 3538948
  221.3 8.2 %slice-start = ((s8[6291456]{0:T(1024)(128)(4,1)}), s8[4194304]{0:T(1024)(128)(4,1)S(1)}, s32[]{:S(2)}) async-start(s8[6291456]{0:T(1024)(128)(4,1)} %bitcast.202), calls=%async_computation.9 | async-start | bytes 8388608
  224.3 5.2 slice-start.1
  233.3 150.9 %reduce-scatter.8.cloned.1.call-start = ((), (), s32[]{:S(2)}) async-start(), calls=%async_computation.7 | async-start | bytes 1474560 | tf_op jit(solution)/shard_map/reduce_scatter | solution.py:1131
  347.9 174.9 %all-gather.8.cloned.1.call-start = ((), (), s32[]{:S(2)}) async-start(), calls=%async_computation.8 | async-start | bytes 1474560 | tf_op jit(solution)/shard_map/all_gather | solution.py:1132
  350.1 29.9 %copy-start.14 = (bf16[2,1024,384]{2,1,0:T(8,128)(2,1)S(1)}, bf16[2,1024,384]{2,1,0:T(8,128)(2,1)}, u32[]{:S(2)}) copy-start(bf16[2,1024,384]{2,1,0:T(8,128)(2,1)} %copy-done.13) | copy-start | bytes 4718596
  350.1 29.9 %copy-start.21 = (bf16[384,256]{1,0:T(8,128)(2,1)S(1)}, bf16[384,256]{1,0:T(8,128)(2,1)}, u32[]{:S(2)}) copy-start(bf16[384,256]{1,0:T(8,128)(2,1)} %param.23) | copy-start | bytes 589828
  350.1 29.9 %copy-start.33 = (f32[384]{0:T(512)S(1)}, f32[384]{0:T(512)}, u32[]{:S(2)}) copy-start(f32[384]{0:T(512)} %copy-done.32) | copy-start | bytes 4612
  350.1 29.9 %copy-start.43 = (f32[384]{0:T(512)S(1)}, f32[384]{0:T(512)}, u32[]{:S(2)}) copy-start(f32[384]{0:T(512)} %copy-done.42) | copy-start | bytes 4612
  350.1 29.9 %copy-start.45 = (f32[384]{0:T(512)S(1)}, f32[384]{0:T(512)}, u32[]{:S(2)}) copy-start(f32[384]{0:T(512)} %copy-done.44) | copy-start | bytes 4612
  350.1 29.9 %copy-start.47 = (f32[384]{0:T(512)S(1)}, f32[384]{0:T(512)}, u32[]{:S(2)}) copy-start(f32[384]{0:T(512)} %copy-done.46) | copy-start | bytes 4612
  350.1 29.9 %copy-start.55 = (f32[384]{0:T(512)S(1)}, f32[384]{0:T(512)}, u32[]{:S(2)}) copy-start(f32[384]{0:T(512)} %copy-done.54) | copy-start | bytes 4612
  350.1 29.9 %copy-start.69 = (f32[2,2,1024,384]{3,2,1,0:T(8,128)S(1)}, f32[2,2,1024,384]{3,2,1,0:T(8,128)}, u32[]{:S(2)}) copy-start(f32[2,2,1024,384]{3,2,1,0:T(8,128)} %get-tuple-element.51) | copy-start | bytes 18874372
  380.0 4.2 copy-start.22
  380.1 4.2 copy-start.35
  380.1 4.2 copy-start.37
  380.1 4.2 copy-start.39
  380.1 4.2 copy-start.41
  380.1 4.2 copy-start.53
  384.2 141.7 %reduce-scatter.6.cloned.1.call-start = ((), (), s32[]{:S(2)}) async-start(), calls=%async_computation.6 | async-start | bytes 7077888 | tf_op jit(solution)/shard_map/reduce_scatter | solution.py:1159
  384.3 15.1 %copy-start.17 = (f32[2,1024,384]{2,1,0:T(8,128)S(1)}, f32[2,1024,384]{2,1,0:T(8,128)}, u32[]{:S(2)}) copy-start(f32[2,1024,384]{2,1,0:T(8,128)} %fusion.34) | copy-start | bytes 9437188
  399.4 2.9 copy-start.66
  399.4 2.9 copy-start.67
  402.3 7.1 %copy-start.18 = (bf16[2,1024,384]{2,1,0:T(8,128)(2,1)}, bf16[2,1024,384]{2,1,0:T(8,128)(2,1)S(1)}, u32[]{:S(2)}) copy-start(bf16[2,1024,384]{2,1,0:T(8,128)(2,1)S(1)} %add_convert_fusion) | copy-start | bytes 4718596
  419.5 4.9 copy-start.24
  419.5 4.9 copy-start.29
  419.5 4.9 copy-start.49
  419.5 4.9 copy-start.57
  420.2 4.2 copy-start.68
  522.9 5.1 copy-start.16
  522.9 5.2 copy-start.26
  522.9 5.2 copy-start.59
  553.5 5.9 %copy-start.6 = (f32[96,6144]{1,0:T(8,128)S(1)}, f32[96,6144]{1,0:T(8,128)}, u32[]{:S(2)}) copy-start(f32[96,6144]{1,0:T(8,128)} %copy-done.5) | copy-start | bytes 7077892
  553.5 10.5 %copy-start.1 = (bf16[192,6144]{1,0:T(8,128)(2,1)S(1)}, bf16[192,6144]{1,0:T(8,128)(2,1)}, u32[]{:S(2)}) copy-start(bf16[192,6144]{1,0:T(8,128)(2,1)} %param.21) | copy-start | bytes 7077892
  (14 other events, 22.6 us)
Sparse Core Ops, SparseCore 0:
  9.7 83.1 all-gather.3
  139.0 69.0 all-gather.5
  233.5 72.7 reduce-scatter.3
  348.1 31.6 reduce-scatter.7
  384.4 32.1 all-gather.7
  418.7 85.5 reduce-scatter.5

commit v3 on v2

--- a/solution.py
+++ b/solution.py
@@ -167,6 +167,145 @@
             one_direction(d == 1)
 
 
+def side_exchange(b_ref, q_ref, b_out, q_out, b_box, q_box, q_stage, *sems):
+    b_keep, q_keep, o_keep, p_keep = sems[:4]
+    (i_send, i_recv, j_send, j_recv, a_send, a_recv, z_send, z_recv, f_send, f_recv) = sems[4:]
+    shares, peers = q_ref.shape[0], q_ref.shape[1]
+    me, item = lax.axis_index("seq"), lax.axis_index("item")
+    step = pl.program_id(0) * pl.num_programs(1) + pl.program_id(1)
+    quarter = pl.num_programs(0) * pl.num_programs(1) // 4
+
+    def other(t):
+        return lax.rem(item + t, peers)
+
+    def origin(t):
+        return lax.rem(item - t + peers, peers)
+
+    def ahead(k):
+        return lax.rem(me + k, shares)
+
+    def behind(k):
+        return lax.rem(me - k + shares, shares)
+
+    def own_b():
+        return pltpu.make_async_copy(b_ref.at[item], b_box.at[0], b_keep)
+
+    def own_q():
+        return pltpu.make_async_copy(q_ref.at[:, item], q_box.at[0], q_keep)
+
+    def share_b(t):
+        return remote(b_ref.at[other(t)], b_box.at[t], i_send, i_recv, t - 1, "item", other(t))
+
+    def share_q(t):
+        return remote(q_ref.at[:, other(t)], q_box.at[t], a_send, a_recv, t - 1, "item", other(t))
+
+    def keep_b():
+        return pltpu.make_async_copy(b_box.at[0], b_out.at[item], o_keep)
+
+    def keep_q():
+        return pltpu.make_async_copy(q_stage.at[me], q_out.at[item, me], p_keep)
+
+    def give_b(t):
+        return remote(b_box.at[0], b_out.at[item], j_send, j_recv, t - 1, "item", other(t))
+
+    def place_q(k):
+        return remote(
+            q_stage.at[ahead(k)], q_out.at[item, me], z_send, z_recv, k, "seq", ahead(k)
+        )
+
+    def forward_q(k, t):
+        source = q_stage.at[me] if isinstance(k, int) else q_out.at[item, behind(k)]
+        return remote(
+            source,
+            q_out.at[item, behind(k)],
+            f_send,
+            f_recv,
+            k * (peers - 1) + t - 1,
+            "item",
+            other(t),
+        )
+
+    @pl.when(step == 0)
+    def _():
+        greet((("seq", me, shares), ("item", item, peers)))
+        each(1, peers, lambda t: share_q(t).start())
+        each(1, peers, lambda t: share_b(t).start())
+        own_b().start()
+        own_q().start()
+
+    @pl.when(step == quarter)
+    def _():
+        own_q().wait()
+        own_b().wait()
+
+        def arrived(t):
+            share_q(t).wait_recv()
+            share_b(t).wait_recv()
+
+        each(1, peers, arrived)
+
+        def sum_q(p):
+            def add(t, total):
+                return total + q_box[t, p].astype(f32)
+
+            q_stage[p] = lax.fori_loop(1, peers, add, q_box[0, p].astype(f32)).astype(bf16)
+
+        each(0, shares, sum_q)
+        rows = 16 if b_box.shape[1] % 16 == 0 else b_box.shape[1]
+
+        def sum_b(r):
+            place = pl.ds(pl.multiple_of(r * rows, rows), rows)
+
+            def add(t, total):
+                return total + b_box[t, place, :].astype(f32)
+
+            total = lax.fori_loop(1, peers, add, b_box[0, place, :].astype(f32))
+            b_box[0, place, :] = total.astype(bf16)
+
+        each(0, b_box.shape[1] // rows, sum_b)
+        each(1, shares, lambda k: place_q(k).start())
+        each(1, peers, lambda t: forward_q(0, t).start())
+        each(1, peers, lambda t: give_b(t).start())
+        keep_b().start()
+        keep_q().start()
+
+    @pl.when(step == 2 * quarter)
+    def _():
+        def pass_on(k):
+            block = q_out.at[item, behind(k)]
+            remote(block, block, z_send, z_recv, k, "seq", behind(k)).wait_recv()
+            each(1, peers, lambda t: forward_q(k, t).start())
+
+        each(1, shares, pass_on)
+
+    @pl.when(step == 3 * quarter)
+    def _():
+        keep_b().wait()
+        keep_q().wait()
+
+        def finish(t):
+            block = b_out.at[origin(t)]
+            remote(block, block, j_send, j_recv, t - 1, "item", other(t)).wait_recv()
+            give_b(t).wait_send()
+            share_b(t).wait_send()
+            share_q(t).wait_send()
+
+        each(1, peers, finish)
+
+        def finish_q(k):
+            def one(t):
+                block = q_out.at[origin(t), behind(k)]
+                remote(
+                    block, block, f_send, f_recv, k * (peers - 1) + t - 1, "item", other(t)
+                ).wait_recv()
+                forward_q(k, t).wait_send()
+
+            each(1, peers, one)
+
+        each(0, shares, finish_q)
+        each(1, shares, lambda k: place_q(k).wait_send())
+
+
 def adjoint_kernel(
     count,
     sel_ref,
@@ -179,21 +318,28 @@
     g_ref,
     h_ref,
     edge_ref,
+    b_ref,
+    q_ref,
     low_ref,
     input_ref,
     gsel_ref,
     decay_ref,
     sums_ref,
+    b_out,
+    q_out,
     pending,
     bc,
     coefs,
     even,
     odd,
+    *side,
 ):
     slots, width = dt_ref.shape[1], dt_ref.shape[3]
     groups = width // lanes
     states = r_ref.shape[1]
     last_block = pl.program_id(1) == pl.num_programs(1) - 1
+
+    side_exchange(b_ref, q_ref, b_out, q_out, *side)
 
     @pl.when(pl.program_id(1) == 0)
     def _():
@@ -373,7 +519,7 @@
     )(selection, x, weight, bias, rate, copies)
 
 
-def scan_adjoint(selection, x, weight, rate, copies, skip, dt, g, h):
+def scan_adjoint(selection, x, weight, rate, copies, skip, dt, g, h, b, q):
     two, slots, length, width = dt.shape
     select = selection.shape[3]
     states = rate.shape[1]
@@ -381,6 +527,8 @@
     block = block_of(length)
     blocks = length // block
     spread = copies.shape[1]
+    shares, peers = q.shape[:2]
+    anywhere, dma = pl.BlockSpec(memory_space=pl.ANY), pltpu.SemaphoreType.DMA
 
     def at(d, i):
         return jnp.where(d == 1, i, blocks - 1 - i)
@@ -409,6 +557,8 @@
             pl.BlockSpec((slots, block, width), lambda d, i: (0, at(d, i), 0)),
             pl.BlockSpec((1, slots, block * states, width), where),
             pl.BlockSpec((1, slots, states, width), edge),
+            anywhere,
+            anywhere,
         ],
         out_specs=[
             pl.BlockSpec((1, slots, block, width), where),
@@ -416,6 +566,8 @@
             pl.BlockSpec((1, slots, block, select), where),
             pl.BlockSpec((1, slots, states, width), lambda d, i: (d, 0, 0, 0)),
             pl.BlockSpec((1, 16, width), by_direction),
+            anywhere,
+            anywhere,
         ],
         out_shape=[
             jax.ShapeDtypeStruct((two, slots, length, width), bf16),
@@ -423,6 +575,8 @@
             jax.ShapeDtypeStruct((two, slots, length, select), bf16),
             jax.ShapeDtypeStruct((two, slots, states, width), f32),
             jax.ShapeDtypeStruct((two, 16, width), f32),
+            jax.ShapeDtypeStruct(b.shape, bf16),
+            jax.ShapeDtypeStruct((peers, shares) + q.shape[2:], bf16),
         ],
         scratch_shapes=[
             pltpu.VMEM((slots, states, width), f32),
@@ -430,13 +584,22 @@
             pltpu.VMEM((slots, block // chunk * 8, chunk * states), f32),
             pltpu.VMEM((slots, chunk * states, 2 * lanes), f32),
             pltpu.VMEM((slots, chunk * states, 2 * lanes), f32),
-        ],
-        compiler_params=pltpu.CompilerParams(vmem_limit_bytes=48 * 2**20),
+            pltpu.VMEM(b.shape, bf16),
+            pltpu.VMEM((peers, shares) + q.shape[2:], bf16),
+            pltpu.VMEM((shares,) + q.shape[2:], bf16),
+        ]
+        + [dma] * 4
+        + [dma((peers - 1,))] * 6
+        + [dma((shares,))] * 2
+        + [dma((shares * (peers - 1),))] * 2,
+        compiler_params=pltpu.CompilerParams(
+            collective_id=6, has_side_effects=True, vmem_limit_bytes=48 * 2**20
+        ),
         cost_estimate=pl.CostEstimate(
             flops=100 * 10**9, bytes_accessed=100 * 2**20, transcendentals=hidden_size
         ),
         name="scan_adjoint",
-    )(selection, x, weight, rate, copies, skip, dt, g, h, h)
+    )(selection, x, weight, rate, copies, skip, dt, g, h, h, b, q)
 
 
 def coefficient_copies(width, rank, states):
@@ -604,11 +767,51 @@
     return out.reshape(v.shape)
 
 
-def head_kernel(w_ref, mod_ref, box_ref, out_ref, parts, *sems):
-    keep, w_send, w_recv, f_send, f_recv, m_send, m_recv = sems
+def head_kernel(line, t_ref, w_ref, mod_ref, all_ref, box_ref, out_ref, parts, *sems):
+    keep, t_keep, u_send, u_recv, d_send, d_recv, p_send, p_recv = sems[:8]
+    w_send, w_recv, f_send, f_recv, m_send, m_recv = sems[8:]
     shares, peers = box_ref.shape[0], box_ref.shape[1]
+    slots, local = t_ref.shape[0], t_ref.shape[1]
     me, item = lax.axis_index("seq"), lax.axis_index("item")
+    pos, core = me // 2, lax.rem(me, 2)
+    partner = me + 1 - 2 * core
     greet((("seq", me, shares), ("item", item, peers)))
+
+    def region(q, c, s):
+        first = pl.multiple_of((q * 2 + c) * local, local)
+        return all_ref.at[s, pl.ds(first, local), :]
+
+    def hop(q, s, source, sends, recvs, k, to):
+        return remote(source, region(q, core, s), sends, recvs, k * slots + s, "seq", to)
+
+    def up(k, s):
+        source = t_ref.at[s] if isinstance(k, int) else region(pos - k, core, s)
+        return hop(pos - k, s, source, u_send, u_recv, k, me + 2)
+
+    def down(k, s):
+        source = t_ref.at[s] if isinstance(k, int) else region(pos + k, core, s)
+        return hop(pos + k, s, source, d_send, d_recv, k, me - 2)
+
+    def across(q, s):
+        return remote(
+            region(q, core, s), region(q, core, s), p_send, p_recv, q * slots + s, "seq", partner
+        )
+
+    def own_across(s):
+        return remote(
+            t_ref.at[s], region(pos, core, s), p_send, p_recv, pos * slots + s, "seq", partner
+        )
+
+    not_last, not_first = pos < line - 1, pos > 0
+    for s in range(slots):
+
+        @pl.when(not_last)
+        def _():
+            up(0, s).start()
+
+        @pl.when(not_first)
+        def _():
+            down(0, s).start()
 
     def modulation(k):
         return remote(
@@ -619,19 +822,21 @@
         to = lax.rem(me + k, shares)
         return remote(w_ref.at[to], box_ref.at[me, item], w_send, w_recv, k, "seq", to)
 
+    each(1, shares, lambda k: modulation(k).start())
     each(1, shares, lambda k: weight(k).start())
-    each(1, shares, lambda k: modulation(k).start())
     own = pltpu.make_async_copy(w_ref.at[me], box_ref.at[me, item], keep)
     own.start()
+    kept = []
+    for s in range(slots):
+        own_across(s).start()
+        kept.append(pltpu.make_async_copy(t_ref.at[s], region(pos, core, s), t_keep.at[s]))
+        kept[-1].start()
 
     def forward(k, t):
         block = box_ref.at[lax.rem(me - k + shares, shares), item]
         return remote(
             block, block, f_send, f_recv, k * (peers - 1) + t - 1, "item", lax.rem(item + t, peers)
         )
-
-    own.wait()
-    each(1, peers, lambda t: forward(0, t).start())
 
     def pass_on(k):
         source = lax.rem(me - k + shares, shares)
@@ -639,13 +844,44 @@
         remote(block, block, w_send, w_recv, k, "seq", source).wait_recv()
         each(1, peers, lambda t: forward(k, t).start())
 
-    each(1, shares, pass_on)
+    def relay(k):
+        for s in range(slots):
+
+            @pl.when(k < pos)
+            def _():
+                q = pos - 1 - k
+                hop(q, s, region(q, core, s), u_send, u_recv, k, partner).wait_recv()
+
+                @pl.when(not_last)
+                def _():
+                    up(k + 1, s).start()
+
+                across(q, s).start()
+
+            @pl.when(k < line - 1 - pos)
+            def _():
+                q = pos + 1 + k
+                hop(q, s, region(q, core, s), d_send, d_recv, k, partner).wait_recv()
+
+                @pl.when(not_first)
+                def _():
+                    down(k + 1, s).start()
+
+                across(q, s).start()
+
+    own.wait()
+    each(1, peers, lambda t: forward(0, t).start())
+    half = shares // 2
+    each(1, half, pass_on)
+    each(0, 1, relay)
+    each(half, shares, pass_on)
 
     def add(k, total):
         modulation(k).wait_recv()
         return total + parts[k - 1]
 
     out_ref[...] = lax.fori_loop(1, shares, add, mod_ref[...])
+    each(1, line - 1, relay)
 
     def finish(k):
         def one(t):
@@ -666,45 +902,74 @@
 
     each(1, shares, drain)
 
-
-def input_columns(blocks, modulation):
+    def drain_tokens(q):
+        for s in range(slots):
+            remote(
+                region(q, core, s),
+                region(q, 1 - core, s),
+                p_send,
+                p_recv,
+                q * slots + s,
+                "seq",
+                partner,
+            ).wait_recv()
+            across(q, s).wait_send()
+
+    each(0, line, drain_tokens)
+
+    def drain_line(k):
+        for s in range(slots):
+
+            @pl.when(not_last & (k <= pos))
+            def _():
+                up(k, s).wait_send()
+
+            @pl.when(not_first & (k <= line - 1 - pos))
+            def _():
+                down(k, s).wait_send()
+
+    each(0, line, drain_line)
+    for copy in kept:
+        copy.wait()
+
+
+def gather_inputs(tokens, blocks, modulation):
     shares, peers = lax.axis_size("seq"), lax.axis_size("item")
+    slots, local, model = tokens.shape
+    line = shares // 2
     vmem, anywhere = pl.BlockSpec(memory_space=pltpu.VMEM), pl.BlockSpec(memory_space=pl.ANY)
     dma = pltpu.SemaphoreType.DMA
     return pl.pallas_call(
-        head_kernel,
-        in_specs=[anywhere, vmem],
-        out_specs=[anywhere, vmem],
+        functools.partial(head_kernel, line),
+        in_specs=[anywhere, anywhere, vmem],
+        out_specs=[anywhere, anywhere, vmem],
         out_shape=[
+            jax.ShapeDtypeStruct((slots, local * shares, model), bf16),
             jax.ShapeDtypeStruct((shares, peers) + blocks.shape[1:], bf16),
             jax.ShapeDtypeStruct(modulation.shape, f32),
         ],
-        scratch_shapes=[
-            pltpu.VMEM((shares - 1,) + modulation.shape, f32),
-            dma,
-            dma((shares,)),
-            dma((shares,)),
-            dma((shares * (peers - 1),)),
-            dma((shares * (peers - 1),)),
-            dma((shares,)),
-            dma((shares,)),
-        ],
+        scratch_shapes=[pltpu.VMEM((shares - 1,) + modulation.shape, f32), dma, dma((slots,))]
+        + [dma((line * slots,))] * 6
+        + [dma((shares,))] * 2
+        + [dma((shares * (peers - 1),))] * 2
+        + [dma((shares,))] * 2,
         compiler_params=pltpu.CompilerParams(collective_id=1, has_side_effects=True),
-        cost_estimate=pl.CostEstimate(flops=40 * 10**9, bytes_accessed=2**20, transcendentals=0),
-        name="input_columns",
-    )(blocks, modulation)
-
-
-def tail_kernel(cuts, g_ref, small_ref, select_ref, *refs):
+        cost_estimate=pl.CostEstimate(flops=60 * 10**9, bytes_accessed=2**20, transcendentals=0),
+        name="gather_inputs",
+    )(tokens, blocks, modulation)
+
+
+def tail_kernel(cuts, m_ref, g_ref, gate_ref, small_ref, select_ref, m_out, *refs):
     if cuts is None:
         g_out, small_out, select_out, *refs = refs
     else:
         in_final, select_final, *refs = refs
         finals, refs = refs[: len(cuts)], refs[len(cuts) :]
         g_out, small_out, select_out, *refs = refs
-    g_box, small_box, select_box, g_stage, *sems = refs
+    m_parts, g_box, small_box, select_box, g_stage, *sems = refs
     (a_send, a_recv, s_send, s_recv, c_send, c_recv, z_send, z_recv, y_send, y_recv) = sems[:10]
-    f_send, f_recv, h_send, h_recv, e_send, e_recv = sems[10:]
+    f_send, f_recv, h_send, h_recv, e_send, e_recv = sems[10:16]
+    m_send, m_recv, n_send, n_recv = sems[16:]
     shares, peers = g_ref.shape[0], g_ref.shape[1]
     me, item = lax.axis_index("seq"), lax.axis_index("item")
     greet((("seq", me, shares), ("item", item, peers)))
@@ -740,6 +1005,14 @@
             g_ref.at[p, other(t)], g_box.at[t - 1, p], a_send, a_recv, flat(k, t), "item", other(t)
         )
 
+    def part(k):
+        return remote(m_ref, m_parts.at[k - 1], m_send, m_recv, k - 1, "seq", ahead(k))
+
+    def forward_modulation(t):
+        block = m_out.at[item]
+        return remote(block, block, n_send, n_recv, t - 1, "item", other(t))
+
+    each(1, shares, lambda k: part(k).start())
     each(1, peers, lambda t: share_small(t).start())
     each(1, shares, lambda k: each(1, peers, lambda t: share_in(k, t).start()))
     each(1, peers, lambda t: share_in(0, t).start())
@@ -790,6 +1063,13 @@
 
     each(1, peers, lambda t: forward_in(0, t).start())
     each(1, peers, lambda t: forward_small(0, t).start())
+
+    def add_part(k, total):
+        part(k).wait_recv()
+        return total + m_parts[k - 1]
+
+    m_out[item] = lax.fori_loop(1, shares, add_part, m_ref[...])
+    each(1, peers, lambda t: forward_modulation(t).start())
 
     def add_select(t, total):
         share_select(t).wait_recv()
@@ -815,17 +1095,23 @@
 
     each(1, shares, pass_on)
 
+    def widen_half(block, half, j, s):
+        rows, mine = block.shape
+        inner = in_final.shape[1] // 2
+        place = pl.ds(pl.multiple_of(j * rows, rows), rows)
+        first = pl.multiple_of(s * mine + half * inner, lanes)
+        in_final[place, pl.ds(first, mine)] = block.astype(f32)
+
     def widen_in(j, s):
-        if cuts is None:
-            return
-        rows, mine = g_ref.shape[2], g_ref.shape[3] // 2
-        inner = in_final.shape[1] // 2
-        block = g_out[j, s].astype(f32)
-        place = pl.ds(pl.multiple_of(j * rows, rows), rows)
-        for half in range(2):
-            first = pl.multiple_of(s * mine + half * inner, lanes)
-            in_final[place, pl.ds(first, mine)] = block[:, half * mine : (half + 1) * mine]
-
+        if cuts is not None:
+            widen_half(g_out[j, s], 0, j, s)
+
+    if cuts is not None:
+        each(
+            0,
+            peers,
+            lambda j: each(0, shares, lambda s: widen_half(gate_ref[j, s], 1, j, s)),
+        )
     each(0, shares, lambda k: widen_in(item, behind(k)))
 
     def finish(k):
@@ -847,6 +1133,9 @@
         block = select_out.at[origin(t)]
         remote(block, block, e_send, e_recv, t - 1, "item", other(t)).wait_recv()
         forward_select(t).wait_send()
+        block = m_out.at[origin(t)]
+        remote(block, block, n_send, n_recv, t - 1, "item", other(t)).wait_recv()
+        forward_modulation(t).wait_send()
         share_small(t).wait_send()
         share_select(t).wait_send()
 
@@ -855,6 +1144,7 @@
     def finish_seq(k):
         spread_small(k).wait_send()
         place_in(k).wait_send()
+        part(k).wait_send()
 
     each(1, shares, finish_seq)
     if cuts is None:
@@ -874,30 +1164,33 @@
                 first += cut
 
 
-def weight_sums(g, small, select, cuts):
+def weight_sums(modulation, g, gate, small, select, cuts):
     shares, peers = g.shape[:2]
     vmem = pl.BlockSpec(memory_space=pltpu.VMEM)
     dma = pltpu.SemaphoreType.DMA
     some = peers - 1
     sizes = [shares * some] * 2 + [some] * 4 + [shares] * 4 + [shares * some] * 4 + [some] * 2
+    sizes += [shares] * 2 + [some] * 2
     kept = [
         ((peers, shares) + g.shape[2:], bf16),
         ((peers, shares) + small.shape[1:], bf16),
         (select.shape, bf16),
     ]
-    inner2 = shares * g.shape[3]
-    direct = (g.shape[3] // 2) % lanes == 0
+    inner2 = 2 * shares * g.shape[3]
+    direct = g.shape[3] % lanes == 0
     outs = kept
     if direct:
         outs = [((peers * g.shape[2], inner2), f32), ((peers * select.shape[1], select.shape[2]), f32)]
         outs += [((cut, inner2), f32) for cut in cuts]
+    outs = [((peers,) + modulation.shape, f32)] + outs
     return pl.pallas_call(
         functools.partial(tail_kernel, cuts if direct else None),
-        in_specs=[vmem] * 3,
+        in_specs=[vmem] * 5,
         out_specs=[vmem] * len(outs),
         out_shape=[jax.ShapeDtypeStruct(shape, kind) for shape, kind in outs],
         scratch_shapes=[pltpu.VMEM(shape, kind) for shape, kind in kept if direct]
         + [
+            pltpu.VMEM((shares - 1,) + modulation.shape, f32),
             pltpu.VMEM((some, shares) + g.shape[2:], bf16),
             pltpu.VMEM((some,) + small.shape[1:], bf16),
             pltpu.VMEM((some,) + select.shape[1:], bf16),
@@ -909,62 +1202,7 @@
         ),
         cost_estimate=pl.CostEstimate(flops=60 * 10**9, bytes_accessed=2**20, transcendentals=0),
         name="weight_sums",
-    )(g, small, select)
-
-
-def modulation_kernel(v_ref, out_ref, parts, m_send, m_recv, f_send, f_recv):
-    shares = parts.shape[0] + 1
-    peers = out_ref.shape[0]
-    me, item = lax.axis_index("seq"), lax.axis_index("item")
-    greet((("seq", me, shares), ("item", item, peers)))
-
-    def part(k):
-        return remote(v_ref, parts.at[k - 1], m_send, m_recv, k - 1, "seq", lax.rem(me + k, shares))
-
-    each(1, shares, lambda k: part(k).start())
-
-    def add(k, total):
-        part(k).wait_recv()
-        return total + parts[k - 1]
-
-    out_ref[item] = lax.fori_loop(1, shares, add, v_ref[...])
-
-    def forward(t):
-        block = out_ref.at[item]
-        return remote(block, block, f_send, f_recv, t - 1, "item", lax.rem(item + t, peers))
-
-    each(1, peers, lambda t: forward(t).start())
-
-    def finish(t):
-        source = lax.rem(item - t + peers, peers)
-        block = out_ref.at[source]
-        remote(block, block, f_send, f_recv, t - 1, "item", source).wait_recv()
-        forward(t).wait_send()
-
-    each(1, peers, finish)
-    each(1, shares, lambda k: part(k).wait_send())
-
-
-def modulation_sums(v):
-    shares, peers = lax.axis_size("seq"), lax.axis_size("item")
-    vmem = pl.BlockSpec(memory_space=pltpu.VMEM)
-    dma = pltpu.SemaphoreType.DMA
-    return pl.pallas_call(
-        modulation_kernel,
-        in_specs=[vmem],
-        out_specs=vmem,
-        out_shape=jax.ShapeDtypeStruct((peers,) + v.shape, f32),
-        scratch_shapes=[
-            pltpu.VMEM((shares - 1,) + v.shape, f32),
-            dma((shares,)),
-            dma((shares,)),
-            dma((peers,)),
-            dma((peers,)),
-        ],
-        compiler_params=pltpu.CompilerParams(collective_id=3, has_side_effects=True),
-        cost_estimate=pl.CostEstimate(flops=10 * 10**9, bytes_accessed=2**20, transcendentals=0),
-        name="modulation_sums",
-    )(v)
+    )(modulation, g, gate, small, select)
 
 
 def filter_windows(x, taps, reverse):
@@ -1026,8 +1264,8 @@
         in_weight, lax.axis_index("item") * share_rows, share_rows, 0
     )
     own_rows = jnp.moveaxis(own_rows.reshape(share_rows, 2, shares, mine), 2, 0)
-    own_in, modulation = input_columns(
-        own_rows.reshape(shares, share_rows, 2 * mine), modulation_part
+    all_tokens, own_in, modulation = gather_inputs(
+        tokens, own_rows.reshape(shares, share_rows, 2 * mine), modulation_part
     )
     own_in = own_in.reshape(model, 2 * mine)
     modulation = modulation + modulation_bias.astype(f32)[None, :]
@@ -1035,7 +1273,6 @@
     scale = modulation[:, None, model : 2 * model]
     gate = modulation[:, None, 2 * model :]
 
-    all_tokens = lax.all_gather(tokens, "seq", axis=1, tiled=True)
     source = all_tokens.astype(f32)
     centered = source - jnp.mean(source, axis=-1, keepdims=True)
     spread = lax.rsqrt(jnp.mean(centered * centered, axis=-1, keepdims=True) + epsilon)
@@ -1071,8 +1308,10 @@
     selection = summed_everywhere(
         jnp.stack(partial).astype(bf16).reshape(2 * slots, length, select), 4
     ).reshape(2, rows, select)
-    selection, late_cotangent = lax.optimization_barrier((selection, cotangent))
-    all_cotangent = lax.all_gather(late_cotangent, "seq", axis=1, tiled=True)
+    own_cotangent = cotangent.astype(f32)
+    own_grad_branch = (valid * gate * own_cotangent).astype(bf16)
+    selection, own_grad_branch = lax.optimization_barrier((selection, own_grad_branch))
+    grad_branch = lax.all_gather(own_grad_branch, "seq", axis=1, tiled=True).reshape(rows, model)
     delta_rank = selection[:, :, :rank]
     selection = selection.reshape(2, slots, length, select)
     copies = coefficient_copies(select, rank, states)
@@ -1093,11 +1332,6 @@
         scanned_sum = scanned_sum + skip[d] * activated[d].astype(f32)
     silu_gate = jax.nn.silu(gate_half)
     mixed_out = (scanned_sum * silu_gate).astype(bf16).reshape(rows, mine)
-    own_cotangent = cotangent.astype(f32)
-
-    grad_branch = (
-        (valid * gate * all_cotangent.astype(f32)).astype(bf16).reshape(rows, model)
-    )
     grad_mixed = dot_cols(grad_branch, out_weight).reshape(slots, length, mine)
     grad_scanned = grad_mixed * silu_gate
     grad_gate_half = grad_mixed * scanned_sum * silu_slope(gate_half)
@@ -1107,11 +1341,13 @@
         .astype(bf16)
         .reshape(slots, length, model)
     )
-    branch_part, grad_out, scan_grad = lax.optimization_barrier(
-        (branch_part, grad_out, grad_scanned)
+    grad_gate_half = grad_gate_half.astype(bf16)
+    grad_in_gate = dot_rows(mixed_in, grad_gate_half.reshape(rows, mine)).astype(bf16)
+    branch_part, grad_out, grad_in_gate, scan_grad = lax.optimization_barrier(
+        (branch_part, grad_out, grad_in_gate, grad_scanned)
     )
     branch_part = lax.psum_scatter(branch_part, "seq", scatter_dimension=1, tiled=True)
-    grad_low, grad_input, grad_parts, grad_rate, grad_sums = scan_adjoint(
+    grad_low, grad_input, grad_parts, grad_rate, grad_sums, grad_out, gate_in = scan_adjoint(
         selection,
         wide_active,
         wide_weight,
@@ -1121,15 +1357,14 @@
         step,
         widen(scan_grad, padded_width),
         hidden,
-    )
+        grad_out.reshape(peers, mine // peers, model),
+        grad_in_gate.reshape(shares, peers, share_rows, mine),
+    )
+    grad_out = grad_out.reshape(mine, model).astype(f32)
     grad_decay = jnp.sum(grad_rate, axis=1)[..., :mine] * ln2
     grad_step_bias = jnp.sum(grad_sums[:, :8, :mine], axis=1)
     grad_skip = jnp.sum(grad_sums[:, 8:, :mine], axis=1)
-    grad_parts, grad_out, branch_part = lax.optimization_barrier(
-        (grad_parts, grad_out, branch_part)
-    )
-    grad_out = lax.psum_scatter(grad_out, "item", scatter_dimension=0, tiled=True)
-    grad_out = lax.all_gather(grad_out, "item", axis=0, tiled=True)
+    grad_parts, branch_part = lax.optimization_barrier((grad_parts, branch_part))
     grad_selection = summed_everywhere(
         grad_parts.reshape(2 * slots, length, select), 5
     ).reshape(2, rows, select)
@@ -1153,43 +1388,24 @@
         )
         for j, window in enumerate(filter_windows(grad_filtered, taps, d == 0)):
             grad_x = grad_x + tap_weight[j, d] * window
+    grad_x = grad_x.astype(bf16)
     grad_projected = (
-        jnp.concatenate([grad_x, grad_gate_half], axis=2).astype(bf16).reshape(rows, 2 * mine)
-    )
-    grad_mixed_in = lax.psum_scatter(
-        dot_cols(grad_projected, own_in).astype(bf16).reshape(slots, length, model),
-        "seq",
-        scatter_dimension=1,
-        tiled=True,
-    ).astype(f32)
-    grad_in = dot_rows(mixed_in, grad_projected).astype(bf16)
-    own_source = tokens.astype(f32)
-    own_centered = own_source - jnp.mean(own_source, axis=-1, keepdims=True)
-    own_spread = lax.rsqrt(
-        jnp.mean(own_centered * own_centered, axis=-1, keepdims=True) + epsilon
-    )
-    normed = own_centered * own_spread
-    grad_normed = grad_mixed_in * (1.0 + scale)
-    grad_source = own_spread * (
-        grad_normed
-        - jnp.mean(grad_normed, axis=-1, keepdims=True)
-        - normed * jnp.mean(grad_normed * normed, axis=-1, keepdims=True)
-    )
-    grad_tokens = (own_cotangent + grad_source).astype(bf16)
+        jnp.concatenate([grad_x, grad_gate_half], axis=2).reshape(rows, 2 * mine)
+    )
+    mixed_part = dot_cols(grad_projected, own_in).astype(bf16).reshape(slots, length, model)
+    grad_mixed_in = lax.psum_scatter(mixed_part, "seq", scatter_dimension=1, tiled=True)
+    wide_part = mixed_part.astype(f32)
+    grad_modulation_part = jnp.concatenate(
+        [
+            jnp.sum(wide_part, axis=1),
+            jnp.sum(wide_part * (centered * spread), axis=1),
+            jnp.sum(valid * own_cotangent * branch_part.astype(f32), axis=1),
+        ],
+        axis=1,
+    )
+    grad_in = dot_rows(mixed_in, grad_x.reshape(rows, mine)).astype(bf16)
     branch = branch_part.astype(f32)
     output = (tokens.astype(f32) + valid * gate * branch).astype(bf16)
-    grad_gate = jnp.sum(valid * own_cotangent * branch, axis=1)
-    grad_modulation = jnp.concatenate(
-        [jnp.sum(grad_mixed_in, axis=1), jnp.sum(grad_mixed_in * normed, axis=1), grad_gate], axis=1
-    )
-    grad_modulation = modulation_sums(grad_modulation).reshape(-1, 3 * model)
-    grad_modulation_weight = lax.dot_general(
-        own_features.astype(f32),
-        grad_modulation,
-        (((0,), (0,)), ((), ())),
-        precision=lax.Precision.HIGHEST,
-        preferred_element_type=f32,
-    )
     small = jnp.concatenate(
         [
             jnp.stack(grad_delta, 1),
@@ -1208,18 +1424,43 @@
     )
     grad_select = jnp.concatenate(grad_select, axis=1).astype(bf16)
     cuts = [rank, states, taps, 1, 1, 1]
-    results = weight_sums(
-        grad_in.reshape(shares, peers, share_rows, 2 * mine),
+    grad_modulation, *results = weight_sums(
+        grad_modulation_part,
+        grad_in.reshape(shares, peers, share_rows, mine),
+        gate_in,
         small.reshape(peers, share, 2 * mine),
         grad_select.reshape(peers, mine // peers, 2 * select),
         cuts,
+    )
+    grad_modulation, grad_mixed_in = lax.optimization_barrier((grad_modulation, grad_mixed_in))
+    grad_mixed_in = grad_mixed_in.astype(f32)
+    grad_modulation = grad_modulation.reshape(-1, 3 * model)
+    own_source = tokens.astype(f32)
+    own_centered = own_source - jnp.mean(own_source, axis=-1, keepdims=True)
+    own_spread = lax.rsqrt(
+        jnp.mean(own_centered * own_centered, axis=-1, keepdims=True) + epsilon
+    )
+    normed = own_centered * own_spread
+    grad_normed = grad_mixed_in * (1.0 + scale)
+    grad_source = own_spread * (
+        grad_normed
+        - jnp.mean(grad_normed, axis=-1, keepdims=True)
+        - normed * jnp.mean(grad_normed * normed, axis=-1, keepdims=True)
+    )
+    grad_tokens = (own_cotangent + grad_source).astype(bf16)
+    grad_modulation_weight = lax.dot_general(
+        own_features.astype(f32),
+        grad_modulation,
+        (((0,), (0,)), ((), ())),
+        precision=lax.Precision.HIGHEST,
+        preferred_element_type=f32,
     )
     if mine % lanes == 0:
         grad_in, grad_select, *small = results
     else:
         grad_in, small, grad_select = results
-        grad_in = grad_in.reshape(peers, shares, share_rows, 2, mine)
-        grad_in = jnp.transpose(grad_in, (0, 2, 3, 1, 4)).reshape(peers * share_rows, 2 * inner)
+        grad_in = jnp.stack([grad_in, gate_in]).reshape(2, peers, shares, share_rows, mine)
+        grad_in = jnp.transpose(grad_in, (1, 3, 0, 2, 4)).reshape(peers * share_rows, 2 * inner)
         grad_in = grad_in.astype(f32)
         small = small.reshape(peers, shares, share, 2, mine)
         small = jnp.transpose(small, (0, 2, 3, 1, 4)).reshape(peers * share, 2 * inner).astype(f32)
@@ -1230,7 +1471,7 @@
         output,
         grad_tokens,
         grad_in,
-        grad_out.astype(f32),
+        grad_out,
         grad_select,
         grad_modulation_weight,
         small[0],

time: 581 us -> 540 us (0.929)
  waiting for transfers between devices: 35.4 us -> 4.12 us
  starting transfers between devices: 10.9 us -> 0.12 us
  matrix products: 76.7 us -> 68.2 us
    all_gather x3 -> x1, waiting for transfers between devices: 34.6 us -> 4.07 us  [per_device(): lax.all_gather(own_grad_branch, 'seq', axis=1, tiled=True)]
    pallas_call x1, Pallas kernels: 85.7 us -> 62.4 us  [weight_sums(): pl.pallas_call(functools.partial(tail_kernel, cuts if direct else None),...]
    pallas_call x2 -> x1, Pallas kernels: 59.2 us -> 76 us  [gather_inputs(): pl.pallas_call(functools.partial(head_kernel, line), in_specs=[anywhere,...]
    reduce_scatter x2 -> x1, starting transfers between devices: 10.5 us -> 0.04 us  [per_device(): lax.psum_scatter(mixed_part, 'seq', scatter_dimension=1, tiled=True)]
    dot_general x4, matrix products: 39.4 us -> 29.6 us  [dot_cols(): lax.dot_general(a, b, (((1,), (1,)), ((), ())), preferred_element_type=f32)]
    pallas_call x1, Pallas kernels: 102 us -> 110 us  [scan_adjoint(): pl.pallas_call(functools.partial(adjoint_kernel, block // chunk), grid=(t...]
    convert_element_type x1 -> x4, other arithmetic: 3.04 us -> 8.85 us  [the longest x1 3.18 us: per_device(): grad_tokens = (own_cotangent + grad_source).astype(bf16)]
    dot_general x6 -> x7, matrix products: 17.9 us -> 20.3 us  [dot_rows(): lax.dot_general(a, b, (((0,), (0,)), ((), ())), preferred_element_type=f32)]
  transfers between devices with their start and end apart: 6 -> 3, of which waited for: 2 -> 1; matrix products, arithmetic and copies ran while one was open for 11% -> 5% of each run, Pallas kernels for 57% -> 44%
where the time goes in v3:
time: 540 us; the launch traced here: 530 us
  Pallas kernels  367 us (68%)
  matrix products  68.2 us (13%)
  local copies, waits for them, and re-layouts  39.2 us (7%)
  other arithmetic  34.9 us (6%)
  between operations  15.8 us (3%)
    pallas_call x1, Pallas kernels, scan_adjoint(): pl.pallas_call(functools.partial(adjoint_kernel, block // chunk), grid=(t...  110 us
    pallas_call x1, Pallas kernels, gather_inputs(): pl.pallas_call(functools.partial(head_kernel, line), in_specs=[anywhere,...  76 us
    pallas_call x1, Pallas kernels, weight_sums(): pl.pallas_call(functools.partial(tail_kernel, cuts if direct else None),...  62.4 us
    pallas_call x1, Pallas kernels, scan_states(): pl.pallas_call(functools.partial(states_kernel, block // chunk), grid=(tw...  61.6 us
    pallas_call x2, Pallas kernels, summed_everywhere(): pl.pallas_call(functools.partial(total_kernel, line), in_specs=[vmem], ou...  56.9 us
    dot_general x4, matrix products, dot_cols(): lax.dot_general(a, b, (((1,), (1,)), ((), ())), preferred_element_type=f32)  29.6 us
    unnamed x209, local copies, waits for them, and re-layouts  26.2 us
    dot_general x7, matrix products, dot_rows(): lax.dot_general(a, b, (((0,), (0,)), ((), ())), preferred_element_type=f32)  20.3 us
  transfers between devices with their start and end apart: 3, of which 1 were waited for; matrix products, arithmetic and copies ran while one was open for 5% of the time, Pallas kernels for 44%

profile of v3, /device:TPU:0, one launch (start us, length us, event | category | flops | bytes accessed | tf_op | source)
XLA Modules:
  0.0 529.6 jit_solution(3111781204822489225)
XLA Ops:
  7.3 1.6 copy-done
  9.5 1.2 reshape.231.w_ref
  11.0 1.0 fusion.90.mod_ref
  12.0 76.0 %gather_inputs.1 = (bf16[2,1024,1536]{2,1,0:T(8,128)(2,1)}, bf16[8,4,48,768]{3,2,1,0:T(8,128)(2,1)}, f32[2,4608]{1,0:T(2,128)}) custom-call(bf16[2,128,1536]{2,1,0:T(8,128)(2,1)} %t_ref.1, bf16[8,48,768]{2,1,0:T(8,128)(2,1)} %reshape.231.w_ref, f32[2,4608]{1,0:T(2,128)} %fusion.90.mod_ref), custom_call_target="tpu_custom_call" | custom-call | flops 60000002048 | bytes 1048576 | tf_op jit(solution)/shard_map/gather_inputs/pallas_call | solution.py:942
  88.0 3.8 convert_reduce_fusion.1
  91.9 0.7 copy-done.14
  92.6 1.8 fusion.5
  94.6 6.2 %fusion.59 = f32[2,1024,768]{2,1,0:T(8,128)S(1)} fusion(bf16[1536,768,1]{1,0,2:T(8,128)(2,1)S(1)} %bitcast.205, bf16[2,1024,1536]{2,1,0:T(8,128)(2,1)S(1)} %copy-done.14, f32[2,1536]{1,0:T(2,128)S(1)} %get-tuple-element.122, f32[2,1536]{1,0:T(2,128)S(1)} %get-tuple-element.123, f32[2,1024]{1,0:T(2,128)S(1)} %add_rsqrt_fusion, ...), kind=kOutput, calls=%fused_computation.117 | convolution fusion | flops 4850712576 | bytes 14983168 | tf_op jit(solution)/shard_map/dot_general | solution.py:1280
  100.8 2.5 copy-done.25
  103.4 1.3 slice.324
  104.9 9.9 %multiply_convert_fusion.3 = (bf16[2,1024,384]{2,1,0:T(8,128)(2,1)S(1)}, bf16[2,1024,384]{2,1,0:T(8,128)(2,1)S(1)}) fusion(bf16[2,1024,384]{2,1,0:T(8,128)(2,1)} %slice.324, f32[384]{0:T(512)S(1)} %get-tuple-element.105, f32[384]{0:T(512)S(1)} %get-tuple-element.106, f32[384]{0:T(512)S(1)} %get-tuple-element.107, f32[384]{0:T(512)S(1)} %get-tuple-element.100, ...), kind=kLoop, calls=%fused_computation.66 | loop fusion | flops 25952256 | bytes 4733952 | tf_op jit(solution)/shard_map/convert_element_type | solution.py:1298
  114.9 0.6 fusion.34
  115.5 0.6 fusion.33
  116.2 30.1 %sum_4.1 = bf16[4,4,2,128,128]{4,3,2,1,0:T(8,128)(2,1)S(1)} custom-call(bf16[4,4,2,128,128]{4,3,2,1,0:T(8,128)(2,1)S(1)} %bitcast.174), custom_call_target="tpu_custom_call" | custom-call | flops 24999999488 | bytes 1048576 | tf_op jit(solution)/shard_map/sum_4/pallas_call | solution.py:743
  146.4 1.0 copy-done.6
  147.4 1.0 fusion.45
  148.5 0.5 copy-done.35
  149.9 2.3 pad_maximum_fusion.x_ref
  152.3 61.6 %scan_states.1 = (f32[2,2,1024,384]{3,2,1,0:T(8,128)}, bf16[2,2,16384,384]{3,2,1,0:T(8,128)(2,1)}, f32[2,2,1024,384]{3,2,1,0:T(8,128)}) custom-call(bf16[2,2,1024,128]{3,2,1,0:T(8,128)(2,1)S(1)} %bitcast.175, bf16[2,2,1024,384]{3,2,1,0:T(8,128)(2,1)S(1)} %pad_maximum_fusion.x_ref, bf16[2,128,384]{2,1,0:T(8,128)(2,1)S(1)} %pad.23.w_ref, ...), custom_call_target="tpu_custom_call" | custom-call | flops 64000000000 | bytes 83886080 | tf_op jit(solution)/shard_map/scan_states/pallas_call | solution.py:487
  213.9 4.1 all-gather.2.cloned.1.call-done
  217.9 13.6 %multiply_convert_fusion = (bf16[2,1024,384]{2,1,0:T(8,128)(2,1)S(1)}, f32[2,1024,384]{2,1,0:T(8,128)S(1)}, f32[2,1024,384]{2,1,0:T(8,128)}) fusion(f32[2,1024,768]{2,1,0:T(8,128)} %copy-done.25, bf16[2,1024,384]{2,1,0:T(8,128)(2,1)} %copy-done.16, f32[384]{0:T(512)S(1)} %get-tuple-element.99, bf16[2,1024,384]{2,1,0:T(8,128)(2,1)} %copy-done.15, ...), kind=kOutput, calls=%fused_computation.60 | convolution fusion | flops 2430861312 | bytes 27921408 | tf_op jit(solution)/shard_map/dot_general | solution.py:30
  231.6 3.4 multiply_convert_fusion.1
  235.1 5.6 %convolution_convert_fusion.1 = bf16[2048,1536]{1,0:T(8,128)(2,1)} fusion(bf16[2048,384]{1,0:T(8,128)(2,1)S(1)} %bitcast.212, bf16[384,1536]{1,0:T(8,128)(2,1)S(1)} %copy-done.83), kind=kOutput, calls=%fused_computation.12 | convolution fusion | flops 2419064832 | bytes 9043968 | tf_op jit(solution)/shard_map/dot_general | solution.py:1340
  240.8 5.1 fusion.31
  245.9 3.7 fusion.30
  249.6 1.1 copy-done.8
  250.8 1.3 copy-done.9
  252.0 110.3 %scan_adjoint.1 = (bf16[2,2,1024,384]{3,2,1,0:T(8,128)(2,1)}, f32[2,2,1024,384]{3,2,1,0:T(8,128)}, bf16[2,2,1024,128]{3,2,1,0:T(8,128)(2,1)S(1)}, f32[2,2,16,384...) custom-call(bf16[2,2,1024,128]{3,2,1,0:T(8,128)(2,1)S(1)} %bitcast.1, ...), custom_call_target="tpu_custom_call" | custom-call | flops 99999997952 | bytes 104857600 | tf_op jit(solution)/shard_map/scan_adjoint/pallas_call | solution.py:546
  362.4 1.0 copy-done.10
  363.3 1.0 copy-done.12
  364.3 1.2 copy-done.11
  365.6 26.8 %sum_5.1 = bf16[4,4,2,128,128]{4,3,2,1,0:T(8,128)(2,1)S(1)} custom-call(bf16[4,4,2,128,128]{4,3,2,1,0:T(8,128)(2,1)S(1)} %bitcast.185), custom_call_target="tpu_custom_call" | custom-call | flops 24999999488 | bytes 1048576 | tf_op jit(solution)/shard_map/sum_5/pallas_call | solution.py:743
  392.7 2.7 fusion.24
  395.4 5.8 %fusion.18 = (bf16[384]{0:T(512)(128)(2,1)S(1)}, bf16[384]{0:T(512)(128)(2,1)S(1)}, bf16[384]{0:T(512)(128)(2,1)S(1)}, bf16[384]{0:T(512)(128)(2,1)S(1)}, bf16[3...) fusion(bf16[2,1024,384]{2,1,0:T(8,128)(2,1)S(1)} %copy-done.22,, ...), kind=kOutput, calls=%fused_computation.40 | convolution fusion | flops 236712192 | bytes 11650560 | tf_op jit(solution)/shard_map/dot_general | solution.py:30
  401.2 2.9 add_convert_fusion
  404.4 0.8 copy-done.23
  405.3 1.1 copy-done.29
  406.4 7.5 %convert_reduce_fusion = (f32[2,1536]{1,0:T(2,128)S(1)}, f32[2,1536]{1,0:T(2,128)S(1)}, bf16[2048,1536]{1,0:T(8,128)(2,1)}) fusion(f32[2,1024]{1,0:T(2,128)S(1)} %copy-done.51, f32[2,1024]{1,0:T(2,128)S(1)} %copy-done.46, bf16[2,1024,1536]{2,1,0:T(8,128)(2,1)S(1)} %bitcast.189, bf16[2048,768]{1,0:T(8,128)(2,1)S(1)} %bitcast.197, ...), kind=kOutput, calls=%fused_computation.1 | convolution fusion | flops 4856997888 | bytes 18128896 | tf_op jit(solution)/shard_map/dot_general | solution.py:30
  413.9 2.7 copy.70
  416.6 2.6 copy.69
  419.7 0.6 add_rsqrt_fusion.1
  420.3 2.2 fusion.93
  422.5 0.5 fusion.51
  423.4 0.7 copy.78
  424.2 1.8 bitcast_convert_fusion
  426.2 1.1 concatenate.36
  427.3 2.2 convolution_convert_fusion.4
  429.5 1.6 convolution_convert_fusion.5
  431.7 6.9 %fusion.32 = bf16[1536,384]{1,0:T(8,128)(2,1)S(1)} fusion(bf16[2,1024,384]{2,1,0:T(8,128)(2,1)S(1)} %copy-done.24, bf16[2,1024,1536]{2,1,0:T(8,128)(2,1)} %get-tuple-element.46, f32[2,1536]{1,0:T(2,128)S(1)} %copy-done.72, f32[2,1536]{1,0:T(2,128)S(1)} %copy-done.43, f32[2,1024]{1,0:T(2,128)S(1)} %copy-done.51, f32[2,1024]{1,0:T(2,128)S(1)} %copy-done.46), kind=kOutput, calls=%fused_computation.73 | convolution fusion | flops 2435383296 | bytes 9084928 | tf_op jit(solution)/shard_map/dot_general | solution.py:26
  438.6 62.4 %weight_sums.1 = (f32[4,2,4608]{2,1,0:T(2,128)S(1)}, f32[192,6144]{1,0:T(8,128)S(1)}, f32[384,256]{1,0:T(8,128)S(1)}, f32[96,6144]{1,0:T(8,128)S(1)}, f32[16,614...) custom-call(f32[2,4608]{1,0:T(2,128)S(1)} %pad_maximum_fusion.4.m_re, ...), custom_call_target="tpu_custom_call" | custom-call | flops 60000002048 | bytes 1048576 | tf_op jit(solution)/shard_map/weight_sums/pallas_call | solution.py:1186
  501.0 2.2 copy-done.2
  503.2 1.4 copy-done.4
  504.7 0.7 reduce_sum.229
  505.4 1.8 fusion.47
  507.2 4.2 fusion.76
  511.4 3.2 fusion.46
  514.7 2.4 copy.108
  517.1 0.7 copy.109
  518.0 1.4 copy.110
  519.4 0.6 copy.111
  520.0 0.6 copy.112
  520.6 0.6 copy.113
  521.2 0.7 copy.114
  522.0 0.6 copy.115
  (255 shorter events, 4.8 us)
Async XLA Ops:
  7.2 3.4 copy-start.74
  7.2 3.5 copy-start.84
  7.2 3.5 copy-start.86
  7.2 210.7 %all-gather.2.cloned.1.call-start = ((), (), s32[]{:S(2)}) async-start(), calls=%async_computation.2 | async-start | bytes 7077888 | tf_op jit(solution)/shard_map/all_gather | solution.py:1314
  10.7 83.7 %copy-start.80 = (f32[2]{0:T(128)}, f32[2]{0:T(128)S(1)}, u32[]{:S(2)}) copy-start(f32[2]{0:T(128)S(1)} %dynamic-slice_convert_fusion.2) | copy-start | bytes 28
  11.0 77.1 %copy-start.82 = (bf16[8,1536]{1,0:T(8,128)(2,1)}, bf16[8,1536]{1,0:T(8,128)(2,1)S(1)}, u32[]{:S(2)}) copy-start(bf16[8,1536]{1,0:T(8,128)(2,1)S(1)} %multiply_convert_fusion.5) | copy-start | bytes 73732
  88.0 4.6 copy-start.14
  94.4 6.3 %copy-start.49 = (f32[2,1024]{1,0:T(2,128)}, f32[2,1024]{1,0:T(2,128)S(1)}, u32[]{:S(2)}) copy-start(f32[2,1024]{1,0:T(2,128)S(1)} %add_rsqrt_fusion) | copy-start | bytes 24580
  94.6 6.2 %copy-start.41 = (f32[2,1536]{1,0:T(2,128)}, f32[2,1536]{1,0:T(2,128)S(1)}, u32[]{:S(2)}) copy-start(f32[2,1536]{1,0:T(2,128)S(1)} %get-tuple-element.123) | copy-start | bytes 36868
  94.6 6.2 %copy-start.70 = (f32[2,1536]{1,0:T(2,128)}, f32[2,1536]{1,0:T(2,128)S(1)}, u32[]{:S(2)}) copy-start(f32[2,1536]{1,0:T(2,128)S(1)} %get-tuple-element.122) | copy-start | bytes 36868
  94.6 52.8 %copy-start.39 = (f32[2,1536]{1,0:T(2,128)}, f32[2,1536]{1,0:T(2,128)S(1)}, u32[]{:S(2)}) copy-start(f32[2,1536]{1,0:T(2,128)S(1)} %get-tuple-element.121) | copy-start | bytes 36868
  104.7 10.2 %copy-start.37 = (bf16[384,256]{1,0:T(8,128)(2,1)S(1)}, bf16[384,256]{1,0:T(8,128)(2,1)}, u32[]{:S(2)}) copy-start(bf16[384,256]{1,0:T(8,128)(2,1)} %param.23) | copy-start | bytes 589828
  104.8 10.6 %copy-start.54 = (f32[384]{0:T(512)}, f32[384]{0:T(512)S(1)}, u32[]{:S(2)}) copy-start(f32[384]{0:T(512)S(1)} %get-tuple-element.100) | copy-start | bytes 4612
  104.9 10.6 %copy-start.56 = (f32[384]{0:T(512)}, f32[384]{0:T(512)S(1)}, u32[]{:S(2)}) copy-start(f32[384]{0:T(512)S(1)} %get-tuple-element.101) | copy-start | bytes 4612
  104.9 10.6 %copy-start.58 = (f32[384]{0:T(512)}, f32[384]{0:T(512)S(1)}, u32[]{:S(2)}) copy-start(f32[384]{0:T(512)S(1)} %get-tuple-element.102) | copy-start | bytes 4612
  104.9 10.6 %copy-start.60 = (f32[384]{0:T(512)}, f32[384]{0:T(512)S(1)}, u32[]{:S(2)}) copy-start(f32[384]{0:T(512)S(1)} %get-tuple-element.103) | copy-start | bytes 4612
  104.9 10.6 %copy-start.62 = (f32[384]{0:T(512)}, f32[384]{0:T(512)S(1)}, u32[]{:S(2)}) copy-start(f32[384]{0:T(512)S(1)} %get-tuple-element.104) | copy-start | bytes 4612
  104.9 10.6 %copy-start.64 = (f32[384]{0:T(512)}, f32[384]{0:T(512)S(1)}, u32[]{:S(2)}) copy-start(f32[384]{0:T(512)S(1)} %get-tuple-element.105) | copy-start | bytes 4612
  104.9 10.6 %copy-start.66 = (f32[384]{0:T(512)}, f32[384]{0:T(512)S(1)}, u32[]{:S(2)}) copy-start(f32[384]{0:T(512)S(1)} %get-tuple-element.106) | copy-start | bytes 4612
  104.9 10.6 %copy-start.68 = (f32[384]{0:T(512)}, f32[384]{0:T(512)S(1)}, u32[]{:S(2)}) copy-start(f32[384]{0:T(512)S(1)} %get-tuple-element.107) | copy-start | bytes 4612
  104.9 10.6 %copy-start.76 = (f32[384]{0:T(512)}, f32[384]{0:T(512)S(1)}, u32[]{:S(2)}) copy-start(f32[384]{0:T(512)S(1)} %get-tuple-element.128) | copy-start | bytes 4612
  104.9 10.6 %copy-start.78 = (f32[384]{0:T(512)}, f32[384]{0:T(512)S(1)}, u32[]{:S(2)}) copy-start(f32[384]{0:T(512)S(1)} %get-tuple-element.129) | copy-start | bytes 4612
  114.8 31.5 %copy-start.15 = (bf16[2,1024,384]{2,1,0:T(8,128)(2,1)}, bf16[2,1024,384]{2,1,0:T(8,128)(2,1)S(1)}, u32[]{:S(2)}) copy-start(bf16[2,1024,384]{2,1,0:T(8,128)(2,1)S(1)} %get-tuple-element.115) | copy-start | bytes 4718596
  114.8 31.5 %copy-start.16 = (bf16[2,1024,384]{2,1,0:T(8,128)(2,1)}, bf16[2,1024,384]{2,1,0:T(8,128)(2,1)S(1)}, u32[]{:S(2)}) copy-start(bf16[2,1024,384]{2,1,0:T(8,128)(2,1)S(1)} %get-tuple-element.116) | copy-start | bytes 4718596
  116.2 31.2 %copy-start.19 = (bf16[2,128,1536]{2,1,0:T(8,128)(2,1)S(1)}, bf16[2,128,1536]{2,1,0:T(8,128)(2,1)}, u32[]{:S(2)}) copy-start(bf16[2,128,1536]{2,1,0:T(8,128)(2,1)} %param.20) | copy-start | bytes 2359300
  148.5 215.9 %reduce-scatter.3.cloned.1.call-start = ((), (), s32[]{:S(2)}) async-start(), calls=%async_computation.3 | async-start | bytes 7077888 | tf_op jit(solution)/shard_map/reduce_scatter | solution.py:1349
  152.2 61.7 %copy-start.3 = (bf16[2,2,1024,384]{3,2,1,0:T(8,128)(2,1)}, bf16[2,2,1024,384]{3,2,1,0:T(8,128)(2,1)S(1)}, u32[]{:S(2)}) copy-start(bf16[2,2,1024,384]{3,2,1,0:T(8,128)(2,1)S(1)} %pad_maximum_fusion.x_ref) | copy-start | bytes 9437188
  231.6 9.2 %copy-start.33 = (bf16[2,1024,384]{2,1,0:T(8,128)(2,1)}, bf16[2,1024,384]{2,1,0:T(8,128)(2,1)S(1)}, u32[]{:S(2)}) copy-start(bf16[2,1024,384]{2,1,0:T(8,128)(2,1)S(1)} %get-tuple-element.110) | copy-start | bytes 4718596
  231.6 3.5 copy-start.83
  231.6 9.2 %slice-start.2 = ((s8[6291456]{0:T(1024)(128)(4,1)}), s8[4194304]{0:T(1024)(128)(4,1)S(1)}, s32[]{:S(2)}) async-start(s8[6291456]{0:T(1024)(128)(4,1)} %bitcast.186), calls=%async_computation.7 | async-start | bytes 8388608
  235.0 5.7 %slice-start.3 = ((s8[6291456]{0:T(1024)(128)(4,1)}), s8[2097152]{0:T(1024)(128)(4,1)S(1)}, s32[]{:S(2)}) async-start(s8[6291456]{0:T(1024)(128)(4,1)} %bitcast.186), calls=%async_computation.8 | async-start | bytes 4194304
  235.0 5.7 %copy-start.42 = (f32[2,1536]{1,0:T(2,128)S(1)}, f32[2,1536]{1,0:T(2,128)}, u32[]{:S(2)}) copy-start(f32[2,1536]{1,0:T(2,128)} %copy-done.41) | copy-start | bytes 36868
  235.0 5.7 %copy-start.45 = (f32[2,1024]{1,0:T(2,128)S(1)}, f32[2,1024]{1,0:T(2,128)}, u32[]{:S(2)}) copy-start(f32[2,1024]{1,0:T(2,128)} %copy-done.44) | copy-start | bytes 24580
  235.1 5.7 %copy-start.50 = (f32[2,1024]{1,0:T(2,128)S(1)}, f32[2,1024]{1,0:T(2,128)}, u32[]{:S(2)}) copy-start(f32[2,1024]{1,0:T(2,128)} %copy-done.49) | copy-start | bytes 24580
  235.1 5.7 %copy-start.71 = (f32[2,1536]{1,0:T(2,128)S(1)}, f32[2,1536]{1,0:T(2,128)}, u32[]{:S(2)}) copy-start(f32[2,1536]{1,0:T(2,128)} %copy-done.70) | copy-start | bytes 36868
  235.1 10.8 %slice-start.6 = ((s8[6291456]{0:T(1024)(128)(4,1)}), s8[4194304]{0:T(1024)(128)(4,1)S(1)}, s32[]{:S(2)}) async-start(s8[6291456]{0:T(1024)(128)(4,1)} %bitcast.228), calls=%async_computation.11 | async-start | bytes 8388608
  240.8 5.1 slice-start.7
  249.6 255.1 %reduce-scatter.5.cloned.1.call-start = ((), (), s32[]{:S(2)}) async-start(), calls=%async_computation.4 | async-start | bytes 7077888 | tf_op jit(solution)/shard_map/reduce_scatter | solution.py:1396
  365.5 27.0 %copy-start.22 = (bf16[2,1024,384]{2,1,0:T(8,128)(2,1)S(1)}, bf16[2,1024,384]{2,1,0:T(8,128)(2,1)}, u32[]{:S(2)}) copy-start(bf16[2,1024,384]{2,1,0:T(8,128)(2,1)} %slice.324) | copy-start | bytes 4718596
  365.6 27.0 %copy-start.38 = (bf16[384,256]{1,0:T(8,128)(2,1)S(1)}, bf16[384,256]{1,0:T(8,128)(2,1)}, u32[]{:S(2)}) copy-start(bf16[384,256]{1,0:T(8,128)(2,1)} %param.23) | copy-start | bytes 589828
  365.6 27.0 %copy-start.55 = (f32[384]{0:T(512)S(1)}, f32[384]{0:T(512)}, u32[]{:S(2)}) copy-start(f32[384]{0:T(512)} %copy-done.54) | copy-start | bytes 4612
  365.6 27.0 %copy-start.65 = (f32[384]{0:T(512)S(1)}, f32[384]{0:T(512)}, u32[]{:S(2)}) copy-start(f32[384]{0:T(512)} %copy-done.64) | copy-start | bytes 4612
  365.6 27.0 %copy-start.67 = (f32[384]{0:T(512)S(1)}, f32[384]{0:T(512)}, u32[]{:S(2)}) copy-start(f32[384]{0:T(512)} %copy-done.66) | copy-start | bytes 4612
  365.6 27.0 %copy-start.69 = (f32[384]{0:T(512)S(1)}, f32[384]{0:T(512)}, u32[]{:S(2)}) copy-start(f32[384]{0:T(512)} %copy-done.68) | copy-start | bytes 4612
  365.6 27.0 %copy-start.79 = (f32[384]{0:T(512)S(1)}, f32[384]{0:T(512)}, u32[]{:S(2)}) copy-start(f32[384]{0:T(512)} %copy-done.78) | copy-start | bytes 4612
  365.6 27.0 %copy-start.87 = (f32[2,2,1024,384]{3,2,1,0:T(8,128)S(1)}, f32[2,2,1024,384]{3,2,1,0:T(8,128)}, u32[]{:S(2)}) copy-start(f32[2,2,1024,384]{3,2,1,0:T(8,128)} %get-tuple-element.59) | copy-start | bytes 18874372
  392.7 12.6 %slice-start.4 = ((s8[6291456]{0:T(1024)(128)(4,1)}), s8[4194304]{0:T(1024)(128)(4,1)S(1)}, s32[]{:S(2)}) async-start(s8[6291456]{0:T(1024)(128)(4,1)} %bitcast.188), calls=%async_computation.9 | async-start | bytes 8388608
  395.4 9.8 %slice-start.5 = ((s8[6291456]{0:T(1024)(128)(4,1)}), s8[2097152]{0:T(1024)(128)(4,1)S(1)}, s32[]{:S(2)}) async-start(s8[6291456]{0:T(1024)(128)(4,1)} %bitcast.188), calls=%async_computation.10 | async-start | bytes 4194304
  413.9 5.2 copy-start.17
  424.2 5.3 %copy-start.21 = (bf16[384,2048]{1,0:T(8,128)(2,1)S(1)}, bf16[384,2048]{1,0:T(8,128)(2,1)}, u32[]{:S(2)}) copy-start(bf16[384,2048]{1,0:T(8,128)(2,1)} %copy.69) | copy-start | bytes 4718596
  426.0 5.2 copy-start.20
  426.0 5.2 copy-start.26
  426.0 5.2 copy-start.81
  427.3 4.3 copy-start.24
  427.3 4.3 copy-start.43
  427.3 4.3 copy-start.72
  431.7 6.9 %copy-start.13 = (bf16[4,8,48,384]{3,2,1,0:T(8,128)(2,1)S(1)}, bf16[4,8,48,384]{3,2,1,0:T(8,128)(2,1)}, u32[]{:S(2)}) copy-start(bf16[4,8,48,384]{3,2,1,0:T(8,128)(2,1)} %copy-done.12) | copy-start | bytes 3538948
  438.6 66.8 %copy-start.18 = (bf16[2,128,1536]{2,1,0:T(8,128)(2,1)S(1)}, bf16[2,128,1536]{2,1,0:T(8,128)(2,1)}, u32[]{:S(2)}) copy-start(bf16[2,128,1536]{2,1,0:T(8,128)(2,1)} %t_ref.1) | copy-start | bytes 2359300
  438.6 66.8 %copy-start.75 = (f32[2,128]{1,0:T(2,128)S(1)}, f32[2,128]{1,0:T(2,128)}, u32[]{:S(2)}) copy-start(f32[2,128]{1,0:T(2,128)} %add_rsqrt_fusion.1) | copy-start | bytes 3076
  504.6 6.8 %copy-start.40 = (f32[2,1536]{1,0:T(2,128)S(1)}, f32[2,1536]{1,0:T(2,128)}, u32[]{:S(2)}) copy-start(f32[2,1536]{1,0:T(2,128)} %copy-done.39) | copy-start | bytes 36868
  505.4 6.0 %copy-start.27 = (bf16[2,128,1536]{2,1,0:T(8,128)(2,1)S(1)}, bf16[2,128,1536]{2,1,0:T(8,128)(2,1)}, u32[]{:S(2)}) copy-start(bf16[2,128,1536]{2,1,0:T(8,128)(2,1)} %reduce-scatter.5.cloned.1.call-done) | copy-start | bytes 2359300
  505.4 9.2 %slice-start = ((s8[4718592]{0:T(1024)(128)(4,1)}), s8[4194304]{0:T(1024)(128)(4,1)S(1)}, s32[]{:S(2)}) async-start(s8[4718592]{0:T(1024)(128)(4,1)} %bitcast.172), calls=%async_computation.5 | async-start | bytes 8388608
  507.2 7.4 %slice-start.1 = ((s8[4718592]{0:T(1024)(128)(4,1)}), s8[524288]{0:T(1024)(128)(4,1)S(1)}, s32[]{:S(2)}) async-start(s8[4718592]{0:T(1024)(128)(4,1)} %bitcast.172), calls=%async_computation.6 | async-start | bytes 1048576
  514.6 8.0 %copy-start.1 = (bf16[192,6144]{1,0:T(8,128)(2,1)S(1)}, bf16[192,6144]{1,0:T(8,128)(2,1)}, u32[]{:S(2)}) copy-start(bf16[192,6144]{1,0:T(8,128)(2,1)} %param.21) | copy-start | bytes 7077892
  (35 other events, 72.8 us)
Sparse Core Ops, SparseCore 0:
  148.6 69.3 all-gather.1
  249.7 75.1 reduce-scatter.2
  414.0 88.8 reduce-scatter.4

commit v4 on v3

--- a/solution.py
+++ b/solution.py
@@ -98,11 +98,12 @@
     bias_ref,
     r_ref,
     copies_ref,
+    skip_ref,
     y_ref,
     h_ref,
     dt_ref,
+    bc_ref,
     state,
-    bc,
     even,
     odd,
 ):
@@ -119,7 +120,7 @@
         dt_ref[0, s] = softplus(
             jnp.dot(selection, w_ref[0], preferred_element_type=f32) + bias_ref[0]
         )
-        bc[s] = place_coefficients(selection, copies_ref[...])
+        bc_ref[0, s] = place_coefficients(selection, copies_ref[...])
 
     def one_direction(reverse):
         mix = spread_matrix()
@@ -130,7 +131,7 @@
         def spread(i, into):
             start = pl.multiple_of(place(i) * chunk, chunk)
             for s in range(slots):
-                both = bc[s, pl.ds(start, chunk), :]
+                both = bc_ref[0, s, pl.ds(start, chunk), :]
                 span = both.shape[1] // 2
                 into[s] = dot_rows(jnp.concatenate([both[:, :span], both[:, span:]], axis=0), mix)
 
@@ -141,7 +142,8 @@
                 h = state[s]
                 rate = r_ref[0]
                 dt = dt_ref[0, s, pl.ds(start, chunk), :]
-                u = dt * x_ref[0, s, pl.ds(start, chunk), :].astype(f32)
+                x = x_ref[0, s, pl.ds(start, chunk), :].astype(f32)
+                u = dt * x
                 kept, sums = [None] * chunk, [None] * chunk
                 for t in order:
                     rows = slice(t * states, (t + 1) * states)
@@ -155,7 +157,8 @@
                 h_ref[0, s, pl.ds(pl.multiple_of(start * states, size), size), :] = jnp.concatenate(
                     kept, axis=0
                 )
-                y_ref[0, s, pl.ds(start, chunk), :] = fold_sublanes(sums)
+                y = fold_sublanes(sums) + skip_ref[0] * x
+                y_ref[0, s, pl.ds(start, chunk), :] = y.astype(bf16)
                 state[s] = h
 
         chunk_sweep(count, body, spread, even, odd)
@@ -308,7 +311,7 @@
 
 def adjoint_kernel(
     count,
-    sel_ref,
+    bc_ref,
     x_ref,
     w_ref,
     r_ref,
@@ -328,7 +331,6 @@
     b_out,
     q_out,
     pending,
-    bc,
     coefs,
     even,
     odd,
@@ -347,9 +349,6 @@
         decay_ref[...] = jnp.zeros_like(decay_ref)
         sums_ref[...] = jnp.zeros_like(sums_ref)
 
-    for s in range(slots):
-        bc[s] = place_coefficients(sel_ref[0, s], copies_ref[...])
-
     def one_direction(reverse):
         mix = spread_matrix()
         picks = (
@@ -363,7 +362,7 @@
         def spread(i, into):
             start = pl.multiple_of(place(i) * chunk, chunk)
             for s in range(slots):
-                both = bc[s, pl.ds(start, chunk), :]
+                both = bc_ref[0, s, pl.ds(start, chunk), :]
                 span = both.shape[1] // 2
                 into[s] = dot_rows(jnp.concatenate([both[:, :span], both[:, span:]], axis=0), mix)
 
@@ -426,7 +425,8 @@
                 slope = jnp.where(dt < 0.03, few, 1.0 - jnp.exp(-dt))
                 grad_pre = (fold_sublanes(rate_sums) * ln2 + weighted * x) * slope
                 low_ref[0, s, pl.ds(start, chunk), :] = grad_pre.astype(bf16)
-                input_ref[0, s, pl.ds(start, chunk), :] = weighted * dt + skip_ref[0] * g
+                direct = weighted * dt + skip_ref[0] * g
+                input_ref[0, s, pl.ds(start, chunk), :] = direct.astype(bf16)
                 gx = g * x
                 sums_ref[0] += jnp.concatenate(
                     [grad_pre[:8] + grad_pre[8:], gx[:8] + gx[8:]], axis=0
@@ -466,10 +466,10 @@
 
 
 def block_of(length):
-    return math.gcd(length, 128)
-
-
-def scan_states(selection, x, weight, bias, rate, copies):
+    return math.gcd(length, 256)
+
+
+def scan_states(selection, x, weight, bias, rate, copies, skip):
     two, slots, length, width = x.shape
     select = selection.shape[3]
     states = rate.shape[1]
@@ -494,20 +494,22 @@
             pl.BlockSpec((1, 1, width), by_direction),
             pl.BlockSpec((1, states, width), by_direction),
             pl.BlockSpec((select, spread), lambda d, i: (0, 0)),
+            pl.BlockSpec((1, 1, width), by_direction),
         ],
         out_specs=[
             pl.BlockSpec((1, slots, block, width), where),
             pl.BlockSpec((1, slots, block * states, width), where),
             pl.BlockSpec((1, slots, block, width), where),
+            pl.BlockSpec((1, slots, block, spread), where),
         ],
         out_shape=[
-            jax.ShapeDtypeStruct((two, slots, length, width), f32),
+            jax.ShapeDtypeStruct((two, slots, length, width), bf16),
             jax.ShapeDtypeStruct((two, slots, length * states, width), bf16),
             jax.ShapeDtypeStruct((two, slots, length, width), f32),
+            jax.ShapeDtypeStruct((two, slots, length, spread), bf16),
         ],
         scratch_shapes=[
             pltpu.VMEM((slots, states, width), f32),
-            pltpu.VMEM((slots, block, spread), bf16),
             pltpu.VMEM((slots, chunk * states, 2 * lanes), f32),
             pltpu.VMEM((slots, chunk * states, 2 * lanes), f32),
         ],
@@ -516,12 +518,12 @@
             flops=64 * 10**9, bytes_accessed=80 * 2**20, transcendentals=hidden_size
         ),
         name="scan_states",
-    )(selection, x, weight, bias, rate, copies)
-
-
-def scan_adjoint(selection, x, weight, rate, copies, skip, dt, g, h, b, q):
+    )(selection, x, weight, bias, rate, copies, skip)
+
+
+def scan_adjoint(bc, x, weight, rate, copies, skip, dt, g, h, b, q):
     two, slots, length, width = dt.shape
-    select = selection.shape[3]
+    select = weight.shape[1]
     states = rate.shape[1]
     hidden_size = two * slots * length * states * width
     block = block_of(length)
@@ -547,7 +549,7 @@
         functools.partial(adjoint_kernel, block // chunk),
         grid=(two, blocks),
         in_specs=[
-            pl.BlockSpec((1, slots, block, select), where),
+            pl.BlockSpec((1, slots, block, spread), where),
             pl.BlockSpec((1, slots, block, width), where),
             pl.BlockSpec((1, select, width), by_direction),
             pl.BlockSpec((1, states, width), by_direction),
@@ -571,7 +573,7 @@
         ],
         out_shape=[
             jax.ShapeDtypeStruct((two, slots, length, width), bf16),
-            jax.ShapeDtypeStruct((two, slots, length, width), f32),
+            jax.ShapeDtypeStruct((two, slots, length, width), bf16),
             jax.ShapeDtypeStruct((two, slots, length, select), bf16),
             jax.ShapeDtypeStruct((two, slots, states, width), f32),
             jax.ShapeDtypeStruct((two, 16, width), f32),
@@ -580,7 +582,6 @@
         ],
         scratch_shapes=[
             pltpu.VMEM((slots, states, width), f32),
-            pltpu.VMEM((slots, block, spread), bf16),
             pltpu.VMEM((slots, block // chunk * 8, chunk * states), f32),
             pltpu.VMEM((slots, chunk * states, 2 * lanes), f32),
             pltpu.VMEM((slots, chunk * states, 2 * lanes), f32),
@@ -599,7 +600,7 @@
             flops=100 * 10**9, bytes_accessed=100 * 2**20, transcendentals=hidden_size
         ),
         name="scan_adjoint",
-    )(selection, x, weight, rate, copies, skip, dt, g, h, h, b, q)
+    )(bc, x, weight, rate, copies, skip, dt, g, h, h, b, q)
 
 
 def coefficient_copies(width, rank, states):
@@ -1277,11 +1278,14 @@
     centered = source - jnp.mean(source, axis=-1, keepdims=True)
     spread = lax.rsqrt(jnp.mean(centered * centered, axis=-1, keepdims=True) + epsilon)
     mixed_in = (centered * spread * (1.0 + scale) + shift).astype(bf16).reshape(rows, model)
-    projected = jnp.dot(mixed_in, own_in, preferred_element_type=f32).reshape(
-        slots, length, 2 * mine
-    )
-    x_half = projected[..., :mine].astype(bf16)
-    gate_half = projected[..., mine:]
+    mixed_in = lax.optimization_barrier(mixed_in)
+    projected = (
+        jnp.dot(mixed_in, own_in, preferred_element_type=f32)
+        .astype(bf16)
+        .reshape(slots, length, 2 * mine)
+    )
+    x_half = projected[..., :mine]
+    gate_half = projected[..., mine:].astype(f32)
 
     tap_weight = own_columns(filter_weight).astype(f32)
     tap_bias = own_columns(filter_bias).astype(f32)
@@ -1323,13 +1327,11 @@
     )
     wide_bias = widen(step_bias[:, None, :], padded_width)
     wide_skip = widen(skip[:, None, :], padded_width)
-    scanned, hidden, step = scan_states(
-        selection, wide_active, wide_weight, wide_bias, wide_rate, copies
+    scanned, hidden, step, bc = scan_states(
+        selection, wide_active, wide_weight, wide_bias, wide_rate, copies, wide_skip
     )
     scanned = scanned[..., :mine]
-    scanned_sum = scanned[0] + scanned[1]
-    for d in range(2):
-        scanned_sum = scanned_sum + skip[d] * activated[d].astype(f32)
+    scanned_sum = scanned[0].astype(f32) + scanned[1].astype(f32)
     silu_gate = jax.nn.silu(gate_half)
     mixed_out = (scanned_sum * silu_gate).astype(bf16).reshape(rows, mine)
     grad_mixed = dot_cols(grad_branch, out_weight).reshape(slots, length, mine)
@@ -1348,7 +1350,7 @@
     )
     branch_part = lax.psum_scatter(branch_part, "seq", scatter_dimension=1, tiled=True)
     grad_low, grad_input, grad_parts, grad_rate, grad_sums, grad_out, gate_in = scan_adjoint(
-        selection,
+        bc,
         wide_active,
         wide_weight,
         wide_rate,
@@ -1368,14 +1370,19 @@
     grad_selection = summed_everywhere(
         grad_parts.reshape(2 * slots, length, select), 5
     ).reshape(2, rows, select)
-    grad_delta = [
-        dot_rows(delta_rank[d], grad_low[d, ..., :mine].reshape(rows, mine)) for d in range(2)
-    ]
+    grad_delta = jnp.einsum(
+        "drk,dre->kde",
+        delta_rank,
+        grad_low[..., :mine].reshape(2, rows, mine),
+        preferred_element_type=f32,
+    )
     grad_x = jnp.zeros((slots, length, mine), f32)
     grad_select, grad_taps, grad_tap_bias = [], [], []
     for d in range(2):
         block = select_weight[:, d * select : (d + 1) * select]
-        grad_select.append(dot_rows(activated[d].reshape(rows, mine), grad_selection[d]))
+        grad_select.append(
+            dot_rows(grad_selection[d], activated[d].reshape(rows, mine)).T
+        )
         grad_active = (
             grad_input[d, ..., :mine]
             + dot_cols(grad_selection[d], block).reshape(slots, length, mine)
@@ -1408,7 +1415,7 @@
     output = (tokens.astype(f32) + valid * gate * branch).astype(bf16)
     small = jnp.concatenate(
         [
-            jnp.stack(grad_delta, 1),
+            grad_delta,
             jnp.swapaxes(grad_decay, 0, 1),
             jnp.stack(grad_taps, 1),
             jnp.stack(grad_tap_bias)[None],

time: 540 us -> 535 us (level)
  the two profiles are of different devices: /device:TPU:0 before, /device:TPU:9 now
where the time goes in v4:
time: 535 us; the launch traced here: 525 us
  Pallas kernels  364 us (68%)
  matrix products  69.1 us (13%)
  local copies, waits for them, and re-layouts  37.4 us (7%)
  other arithmetic  34.3 us (6%)
  between operations  15.6 us (3%)
    pallas_call x1, Pallas kernels, scan_adjoint(): pl.pallas_call(functools.partial(adjoint_kernel, block // chunk), grid=(t...  107 us
    pallas_call x1, Pallas kernels, gather_inputs(): pl.pallas_call(functools.partial(head_kernel, line), in_specs=[anywhere,...  70.6 us
    pallas_call x2, Pallas kernels, summed_everywhere(): pl.pallas_call(functools.partial(total_kernel, line), in_specs=[vmem], ou...  66.3 us
    pallas_call x1, Pallas kernels, scan_states(): pl.pallas_call(functools.partial(states_kernel, block // chunk), grid=(tw...  61.4 us
    pallas_call x1, Pallas kernels, weight_sums(): pl.pallas_call(functools.partial(tail_kernel, cuts if direct else None),...  59.1 us
    dot_general x4, matrix products, dot_cols(): lax.dot_general(a, b, (((1,), (1,)), ((), ())), preferred_element_type=f32)  27 us
    unnamed x189, local copies, waits for them, and re-layouts  27 us
    dot_general x5, matrix products, dot_rows(): lax.dot_general(a, b, (((0,), (0,)), ((), ())), preferred_element_type=f32)  21 us
  transfers between devices with their start and end apart: 3, of which 1 were waited for; matrix products, arithmetic and copies ran while one was open for 5% of the time, Pallas kernels for 43%

profile of v4, /device:TPU:9, one launch (start us, length us, event | category | flops | bytes accessed | tf_op | source)
XLA Modules:
  0.0 524.8 jit_solution(11594855370422794299)
XLA Ops:
  7.3 1.6 copy-done
  9.0 0.5 copy.50
  9.4 1.2 reshape.242.w_ref
  10.9 2.5 fusion.84.mod_ref
  13.4 70.6 %gather_inputs.1 = (bf16[2,1024,1536]{2,1,0:T(8,128)(2,1)}, bf16[8,4,48,768]{3,2,1,0:T(8,128)(2,1)}, f32[2,4608]{1,0:T(2,128)}) custom-call(bf16[2,128,1536]{2,1,0:T(8,128)(2,1)} %t_ref.1, bf16[8,48,768]{2,1,0:T(8,128)(2,1)} %reshape.242.w_ref, f32[2,4608]{1,0:T(2,128)} %fusion.84.mod_ref), custom_call_target="tpu_custom_call" | custom-call | flops 60000002048 | bytes 1048576 | tf_op jit(solution)/shard_map/gather_inputs/pallas_call | solution.py:943
  84.0 3.8 convert_reduce_fusion.1
  87.9 0.7 copy-done.13
  88.6 1.8 fusion.5
  90.7 0.5 copy-done.75
  91.1 2.7 fusion.4
  93.9 5.2 convolution_convert_fusion.2
  99.2 1.6 copy-done.37
  100.8 1.3 slice.185
  102.4 10.1 %multiply_convert_fusion.1 = (bf16[2,1024,384]{2,1,0:T(8,128)(2,1)S(1)}, bf16[2,1024,384]{2,1,0:T(8,128)(2,1)S(1)}) fusion(bf16[2,1024,384]{2,1,0:T(8,128)(2,1)} %slice.185, f32[384]{0:T(512)S(1)} %get-tuple-element.106, f32[384]{0:T(512)S(1)} %get-tuple-element.107, f32[384]{0:T(512)S(1)} %get-tuple-element.108, f32[384]{0:T(512)S(1)} %get-tuple-element.101, ...), kind=kLoop, calls=%fused_computation.74 | loop fusion | flops 25952256 | bytes 4733952 | tf_op jit(solution)/shard_map/convert_element_type | solution.py:1302
  112.5 0.6 fusion.37
  113.2 0.4 copy-done.14
  113.6 0.6 fusion.38
  114.3 36.3 %sum_4.1 = bf16[4,4,2,128,128]{4,3,2,1,0:T(8,128)(2,1)S(1)} custom-call(bf16[4,4,2,128,128]{4,3,2,1,0:T(8,128)(2,1)S(1)} %bitcast.160), custom_call_target="tpu_custom_call" | custom-call | flops 24999999488 | bytes 1048576 | tf_op jit(solution)/shard_map/sum_4/pallas_call | solution.py:744
  150.7 1.0 fusion.49
  151.9 0.8 copy-done.36
  153.2 1.1 copy.68
  154.4 3.9 pad_maximum_fusion.x_ref
  158.3 61.4 %scan_states.1 = (bf16[2,2,1024,384]{3,2,1,0:T(8,128)(2,1)S(1)}, bf16[2,2,16384,384]{3,2,1,0:T(8,128)(2,1)}, f32[2,2,1024,384]{3,2,1,0:T(8,128)}, bf16[2,2,1024,512]{3,2,1,0:T(8,128)(2,1)}) custom-call(bf16[2,2,1024,128]{3,2,1,0:T(8,128)(2,1)S(1)} %bitcast.158, bf16[2,2,1024,384]{3,2,1,0:T(8,128)(2,1)} %pad_maximum_fusion.x_ref, ...), custom_call_target="tpu_custom_call" | custom-call | flops 64000000000 | bytes 83886080 | tf_op jit(solution)/shard_map/scan_states/pallas_call | solution.py:487
  219.7 1.7 copy-done.10
  221.4 10.6 %fusion.55 = (f32[2,1024,384]{2,1,0:T(8,128)}, bf16[2,1024,384]{2,1,0:T(8,128)(2,1)S(1)}, bf16[2,1024,384]{2,1,0:T(8,128)(2,1)S(1)}) fusion(bf16[2,1024,768]{2,1,0:T(8,128)(2,1)} %bitcast.198, bf16[2,2,1024,384]{3,2,1,0:T(8,128)(2,1)} %copy-done.10, bf16[2,1024,1536]{2,1,0:T(8,128)(2,1)} %all-gather.2.cloned.1.call-done, bf16[384,1536]{1,0:T(8,128)(2,1)S(1)} %copy-done.79), kind=kOutput, calls=%fused_computation.115 | convolution fusion | flops 2430074880 | bytes 18481152 | tf_op jit(solution)/shard_map/dot_general | solution.py:30
  232.0 7.8 %convolution_convert_fusion.4 = bf16[1536,384]{1,0:T(8,128)(2,1)} fusion(bf16[2048,1536]{1,0:T(8,128)(2,1)} %bitcast.182, bf16[2048,384]{1,0:T(8,128)(2,1)S(1)} %bitcast.195), kind=kOutput, calls=%fused_computation.79 | convolution fusion | flops 2416508928 | bytes 9043968 | tf_op jit(solution)/shard_map/dot_general | solution.py:26
  239.9 5.2 convolution_convert_fusion.1
  245.1 2.6 fusion.36
  247.8 106.7 %scan_adjoint.1 = (bf16[2,2,1024,384]{3,2,1,0:T(8,128)(2,1)}, bf16[2,2,1024,384]{3,2,1,0:T(8,128)(2,1)}, bf16[2,2,1024,128]{3,2,1,0:T(8,128)(2,1)S(1)}, f32[2,2,...) custom-call(bf16[2,2,1024,512]{3,2,1,0:T(8,128)(2,1)} %get-tuple-ele, ...), custom_call_target="tpu_custom_call" | custom-call | flops 99999997952 | bytes 104857600 | tf_op jit(solution)/shard_map/scan_adjoint/pallas_call | solution.py:548
  354.6 1.0 copy-done.8
  355.5 1.0 copy-done.11
  356.6 1.2 copy-done.9
  357.8 30.0 %sum_5.1 = bf16[4,4,2,128,128]{4,3,2,1,0:T(8,128)(2,1)S(1)} custom-call(bf16[4,4,2,128,128]{4,3,2,1,0:T(8,128)(2,1)S(1)} %bitcast.167), custom_call_target="tpu_custom_call" | custom-call | flops 24999999488 | bytes 1048576 | tf_op jit(solution)/shard_map/sum_5/pallas_call | solution.py:744
  388.1 2.8 fusion.30
  391.0 6.1 %fusion.86 = (bf16[384]{0:T(512)(128)(2,1)S(1)}, bf16[384]{0:T(512)(128)(2,1)S(1)}, bf16[384]{0:T(512)(128)(2,1)S(1)}, bf16[384]{0:T(512)(128)(2,1)S(1)}, bf16[3...) fusion(bf16[2,1024,768]{2,1,0:T(8,128)(2,1)S(1)} %bitcast.199, ...), kind=kOutput, calls=%fused_computation.197 | convolution fusion | flops 238285056 | bytes 11650560 | tf_op jit(solution)/shard_map/dot_general | solution.py:30
  397.1 2.9 add_convert_fusion
  400.3 0.8 copy-done.23
  401.2 1.1 copy-done.29
  402.3 7.5 %convert_reduce_fusion = (f32[2,1536]{1,0:T(2,128)S(1)}, f32[2,1536]{1,0:T(2,128)S(1)}, bf16[2048,1536]{1,0:T(8,128)(2,1)}) fusion(f32[2,1024]{1,0:T(2,128)S(1)} %copy-done.48, f32[2,1024]{1,0:T(2,128)S(1)} %copy-done.44, bf16[2,1024,1536]{2,1,0:T(8,128)(2,1)S(1)} %bitcast.169, bf16[2048,768]{1,0:T(8,128)(2,1)S(1)} %bitcast.177, ...), kind=kOutput, calls=%fused_computation.1 | convolution fusion | flops 4856997888 | bytes 18128896 | tf_op jit(solution)/shard_map/dot_general | solution.py:30
  409.8 1.2 copy-done.7
  411.0 1.3 copy.54
  412.3 2.6 copy.57
  415.0 2.7 copy.58
  418.2 2.6 fusion.54
  420.9 1.8 bitcast_convert_fusion
  423.1 2.1 convolution_convert_fusion.9
  425.2 2.0 convolution_convert_fusion.8
  427.7 6.4 %convolution_convert_fusion.3 = bf16[1536,384]{1,0:T(8,128)(2,1)S(1)} fusion(bf16[2048,1536]{1,0:T(8,128)(2,1)} %bitcast.183, bf16[2048,384]{1,0:T(8,128)(2,1)S(1)} %bitcast.184), kind=kOutput, calls=%fused_computation.78 | convolution fusion | flops 2416508928 | bytes 9043968 | tf_op jit(solution)/shard_map/dot_general | solution.py:26
  434.1 59.1 %weight_sums.1 = (f32[4,2,4608]{2,1,0:T(2,128)S(1)}, f32[192,6144]{1,0:T(8,128)S(1)}, f32[384,256]{1,0:T(8,128)S(1)}, f32[96,6144]{1,0:T(8,128)S(1)}, f32[16,614...) custom-call(f32[2,4608]{1,0:T(2,128)S(1)} %pad_maximum_fusion.4.m_re, ...), custom_call_target="tpu_custom_call" | custom-call | flops 60000002048 | bytes 1048576 | tf_op jit(solution)/shard_map/weight_sums/pallas_call | solution.py:1187
  493.3 2.2 copy-done.2
  495.5 1.4 copy-done.4
  496.9 3.9 reduce-scatter.5.cloned.1.call-done
  500.9 0.7 reduce_sum.229
  501.6 4.2 fusion.72
  505.8 0.5 fusion.51
  506.4 3.5 fusion.50
  509.8 2.4 copy.93
  512.2 0.7 copy.94
  513.2 1.4 copy.95
  514.6 0.6 copy.96
  515.2 0.6 copy.97
  515.8 0.6 copy.98
  516.5 0.7 copy.99
  517.2 0.6 copy.100
  (229 shorter events, 3.9 us)
Async XLA Ops:
  7.2 3.4 copy-start.80
  7.2 3.4 copy-start.81
  7.2 214.2 %all-gather.2.cloned.1.call-start = ((), (), s32[]{:S(2)}) async-start(), calls=%async_computation.2 | async-start | bytes 7077888 | tf_op jit(solution)/shard_map/all_gather | solution.py:1318
  10.8 73.2 %copy-start.77 = (bf16[8,1536]{1,0:T(8,128)(2,1)}, bf16[8,1536]{1,0:T(8,128)(2,1)S(1)}, u32[]{:S(2)}) copy-start(bf16[8,1536]{1,0:T(8,128)(2,1)S(1)} %multiply_convert_fusion.3) | copy-start | bytes 73732
  84.0 4.6 copy-start.13
  90.4 3.4 copy-start.47
  90.7 3.2 copy-start.41
  90.7 60.0 %copy-start.45 = (f32[2,1536]{1,0:T(2,128)}, f32[2,1536]{1,0:T(2,128)S(1)}, u32[]{:S(2)}) copy-start(f32[2,1536]{1,0:T(2,128)S(1)} %get-tuple-element.120) | copy-start | bytes 36868
  93.9 5.3 %copy-start.22 = (bf16[2,1024,1536]{2,1,0:T(8,128)(2,1)}, bf16[2,1024,1536]{2,1,0:T(8,128)(2,1)S(1)}, u32[]{:S(2)}) copy-start(bf16[2,1024,1536]{2,1,0:T(8,128)(2,1)S(1)} %fusion.4) | copy-start | bytes 18874372
  99.2 3.0 copy-start.49
  99.2 3.0 copy-start.69
  102.1 10.4 %copy-start.39 = (bf16[384,256]{1,0:T(8,128)(2,1)S(1)}, bf16[384,256]{1,0:T(8,128)(2,1)}, u32[]{:S(2)}) copy-start(bf16[384,256]{1,0:T(8,128)(2,1)} %param.23) | copy-start | bytes 589828
  102.3 10.8 %copy-start.53 = (f32[384]{0:T(512)}, f32[384]{0:T(512)S(1)}, u32[]{:S(2)}) copy-start(f32[384]{0:T(512)S(1)} %get-tuple-element.101) | copy-start | bytes 4612
  102.3 10.8 %copy-start.55 = (f32[384]{0:T(512)}, f32[384]{0:T(512)S(1)}, u32[]{:S(2)}) copy-start(f32[384]{0:T(512)S(1)} %get-tuple-element.102) | copy-start | bytes 4612
  102.3 10.8 %copy-start.57 = (f32[384]{0:T(512)}, f32[384]{0:T(512)S(1)}, u32[]{:S(2)}) copy-start(f32[384]{0:T(512)S(1)} %get-tuple-element.103) | copy-start | bytes 4612
  102.3 10.8 %copy-start.59 = (f32[384]{0:T(512)}, f32[384]{0:T(512)S(1)}, u32[]{:S(2)}) copy-start(f32[384]{0:T(512)S(1)} %get-tuple-element.104) | copy-start | bytes 4612
  102.3 10.8 %copy-start.61 = (f32[384]{0:T(512)}, f32[384]{0:T(512)S(1)}, u32[]{:S(2)}) copy-start(f32[384]{0:T(512)S(1)} %get-tuple-element.105) | copy-start | bytes 4612
  102.3 10.8 %copy-start.63 = (f32[384]{0:T(512)}, f32[384]{0:T(512)S(1)}, u32[]{:S(2)}) copy-start(f32[384]{0:T(512)S(1)} %get-tuple-element.106) | copy-start | bytes 4612
  102.3 10.8 %copy-start.65 = (f32[384]{0:T(512)}, f32[384]{0:T(512)S(1)}, u32[]{:S(2)}) copy-start(f32[384]{0:T(512)S(1)} %get-tuple-element.107) | copy-start | bytes 4612
  102.4 10.8 %copy-start.67 = (f32[384]{0:T(512)}, f32[384]{0:T(512)S(1)}, u32[]{:S(2)}) copy-start(f32[384]{0:T(512)S(1)} %get-tuple-element.108) | copy-start | bytes 4612
  102.4 10.8 %copy-start.71 = (f32[384]{0:T(512)}, f32[384]{0:T(512)S(1)}, u32[]{:S(2)}) copy-start(f32[384]{0:T(512)S(1)} %get-tuple-element.128) | copy-start | bytes 4612
  102.4 10.8 %copy-start.73 = (f32[384]{0:T(512)}, f32[384]{0:T(512)S(1)}, u32[]{:S(2)}) copy-start(f32[384]{0:T(512)S(1)} %get-tuple-element.127) | copy-start | bytes 4612
  114.3 36.4 %copy-start.18 = (bf16[2,128,1536]{2,1,0:T(8,128)(2,1)S(1)}, bf16[2,128,1536]{2,1,0:T(8,128)(2,1)}, u32[]{:S(2)}) copy-start(bf16[2,128,1536]{2,1,0:T(8,128)(2,1)} %param.20) | copy-start | bytes 2359300
  114.3 37.5 %copy-start.51 = (f32[6144]{0:T(1024)S(1)}, f32[6144]{0:T(1024)}, u32[]{:S(2)}) copy-start(f32[6144]{0:T(1024)} %param.28) | copy-start | bytes 73732
  114.3 37.5 %copy-start.52 = (f32[6144]{0:T(1024)S(1)}, f32[6144]{0:T(1024)}, u32[]{:S(2)}) copy-start(f32[6144]{0:T(1024)} %param.30) | copy-start | bytes 73732
  150.7 7.6 %copy-start.6 = (bf16[4,4,2,128,128]{4,3,2,1,0:T(8,128)(2,1)}, bf16[4,4,2,128,128]{4,3,2,1,0:T(8,128)(2,1)S(1)}, u32[]{:S(2)}) copy-start(bf16[4,4,2,128,128]{4,3,2,1,0:T(8,128)(2,1)S(1)} %sum_4.1) | copy-start | bytes 3145732
  151.8 204.8 %reduce-scatter.3.cloned.1.call-start = ((), (), s32[]{:S(2)}) async-start(), calls=%async_computation.3 | async-start | bytes 7077888 | tf_op jit(solution)/shard_map/reduce_scatter | solution.py:1351
  158.3 63.1 %copy-start.79 = (bf16[384,1536]{1,0:T(8,128)(2,1)S(1)}, bf16[384,1536]{1,0:T(8,128)(2,1)}, u32[]{:S(2)}) copy-start(bf16[384,1536]{1,0:T(8,128)(2,1)} %param.22) | copy-start | bytes 3538948
  232.0 7.8 %copy-start.34 = (bf16[2,1024,384]{2,1,0:T(8,128)(2,1)}, bf16[2,1024,384]{2,1,0:T(8,128)(2,1)S(1)}, u32[]{:S(2)}) copy-start(bf16[2,1024,384]{2,1,0:T(8,128)(2,1)S(1)} %get-tuple-element.112) | copy-start | bytes 4718596
  239.9 5.2 copy-start.78
  247.8 253.0 %reduce-scatter.5.cloned.1.call-start = ((), (), s32[]{:S(2)}) async-start(), calls=%async_computation.4 | async-start | bytes 7077888 | tf_op jit(solution)/shard_map/reduce_scatter | solution.py:1403
  357.8 30.2 %copy-start.21 = (bf16[2,1024,384]{2,1,0:T(8,128)(2,1)S(1)}, bf16[2,1024,384]{2,1,0:T(8,128)(2,1)}, u32[]{:S(2)}) copy-start(bf16[2,1024,384]{2,1,0:T(8,128)(2,1)} %slice.185) | copy-start | bytes 4718596
  357.8 30.2 %copy-start.40 = (bf16[384,256]{1,0:T(8,128)(2,1)S(1)}, bf16[384,256]{1,0:T(8,128)(2,1)}, u32[]{:S(2)}) copy-start(bf16[384,256]{1,0:T(8,128)(2,1)} %param.23) | copy-start | bytes 589828
  357.8 30.2 %copy-start.56 = (f32[384]{0:T(512)S(1)}, f32[384]{0:T(512)}, u32[]{:S(2)}) copy-start(f32[384]{0:T(512)} %copy-done.55) | copy-start | bytes 4612
  357.8 30.2 %copy-start.58 = (f32[384]{0:T(512)S(1)}, f32[384]{0:T(512)}, u32[]{:S(2)}) copy-start(f32[384]{0:T(512)} %copy-done.57) | copy-start | bytes 4612
  357.8 30.2 %copy-start.60 = (f32[384]{0:T(512)S(1)}, f32[384]{0:T(512)}, u32[]{:S(2)}) copy-start(f32[384]{0:T(512)} %copy-done.59) | copy-start | bytes 4612
  357.8 30.2 %copy-start.62 = (f32[384]{0:T(512)S(1)}, f32[384]{0:T(512)}, u32[]{:S(2)}) copy-start(f32[384]{0:T(512)} %copy-done.61) | copy-start | bytes 4612
  357.8 30.2 %copy-start.74 = (f32[384]{0:T(512)S(1)}, f32[384]{0:T(512)}, u32[]{:S(2)}) copy-start(f32[384]{0:T(512)} %copy-done.73) | copy-start | bytes 4612
  357.8 30.2 %copy-start.83 = (bf16[2,2,1024,384]{3,2,1,0:T(8,128)(2,1)S(1)}, bf16[2,2,1024,384]{3,2,1,0:T(8,128)(2,1)}, u32[]{:S(2)}) copy-start(bf16[2,2,1024,384]{3,2,1,0:T(8,128)(2,1)} %get-tuple-element.61) | copy-start | bytes 9437188
  387.9 3.0 copy-start.30
  387.9 2.9 copy-start.32
  388.0 2.9 copy-start.38
  388.0 2.9 copy-start.54
  388.0 2.9 copy-start.64
  388.1 2.9 copy-start.66
  388.1 13.1 %slice-start = ((s8[6291456]{0:T(1024)(128)(4,1)}), s8[4194304]{0:T(1024)(128)(4,1)S(1)}, s32[]{:S(2)}) async-start(s8[6291456]{0:T(1024)(128)(4,1)} %bitcast.168), calls=%async_computation.5 | async-start | bytes 8388608
  391.0 10.2 %slice-start.1 = ((s8[6291456]{0:T(1024)(128)(4,1)}), s8[2097152]{0:T(1024)(128)(4,1)S(1)}, s32[]{:S(2)}) async-start(s8[6291456]{0:T(1024)(128)(4,1)} %bitcast.168), calls=%async_computation.6 | async-start | bytes 4194304
  397.1 2.9 copy-start.35
  412.3 5.3 %copy-start.16 = (bf16[2,128,1536]{2,1,0:T(8,128)(2,1)S(1)}, bf16[2,128,1536]{2,1,0:T(8,128)(2,1)}, u32[]{:S(2)}) copy-start(bf16[2,128,1536]{2,1,0:T(8,128)(2,1)} %t_ref.1) | copy-start | bytes 2359300
  415.0 3.2 copy-start.25
  420.9 4.3 copy-start.31
  422.7 4.5 copy-start.19
  422.7 4.5 copy-start.26
  422.7 4.5 copy-start.76
  423.1 4.6 copy-start.24
  427.7 6.4 %copy-start.12 = (bf16[4,8,48,384]{3,2,1,0:T(8,128)(2,1)S(1)}, bf16[4,8,48,384]{3,2,1,0:T(8,128)(2,1)}, u32[]{:S(2)}) copy-start(bf16[4,8,48,384]{3,2,1,0:T(8,128)(2,1)} %copy-done.11) | copy-start | bytes 3538948
  496.9 8.9 %copy-start.17 = (bf16[2,128,1536]{2,1,0:T(8,128)(2,1)S(1)}, bf16[2,128,1536]{2,1,0:T(8,128)(2,1)}, u32[]{:S(2)}) copy-start(bf16[2,128,1536]{2,1,0:T(8,128)(2,1)} %t_ref.1) | copy-start | bytes 2359300
  496.9 8.9 %copy-start.42 = (f32[2,1536]{1,0:T(2,128)S(1)}, f32[2,1536]{1,0:T(2,128)}, u32[]{:S(2)}) copy-start(f32[2,1536]{1,0:T(2,128)} %copy-done.41) | copy-start | bytes 36868
  496.9 9.5 %copy-start.20 = (bf16[2,128,1536]{2,1,0:T(8,128)(2,1)S(1)}, bf16[2,128,1536]{2,1,0:T(8,128)(2,1)}, u32[]{:S(2)}) copy-start(bf16[2,128,1536]{2,1,0:T(8,128)(2,1)} %param.20) | copy-start | bytes 2359300
  496.9 9.5 %copy-start.46 = (f32[2,1536]{1,0:T(2,128)S(1)}, f32[2,1536]{1,0:T(2,128)}, u32[]{:S(2)}) copy-start(f32[2,1536]{1,0:T(2,128)} %copy-done.45) | copy-start | bytes 36868
  501.6 4.2 copy-start.27
  505.8 4.0 copy-start.3
  509.8 3.4 copy-start.5
  509.8 8.0 %copy-start.1 = (bf16[192,6144]{1,0:T(8,128)(2,1)S(1)}, bf16[192,6144]{1,0:T(8,128)(2,1)}, u32[]{:S(2)}) copy-start(bf16[192,6144]{1,0:T(8,128)(2,1)} %param.21) | copy-start | bytes 7077892
  (25 other events, 45.3 us)
Sparse Core Ops, SparseCore 0:
  151.9 65.1 all-gather.1
  247.9 77.1 reduce-scatter.2
  409.9 90.7 reduce-scatter.4

commit v5 on v4

--- a/solution.py
+++ b/solution.py
@@ -652,7 +652,7 @@
     pl.semaphore_wait(barrier, total)
 
 
-def total_kernel(line, v_ref, o_ref, pairbox, stage, inbox, *sems):
+def total_kernel(line, produce, v_ref, o_ref, pairbox, stage, inbox, *sems):
     pair_send, pair_recv, sum_send, sum_recv, out_send, out_recv, fwd_send, fwd_recv = sems
     me = lax.axis_index("seq")
     pos, core = me // 2, lax.rem(me, 2)
@@ -669,7 +669,11 @@
     pl.semaphore_wait(barrier, line)
 
     pair = remote(v_ref.at[:, :, 1 - core], pairbox, pair_send, pair_recv, 0, "seq", partner)
+    if produce is not None:
+        produce(1 - core)
     pair.start()
+    if produce is not None:
+        produce(core)
     pair.wait_recv()
 
     def own(q):
@@ -742,7 +746,7 @@
     dma = pltpu.SemaphoreType.DMA
     blocks = v.reshape(batch, line, 2, rows, width)
     out = pl.pallas_call(
-        functools.partial(total_kernel, line),
+        functools.partial(total_kernel, line, None),
         in_specs=[vmem],
         out_specs=vmem,
         out_shape=jax.ShapeDtypeStruct(blocks.shape, bf16),
@@ -766,6 +770,71 @@
         name="sum_" + str(call),
     )(blocks)
     return out.reshape(v.shape)
+
+
+def filter_kernel(line, x_ref, tap_ref, bias_ref, select_ref, o_ref, a_ref, padded, v_ref, *rest):
+    slots, length, width = x_ref.shape
+    taps = tap_ref.shape[1]
+    rows = v_ref.shape[3]
+    rim = 8
+    edge = jnp.zeros((slots, rim, width), f32)
+    padded[:, :rim, :] = edge
+    padded[:, rim + length :, :] = edge
+    padded[:, rim : rim + length, :] = x_ref[...].astype(f32)
+
+    def produce(core):
+        def block(q):
+            start = pl.multiple_of((q * 2 + core) * rows, rows)
+            for s in range(slots):
+                near = padded[s, pl.ds(start, rows + 2 * rim), :]
+                for d in range(2):
+                    total = bias_ref[d]
+                    for j in range(taps):
+                        first = rim + (taps - 1 - j if d == 1 else j - taps + 1)
+                        total = total + tap_ref[d, j : j + 1, :] * near[first : first + rows]
+                    active = (total / (1.0 + jnp.exp(-total))).astype(bf16)
+                    a_ref[d, s, pl.ds(start, rows), :] = active
+                    v_ref[d * slots + s, q, core] = jnp.dot(
+                        active, select_ref[d], preferred_element_type=f32
+                    ).astype(bf16)
+
+        each(0, line, block)
+
+    total_kernel(line, produce, v_ref, o_ref, *rest)
+
+
+def filter_and_select(x, taps, bias, select):
+    slots, length, width = x.shape
+    batch, columns = 2 * slots, select.shape[2]
+    shares = lax.axis_size("seq")
+    line, rows = shares // 2, length // shares
+    vmem = pl.BlockSpec(memory_space=pltpu.VMEM)
+    dma = pltpu.SemaphoreType.DMA
+    blocks = (batch, line, 2, rows, columns)
+    out, active = pl.pallas_call(
+        functools.partial(filter_kernel, line),
+        in_specs=[vmem] * 4,
+        out_specs=[vmem] * 2,
+        out_shape=[
+            jax.ShapeDtypeStruct(blocks, bf16),
+            jax.ShapeDtypeStruct((2, slots, length, width), bf16),
+        ],
+        scratch_shapes=[
+            pltpu.VMEM((slots, length + 16, width), f32),
+            pltpu.VMEM(blocks, bf16),
+            pltpu.VMEM((batch, line, rows, columns), bf16),
+            pltpu.VMEM((line, batch, rows, columns), bf16),
+            pltpu.VMEM((line, batch, rows, columns), bf16),
+        ]
+        + [dma((1,))] * 2
+        + [dma((line,))] * 6,
+        compiler_params=pltpu.CompilerParams(
+            collective_id=4, has_side_effects=True, vmem_limit_bytes=40 * 2**20
+        ),
+        cost_estimate=pl.CostEstimate(flops=30 * 10**9, bytes_accessed=2**20, transcendentals=0),
+        name="filter_and_select",
+    )(x, taps, bias, select)
+    return out.reshape(batch, length, columns), active
 
 
 def head_kernel(line, t_ref, w_ref, mod_ref, all_ref, box_ref, out_ref, parts, *sems):
@@ -1067,9 +1136,9 @@
 
     def add_part(k, total):
         part(k).wait_recv()
-        return total + m_parts[k - 1]
-
-    m_out[item] = lax.fori_loop(1, shares, add_part, m_ref[...])
+        return total + m_parts[k - 1].astype(f32)
+
+    m_out[item] = lax.fori_loop(1, shares, add_part, m_ref[...].astype(f32))
     each(1, peers, lambda t: forward_modulation(t).start())
 
     def add_select(t, total):
@@ -1191,7 +1260,7 @@
         out_shape=[jax.ShapeDtypeStruct(shape, kind) for shape, kind in outs],
         scratch_shapes=[pltpu.VMEM(shape, kind) for shape, kind in kept if direct]
         + [
-            pltpu.VMEM((shares - 1,) + modulation.shape, f32),
+            pltpu.VMEM((shares - 1,) + modulation.shape, bf16),
             pltpu.VMEM((some, shares) + g.shape[2:], bf16),
             pltpu.VMEM((some,) + small.shape[1:], bf16),
             pltpu.VMEM((some,) + select.shape[1:], bf16),
@@ -1294,24 +1363,17 @@
     rate = -jnp.exp(own_columns(decay_log))
     skip = own_columns(skip_gain)
 
-    filtered, activated, partial = [], [], []
-    for d in range(2):
-        f = tap_bias[d]
-        for j, window in enumerate(filter_windows(x_half, taps, d == 1)):
-            f = f + tap_weight[j, d] * window.astype(f32)
-        a = jax.nn.silu(f).astype(bf16)
-        filtered.append(f)
-        activated.append(a)
-        partial.append(
-            jnp.dot(
-                a.reshape(rows, mine),
-                select_weight[:, d * select : (d + 1) * select],
-                preferred_element_type=f32,
-            )
-        )
-    selection = summed_everywhere(
-        jnp.stack(partial).astype(bf16).reshape(2 * slots, length, select), 4
-    ).reshape(2, rows, select)
+    wide_taps = widen(jnp.swapaxes(tap_weight, 0, 1), padded_width)
+    wide_select = jnp.swapaxes(select_weight.reshape(mine, 2, select), 0, 1)
+    wide_select = jnp.pad(wide_select, ((0, 0), (0, padded_width - mine), (0, 0)))
+    selection, wide_active = filter_and_select(
+        widen(x_half, padded_width),
+        wide_taps,
+        widen(tap_bias[:, None, :], padded_width),
+        wide_select,
+    )
+    selection = selection.reshape(2, rows, select)
+    activated = [wide_active[d, ..., :mine] for d in range(2)]
     own_cotangent = cotangent.astype(f32)
     own_grad_branch = (valid * gate * own_cotangent).astype(bf16)
     selection, own_grad_branch = lax.optimization_barrier((selection, own_grad_branch))
@@ -1319,7 +1381,6 @@
     delta_rank = selection[:, :, :rank]
     selection = selection.reshape(2, slots, length, select)
     copies = coefficient_copies(select, rank, states)
-    wide_active = widen(jnp.stack(activated), padded_width)
     wide_rate = widen(jnp.swapaxes(rate, 0, 1) * log2e, padded_width)
     wide_weight = widen(
         jnp.pad(jnp.swapaxes(step_weight, 0, 1), ((0, 0), (0, select - rank), (0, 0))),
@@ -1334,15 +1395,16 @@
     scanned_sum = scanned[0].astype(f32) + scanned[1].astype(f32)
     silu_gate = jax.nn.silu(gate_half)
     mixed_out = (scanned_sum * silu_gate).astype(bf16).reshape(rows, mine)
+    branch_part = (
+        jnp.dot(mixed_out, out_weight, preferred_element_type=f32)
+        .astype(bf16)
+        .reshape(slots, length, model)
+    )
+    branch_part, grad_branch = lax.optimization_barrier((branch_part, grad_branch))
     grad_mixed = dot_cols(grad_branch, out_weight).reshape(slots, length, mine)
     grad_scanned = grad_mixed * silu_gate
     grad_gate_half = grad_mixed * scanned_sum * silu_slope(gate_half)
     grad_out = dot_rows(mixed_out, grad_branch).astype(bf16)
-    branch_part = (
-        jnp.dot(mixed_out, out_weight, preferred_element_type=f32)
-        .astype(bf16)
-        .reshape(slots, length, model)
-    )
     grad_gate_half = grad_gate_half.astype(bf16)
     grad_in_gate = dot_rows(mixed_in, grad_gate_half.reshape(rows, mine)).astype(bf16)
     branch_part, grad_out, grad_in_gate, scan_grad = lax.optimization_barrier(
@@ -1362,7 +1424,9 @@
         grad_out.reshape(peers, mine // peers, model),
         grad_in_gate.reshape(shares, peers, share_rows, mine),
     )
-    grad_out = grad_out.reshape(mine, model).astype(f32)
+    grad_out, grad_low = lax.optimization_barrier(
+        (grad_out.reshape(mine, model).astype(f32), grad_low)
+    )
     grad_decay = jnp.sum(grad_rate, axis=1)[..., :mine] * ln2
     grad_step_bias = jnp.sum(grad_sums[:, :8, :mine], axis=1)
     grad_skip = jnp.sum(grad_sums[:, 8:, :mine], axis=1)
@@ -1377,6 +1441,12 @@
         preferred_element_type=f32,
     )
     grad_x = jnp.zeros((slots, length, mine), f32)
+    filtered = []
+    for d in range(2):
+        f = tap_bias[d]
+        for j, window in enumerate(filter_windows(x_half, taps, d == 1)):
+            f = f + tap_weight[j, d] * window.astype(f32)
+        filtered.append(f)
     grad_select, grad_taps, grad_tap_bias = [], [], []
     for d in range(2):
         block = select_weight[:, d * select : (d + 1) * select]
@@ -1432,7 +1502,7 @@
     grad_select = jnp.concatenate(grad_select, axis=1).astype(bf16)
     cuts = [rank, states, taps, 1, 1, 1]
     grad_modulation, *results = weight_sums(
-        grad_modulation_part,
+        grad_modulation_part.astype(bf16),
         grad_in.reshape(shares, peers, share_rows, mine),
         gate_in,
         small.reshape(peers, share, 2 * mine),

time: 535 us -> 522 us (0.976)
  the two profiles are of different devices: /device:TPU:9 before, /device:TPU:0 now
where the time goes in v5:
time: 522 us; the launch traced here: 514 us
  Pallas kernels  372 us (71%)
  matrix products  56.2 us (11%)
  local copies, waits for them, and re-layouts  40.6 us (8%)
  other arithmetic  29.9 us (6%)
  between operations  15.5 us (3%)
    pallas_call x1, Pallas kernels, scan_adjoint(): pl.pallas_call(functools.partial(adjoint_kernel, block // chunk), grid=(t...  110 us
    pallas_call x1, Pallas kernels, gather_inputs(): pl.pallas_call(functools.partial(head_kernel, line), in_specs=[anywhere,...  76 us
    pallas_call x1, Pallas kernels, weight_sums(): pl.pallas_call(functools.partial(tail_kernel, cuts if direct else None),...  61.8 us
    pallas_call x1, Pallas kernels, scan_states(): pl.pallas_call(functools.partial(states_kernel, block // chunk), grid=(tw...  61.2 us
    pallas_call x1, Pallas kernels, filter_and_select(): pl.pallas_call(functools.partial(filter_kernel, line), in_specs=[vmem] *...  36.4 us
    unnamed x179, local copies, waits for them, and re-layouts  27.9 us
    pallas_call x1, Pallas kernels, summed_everywhere(): pl.pallas_call(functools.partial(total_kernel, line, None), in_specs=[vme...  26.5 us
    dot_general x4, matrix products, dot_cols(): lax.dot_general(a, b, (((1,), (1,)), ((), ())), preferred_element_type=f32)  20.2 us
  transfers between devices with their start and end apart: 3, of which 0 were waited for; matrix products, arithmetic and copies ran while one was open for 6% of the time, Pallas kernels for 45%

profile of v5, /device:TPU:0, one launch (start us, length us, event | category | flops | bytes accessed | tf_op | source)
XLA Modules:
  0.0 514.1 jit_solution(11038620269881669492)
XLA Ops:
  7.3 1.6 copy-done
  9.0 0.5 copy.53
  9.5 1.2 reshape.237.w_ref
  11.0 1.0 fusion.79.mod_ref
  12.0 76.0 %gather_inputs.1 = (bf16[2,1024,1536]{2,1,0:T(8,128)(2,1)}, bf16[8,4,48,768]{3,2,1,0:T(8,128)(2,1)}, f32[2,4608]{1,0:T(2,128)}) custom-call(bf16[2,128,1536]{2,1,0:T(8,128)(2,1)} %t_ref.1, bf16[8,48,768]{2,1,0:T(8,128)(2,1)} %reshape.237.w_ref, f32[2,4608]{1,0:T(2,128)} %fusion.79.mod_ref), custom_call_target="tpu_custom_call" | custom-call | flops 60000002048 | bytes 1048576 | tf_op jit(solution)/shard_map/gather_inputs/pallas_call | solution.py:1012
  88.0 3.8 convert_reduce_fusion
  91.9 0.7 copy-done.20
  92.6 1.8 fusion.7
  94.6 2.7 fusion.5
  97.4 5.2 %convolution_convert_fusion.2 = bf16[2048,768]{1,0:T(8,128)(2,1)S(1)} fusion(bf16[2048,1536]{1,0:T(8,128)(2,1)S(1)} %bitcast.177, bf16[1536,768]{1,0:T(8,128)(2,1)S(1)} %bitcast.187), kind=kOutput, calls=%fused_computation.31 | convolution fusion | flops 4833411072 | bytes 11796480 | tf_op jit(solution)/shard_map/dot_general | solution.py:1352
  102.7 1.6 copy-done.22
  105.0 1.0 fusion.47
  106.0 36.4 %filter_and_select.1 = (bf16[4,4,2,128,128]{4,3,2,1,0:T(8,128)(2,1)S(1)}, bf16[2,2,1024,384]{3,2,1,0:T(8,128)(2,1)S(1)}) custom-call(bf16[2,1024,384]{2,1,0:T(8,128)(2,1)S(1)} %slice.189.x_ref, f32[2,4,384]{2,1,0:T(4,128)S(1)} %get-tuple-element.133.tap_ref, f32[2,1,384]{2,1,0:T(1,128)S(1)} %dynamic-slice_convert_fusion.bias_ref, ...), custom_call_target="tpu_custom_call" | custom-call | flops 30000001024 | bytes 1048576 | tf_op jit(solution)/shard_map/filter_and_select/pallas_call | solution.py:814
  142.4 1.7 copy-done.3
  144.1 1.0 copy-done.11
  146.3 1.2 copy-done.12
  147.5 61.2 %scan_states.1 = (bf16[2,2,1024,384]{3,2,1,0:T(8,128)(2,1)S(1)}, bf16[2,2,16384,384]{3,2,1,0:T(8,128)(2,1)}, f32[2,2,1024,384]{3,2,1,0:T(8,128)}, bf16[2,2,1024,512]{3,2,1,0:T(8,128)(2,1)}) custom-call(bf16[2,2,1024,128]{3,2,1,0:T(8,128)(2,1)S(1)} %bitcast.154, bf16[2,2,1024,384]{3,2,1,0:T(8,128)(2,1)} %copy-done.3, bf16[2,128,384]{2,1,0:T(8,128)(2,1)S(1)} %pad.22.w_ref, ...), custom_call_target="tpu_custom_call" | custom-call | flops 64000000000 | bytes 83886080 | tf_op jit(solution)/shard_map/scan_states/pallas_call | solution.py:487
  208.7 1.2 fusion.33
  209.9 1.1 copy-done.43
  211.0 5.2 %convolution_convert_fusion.1 = bf16[2048,1536]{1,0:T(8,128)(2,1)} fusion(bf16[2048,384]{1,0:T(8,128)(2,1)S(1)} %bitcast.196, bf16[384,1536]{1,0:T(8,128)(2,1)S(1)} %copy-done.67), kind=kOutput, calls=%fused_computation.11 | convolution fusion | flops 2419064832 | bytes 9043968 | tf_op jit(solution)/shard_map/dot_general | solution.py:1399
  216.3 7.1 %convolution_convert_fusion.5 = bf16[384,1536]{1,0:T(8,128)(2,1)} fusion(bf16[2048,384]{1,0:T(8,128)(2,1)} %bitcast.197, bf16[2048,1536]{1,0:T(8,128)(2,1)} %bitcast.213), kind=kOutput, calls=%fused_computation.72 | convolution fusion | flops 2416508928 | bytes 9043968 | tf_op jit(solution)/shard_map/dot_general | solution.py:26
  223.4 3.5 fusion.85
  226.8 3.4 fusion.51
  230.2 4.6 convolution_convert_fusion.4
  235.0 0.6 copy-done.16
  235.7 0.5 copy-done.17
  236.2 109.6 %scan_adjoint.1 = (bf16[2,2,1024,384]{3,2,1,0:T(8,128)(2,1)}, bf16[2,2,1024,384]{3,2,1,0:T(8,128)(2,1)}, bf16[2,2,1024,128]{3,2,1,0:T(8,128)(2,1)S(1)}, f32[2,2,...) custom-call(bf16[2,2,1024,512]{3,2,1,0:T(8,128)(2,1)} %get-tuple-ele, ...), custom_call_target="tpu_custom_call" | custom-call | flops 99999997952 | bytes 104857600 | tf_op jit(solution)/shard_map/scan_adjoint/pallas_call | solution.py:548
  345.8 1.0 copy-done.9
  346.8 0.6 copy-done.13
  347.4 1.1 copy-done.18
  348.5 26.5 %sum_5.1 = bf16[4,4,2,128,128]{4,3,2,1,0:T(8,128)(2,1)S(1)} custom-call(bf16[4,4,2,128,128]{4,3,2,1,0:T(8,128)(2,1)S(1)} %bitcast.162), custom_call_target="tpu_custom_call" | custom-call | flops 24999999488 | bytes 1048576 | tf_op jit(solution)/shard_map/sum_5/pallas_call | solution.py:748
  375.2 2.7 fusion.31
  378.0 6.7 %fusion.82 = (bf16[384]{0:T(512)(128)(2,1)S(1)}, bf16[384]{0:T(512)(128)(2,1)S(1)}, bf16[384]{0:T(512)(128)(2,1)}, bf16[384]{0:T(512)(128)(2,1)S(1)}, bf16[384]{...) fusion(bf16[2,1024,768]{2,1,0:T(8,128)(2,1)S(1)} %bitcast.170, ...), kind=kOutput, calls=%fused_computation.184 | convolution fusion | flops 238285056 | bytes 11650560 | tf_op jit(solution)/shard_map/dot_general | solution.py:30
  384.7 2.9 add_convert_fusion
  387.9 0.8 copy-done.31
  388.7 1.1 copy-done.38
  389.8 7.3 %fusion.6 = (bf16[2,1536]{1,0:T(2,128)(2,1)S(1)}, bf16[2048,1536]{1,0:T(8,128)(2,1)}) fusion(bf16[2,1024,1536]{2,1,0:T(8,128)(2,1)S(1)} %bitcast.164, f32[2,1024]{1,0:T(2,128)S(1)} %copy-done.55, f32[2,1024]{1,0:T(2,128)S(1)} %copy-done.51, bf16[2048,768]{1,0:T(8,128)(2,1)S(1)} %bitcast.166, bf16[1536,768]{1,0:T(8,128)(2,1)S(1)} %bitcast.188), kind=kOutput, calls=%fused_computation.8 | convolution fusion | flops 4853855232 | bytes 18110464 | tf_op jit(solution)/shard_map/dot_general | solution.py:30
  397.2 2.4 copy.59
  399.6 2.0 fusion.83
  401.6 2.6 copy.63
  404.2 2.7 copy.62
  407.5 1.8 bitcast_convert_fusion
  409.2 0.8 copy-done.34
  410.0 0.7 fusion.50
  411.3 2.2 convolution_convert_fusion.7
  413.5 2.0 convolution_convert_fusion.8
  415.6 0.4 fusion.45
  416.0 4.1 bitcast_reduce_fusion
  420.1 3.5 convolution_convert_fusion.3
  423.6 61.8 %weight_sums.1 = (f32[4,2,4608]{2,1,0:T(2,128)S(1)}, f32[192,6144]{1,0:T(8,128)S(1)}, f32[384,256]{1,0:T(8,128)S(1)}, f32[96,6144]{1,0:T(8,128)S(1)}, f32[16,614...) custom-call(bf16[2,4608]{1,0:T(2,128)(2,1)S(1)} %pad_maximum_fusion., ...), custom_call_target="tpu_custom_call" | custom-call | flops 60000002048 | bytes 1048576 | tf_op jit(solution)/shard_map/weight_sums/pallas_call | solution.py:1256
  485.5 2.2 copy-done.2
  487.7 1.4 copy-done.5
  489.2 0.7 reduce_sum.229
  489.9 1.8 fusion.49
  491.7 4.2 fusion.67
  495.9 3.2 fusion.48
  499.1 2.4 copy.100
  501.5 0.7 copy.101
  502.5 1.4 copy.102
  503.9 0.6 copy.103
  504.5 0.6 copy.104
  505.1 0.6 copy.105
  505.7 0.7 copy.106
  506.5 0.6 copy.107
  (224 shorter events, 4.2 us)
Async XLA Ops:
  7.2 3.4 copy-start.61
  7.2 3.4 copy-start.70
  7.2 3.5 copy-start.69
  7.2 3.5 copy-start.71
  7.2 209.0 %all-gather.2.cloned.1.call-start = ((), (), s32[]{:S(2)}) async-start(), calls=%async_computation.2 | async-start | bytes 7077888 | tf_op jit(solution)/shard_map/all_gather | solution.py:1380
  8.9 2.1 copy-start.42
  10.7 83.7 %copy-start.62 = (f32[2]{0:T(128)}, f32[2]{0:T(128)S(1)}, u32[]{:S(2)}) copy-start(f32[2]{0:T(128)S(1)} %dynamic-slice_convert_fusion.1) | copy-start | bytes 28
  11.0 77.1 %copy-start.64 = (bf16[8,1536]{1,0:T(8,128)(2,1)}, bf16[8,1536]{1,0:T(8,128)(2,1)S(1)}, u32[]{:S(2)}) copy-start(bf16[8,1536]{1,0:T(8,128)(2,1)S(1)} %multiply_convert_fusion.1) | copy-start | bytes 73732
  88.0 4.6 copy-start.20
  92.6 2.0 copy-start.50
  94.4 2.9 copy-start.54
  94.6 2.8 copy-start.48
  94.6 10.4 %copy-start.52 = (f32[2,1536]{1,0:T(2,128)}, f32[2,1536]{1,0:T(2,128)S(1)}, u32[]{:S(2)}) copy-start(f32[2,1536]{1,0:T(2,128)S(1)} %get-tuple-element.129) | copy-start | bytes 36868
  94.6 2.8 copy-start.37
  97.4 5.3 %copy-start.30 = (bf16[2,1024,1536]{2,1,0:T(8,128)(2,1)}, bf16[2,1024,1536]{2,1,0:T(8,128)(2,1)S(1)}, u32[]{:S(2)}) copy-start(bf16[2,1024,1536]{2,1,0:T(8,128)(2,1)S(1)} %fusion.5) | copy-start | bytes 18874372
  102.7 1.9 copy-start.46
  102.7 2.3 copy-start.26
  104.5 38.0 %copy-start.7 = (bf16[2,1024,384]{2,1,0:T(8,128)(2,1)}, bf16[2,1024,384]{2,1,0:T(8,128)(2,1)S(1)}, u32[]{:S(2)}) copy-start(bf16[2,1024,384]{2,1,0:T(8,128)(2,1)S(1)} %slice.189.x_ref) | copy-start | bytes 4718596
  106.0 39.4 %copy-start.44 = (bf16[96,6144]{1,0:T(8,128)(2,1)S(1)}, bf16[96,6144]{1,0:T(8,128)(2,1)}, u32[]{:S(2)}) copy-start(bf16[96,6144]{1,0:T(8,128)(2,1)} %param.25) | copy-start | bytes 3538948
  145.1 203.4 %reduce-scatter.3.cloned.1.call-start = ((), (), s32[]{:S(2)}) async-start(), calls=%async_computation.3 | async-start | bytes 7077888 | tf_op jit(solution)/shard_map/reduce_scatter | solution.py:1413
  146.2 62.5 %copy-start.15 = (f32[2,16,384]{2,1,0:T(8,128)}, f32[2,16,384]{2,1,0:T(8,128)S(1)}, u32[]{:S(2)}) copy-start(f32[2,16,384]{2,1,0:T(8,128)S(1)} %fusion.60.r_ref) | copy-start | bytes 147460
  147.5 61.2 %copy-start.23 = (bf16[2048,768]{1,0:T(8,128)(2,1)S(1)}, bf16[2048,768]{1,0:T(8,128)(2,1)}, u32[]{:S(2)}) copy-start(bf16[2048,768]{1,0:T(8,128)(2,1)} %copy-done.22) | copy-start | bytes 9437188
  208.7 2.3 copy-start.67
  216.3 7.1 %copy-start.66 = (bf16[2,1024,1536]{2,1,0:T(8,128)(2,1)S(1)}, bf16[2,1024,1536]{2,1,0:T(8,128)(2,1)}, u32[]{:S(2)}) copy-start(bf16[2,1024,1536]{2,1,0:T(8,128)(2,1)} %all-gather.2.cloned.1.call-done) | copy-start | bytes 18874372
  216.3 7.1 %copy-start.68 = (bf16[384,1536]{1,0:T(8,128)(2,1)S(1)}, bf16[384,1536]{1,0:T(8,128)(2,1)}, u32[]{:S(2)}) copy-start(bf16[384,1536]{1,0:T(8,128)(2,1)} %param.22) | copy-start | bytes 3538948
  216.3 14.0 %slice-start.4 = ((s8[6291456]{0:T(1024)(128)(4,1)}), s8[4194304]{0:T(1024)(128)(4,1)S(1)}, s32[]{:S(2)}) async-start(s8[6291456]{0:T(1024)(128)(4,1)} %bitcast.178), calls=%async_computation.9 | async-start | bytes 8388608
  223.4 3.5 copy-start.24
  223.4 6.9 %slice-start.5 = ((s8[6291456]{0:T(1024)(128)(4,1)}), s8[2097152]{0:T(1024)(128)(4,1)S(1)}, s32[]{:S(2)}) async-start(s8[6291456]{0:T(1024)(128)(4,1)} %bitcast.178), calls=%async_computation.10 | async-start | bytes 4194304
  230.2 4.7 copy-start.28
  234.9 254.2 %reduce-scatter.5.cloned.1.call-start = ((), (), s32[]{:S(2)}) async-start(), calls=%async_computation.4 | async-start | bytes 7077888 | tf_op jit(solution)/shard_map/reduce_scatter | solution.py:1473
  348.5 26.7 %copy-start.8 = (bf16[2,1024,384]{2,1,0:T(8,128)(2,1)S(1)}, bf16[2,1024,384]{2,1,0:T(8,128)(2,1)}, u32[]{:S(2)}) copy-start(bf16[2,1024,384]{2,1,0:T(8,128)(2,1)} %copy-done.7) | copy-start | bytes 4718596
  348.5 26.7 %copy-start.47 = (bf16[384,256]{1,0:T(8,128)(2,1)S(1)}, bf16[384,256]{1,0:T(8,128)(2,1)}, u32[]{:S(2)}) copy-start(bf16[384,256]{1,0:T(8,128)(2,1)} %param.23) | copy-start | bytes 589828
  348.5 26.7 %copy-start.72 = (bf16[2,2,1024,384]{3,2,1,0:T(8,128)(2,1)S(1)}, bf16[2,2,1024,384]{3,2,1,0:T(8,128)(2,1)}, u32[]{:S(2)}) copy-start(bf16[2,2,1024,384]{3,2,1,0:T(8,128)(2,1)} %get-tuple-element.71) | copy-start | bytes 9437188
  375.1 2.8 copy-start.41
  375.1 2.8 copy-start.39
  375.2 2.8 copy-start.25
  375.2 13.5 %slice-start.2 = ((s8[6291456]{0:T(1024)(128)(4,1)}), s8[4194304]{0:T(1024)(128)(4,1)S(1)}, s32[]{:S(2)}) async-start(s8[6291456]{0:T(1024)(128)(4,1)} %bitcast.163), calls=%async_computation.7 | async-start | bytes 8388608
  378.0 10.7 %slice-start.3 = ((s8[6291456]{0:T(1024)(128)(4,1)}), s8[2097152]{0:T(1024)(128)(4,1)S(1)}, s32[]{:S(2)}) async-start(s8[6291456]{0:T(1024)(128)(4,1)} %bitcast.163), calls=%async_computation.8 | async-start | bytes 4194304
  384.7 2.9 copy-start.29
  387.6 2.2 copy-start.38
  387.6 2.2 copy-start.51
  387.6 2.2 copy-start.55
  397.1 2.4 copy-start.4
  401.6 5.3 %copy-start.21 = (bf16[2,128,1536]{2,1,0:T(8,128)(2,1)S(1)}, bf16[2,128,1536]{2,1,0:T(8,128)(2,1)}, u32[]{:S(2)}) copy-start(bf16[2,128,1536]{2,1,0:T(8,128)(2,1)} %t_ref.1) | copy-start | bytes 2359300
  404.2 3.2 copy-start.10
  406.9 2.4 copy-start.33
  406.9 3.2 copy-start.34
  407.5 3.3 copy-start.14
  410.7 2.8 copy-start.40
  410.7 4.8 copy-start.27
  410.8 4.8 copy-start.35
  410.8 4.8 copy-start.63
  411.2 8.9 %slice-start.6 = ((s8[6291456]{0:T(1024)(128)(4,1)}), s8[4194304]{0:T(1024)(128)(4,1)S(1)}, s32[]{:S(2)}) async-start(s8[6291456]{0:T(1024)(128)(4,1)} %bitcast.181), calls=%async_computation.11 | async-start | bytes 8388608
  415.6 4.5 slice-start.7
  416.0 4.1 copy-start.32
  420.1 3.5 copy-start.19
  423.6 66.2 %copy-start.49 = (f32[2,1536]{1,0:T(2,128)S(1)}, f32[2,1536]{1,0:T(2,128)}, u32[]{:S(2)}) copy-start(f32[2,1536]{1,0:T(2,128)} %copy-done.48) | copy-start | bytes 36868
  485.5 2.2 copy-start.2
  489.1 6.8 %copy-start.53 = (f32[2,1536]{1,0:T(2,128)S(1)}, f32[2,1536]{1,0:T(2,128)}, u32[]{:S(2)}) copy-start(f32[2,1536]{1,0:T(2,128)} %copy-done.52) | copy-start | bytes 36868
  489.9 6.0 %copy-start.36 = (bf16[2,128,1536]{2,1,0:T(8,128)(2,1)S(1)}, bf16[2,128,1536]{2,1,0:T(8,128)(2,1)}, u32[]{:S(2)}) copy-start(bf16[2,128,1536]{2,1,0:T(8,128)(2,1)} %reduce-scatter.5.cloned.1.call-done) | copy-start | bytes 2359300
  489.9 9.2 %slice-start = ((s8[4718592]{0:T(1024)(128)(4,1)}), s8[4194304]{0:T(1024)(128)(4,1)S(1)}, s32[]{:S(2)}) async-start(s8[4718592]{0:T(1024)(128)(4,1)} %bitcast.151), calls=%async_computation.5 | async-start | bytes 8388608
  491.7 7.4 %slice-start.1 = ((s8[4718592]{0:T(1024)(128)(4,1)}), s8[524288]{0:T(1024)(128)(4,1)S(1)}, s32[]{:S(2)}) async-start(s8[4718592]{0:T(1024)(128)(4,1)} %bitcast.151), calls=%async_computation.6 | async-start | bytes 1048576
  499.1 3.4 copy-start.6
  499.1 8.0 %copy-start.1 = (bf16[192,6144]{1,0:T(8,128)(2,1)S(1)}, bf16[192,6144]{1,0:T(8,128)(2,1)}, u32[]{:S(2)}) copy-start(bf16[192,6144]{1,0:T(8,128)(2,1)} %param.21) | copy-start | bytes 7077892
  (20 other events, 28.5 us)
Sparse Core Ops, SparseCore 0:
  145.2 69.1 all-gather.1
  235.0 79.0 reduce-scatter.2
  397.3 86.7 reduce-scatter.4

commit v6 on v5

--- a/solution.py
+++ b/solution.py
@@ -948,9 +948,9 @@
 
     def add(k, total):
         modulation(k).wait_recv()
-        return total + parts[k - 1]
-
-    out_ref[...] = lax.fori_loop(1, shares, add, mod_ref[...])
+        return total + parts[k - 1].astype(f32)
+
+    out_ref[...] = lax.fori_loop(1, shares, add, mod_ref[...].astype(f32))
     each(1, line - 1, relay)
 
     def finish(k):
@@ -1018,7 +1018,7 @@
             jax.ShapeDtypeStruct((shares, peers) + blocks.shape[1:], bf16),
             jax.ShapeDtypeStruct(modulation.shape, f32),
         ],
-        scratch_shapes=[pltpu.VMEM((shares - 1,) + modulation.shape, f32), dma, dma((slots,))]
+        scratch_shapes=[pltpu.VMEM((shares - 1,) + modulation.shape, bf16), dma, dma((slots,))]
         + [dma((line * slots,))] * 6
         + [dma((shares,))] * 2
         + [dma((shares * (peers - 1),))] * 2
@@ -1335,7 +1335,7 @@
     )
     own_rows = jnp.moveaxis(own_rows.reshape(share_rows, 2, shares, mine), 2, 0)
     all_tokens, own_in, modulation = gather_inputs(
-        tokens, own_rows.reshape(shares, share_rows, 2 * mine), modulation_part
+        tokens, own_rows.reshape(shares, share_rows, 2 * mine), modulation_part.astype(bf16)
     )
     own_in = own_in.reshape(model, 2 * mine)
     modulation = modulation + modulation_bias.astype(f32)[None, :]

time: 522 us -> 519 us (level)
  no operation moved by 1% of the time
where the time goes in v6:
time: 519 us; the launch traced here: 511 us
  Pallas kernels  369 us (71%)
  matrix products  56.2 us (11%)
  local copies, waits for them, and re-layouts  40.6 us (8%)
  other arithmetic  29.9 us (6%)
  between operations  15.5 us (3%)
    pallas_call x1, Pallas kernels, scan_adjoint(): pl.pallas_call(functools.partial(adjoint_kernel, block // chunk), grid=(t...  110 us
    pallas_call x1, Pallas kernels, gather_inputs(): pl.pallas_call(functools.partial(head_kernel, line), in_specs=[anywhere,...  73.6 us
    pallas_call x1, Pallas kernels, weight_sums(): pl.pallas_call(functools.partial(tail_kernel, cuts if direct else None),...  61.8 us
    pallas_call x1, Pallas kernels, scan_states(): pl.pallas_call(functools.partial(states_kernel, block // chunk), grid=(tw...  61.2 us
    pallas_call x1, Pallas kernels, filter_and_select(): pl.pallas_call(functools.partial(filter_kernel, line), in_specs=[vmem] *...  36.1 us
    unnamed x179, local copies, waits for them, and re-layouts  27.9 us
    pallas_call x1, Pallas kernels, summed_everywhere(): pl.pallas_call(functools.partial(total_kernel, line, None), in_specs=[vme...  26.5 us
    dot_general x4, matrix products, dot_cols(): lax.dot_general(a, b, (((1,), (1,)), ((), ())), preferred_element_type=f32)  20.2 us
  transfers between devices with their start and end apart: 3, of which 0 were waited for; matrix products, arithmetic and copies ran while one was open for 6% of the time, Pallas kernels for 45%

profile of v6, /device:TPU:0, one launch (start us, length us, event | category | flops | bytes accessed | tf_op | source)
XLA Modules:
  0.0 511.4 jit_solution(4972423250997896496)
XLA Ops:
  7.3 1.6 copy-done
  9.0 0.5 copy.53
  9.5 1.2 reshape.237.w_ref
  11.0 1.0 convolution_convert_fusion.2.mod_ref
  12.0 73.6 %gather_inputs.1 = (bf16[2,1024,1536]{2,1,0:T(8,128)(2,1)}, bf16[8,4,48,768]{3,2,1,0:T(8,128)(2,1)}, f32[2,4608]{1,0:T(2,128)}) custom-call(bf16[2,128,1536]{2,1,0:T(8,128)(2,1)} %t_ref.1, bf16[8,48,768]{2,1,0:T(8,128)(2,1)} %reshape.237.w_ref, bf16[2,4608]{1,0:T(2,128)(2,1)} %convolution_convert_fusion.2.mod_ref), custom_call_target="tpu_custom_call" | custom-call | flops 60000002048 | bytes 1048576 | tf_op jit(solution)/shard_map/gather_inputs/pallas_call | solution.py:1012
  85.6 3.8 convert_reduce_fusion
  89.4 0.7 copy-done.20
  90.2 1.8 fusion.7
  92.2 2.7 fusion.5
  94.9 5.2 %convolution_convert_fusion.3 = bf16[2048,768]{1,0:T(8,128)(2,1)S(1)} fusion(bf16[2048,1536]{1,0:T(8,128)(2,1)S(1)} %bitcast.177, bf16[1536,768]{1,0:T(8,128)(2,1)S(1)} %bitcast.187), kind=kOutput, calls=%fused_computation.32 | convolution fusion | flops 4833411072 | bytes 11796480 | tf_op jit(solution)/shard_map/dot_general | solution.py:1352
  100.3 1.6 copy-done.22
  102.5 1.0 fusion.47
  103.6 36.1 %filter_and_select.1 = (bf16[4,4,2,128,128]{4,3,2,1,0:T(8,128)(2,1)S(1)}, bf16[2,2,1024,384]{3,2,1,0:T(8,128)(2,1)S(1)}) custom-call(bf16[2,1024,384]{2,1,0:T(8,128)(2,1)S(1)} %slice.189.x_ref, f32[2,4,384]{2,1,0:T(4,128)S(1)} %get-tuple-element.133.tap_ref, f32[2,1,384]{2,1,0:T(1,128)S(1)} %dynamic-slice_convert_fusion.bias_ref, ...), custom_call_target="tpu_custom_call" | custom-call | flops 30000001024 | bytes 1048576 | tf_op jit(solution)/shard_map/filter_and_select/pallas_call | solution.py:814
  139.7 1.7 copy-done.3
  141.4 1.0 copy-done.11
  143.5 1.2 copy-done.12
  144.7 61.2 %scan_states.1 = (bf16[2,2,1024,384]{3,2,1,0:T(8,128)(2,1)S(1)}, bf16[2,2,16384,384]{3,2,1,0:T(8,128)(2,1)}, f32[2,2,1024,384]{3,2,1,0:T(8,128)}, bf16[2,2,1024,512]{3,2,1,0:T(8,128)(2,1)}) custom-call(bf16[2,2,1024,128]{3,2,1,0:T(8,128)(2,1)S(1)} %bitcast.154, bf16[2,2,1024,384]{3,2,1,0:T(8,128)(2,1)} %copy-done.3, bf16[2,128,384]{2,1,0:T(8,128)(2,1)S(1)} %pad.22.w_ref, ...), custom_call_target="tpu_custom_call" | custom-call | flops 64000000000 | bytes 83886080 | tf_op jit(solution)/shard_map/scan_states/pallas_call | solution.py:487
  205.9 1.2 fusion.33
  207.1 1.1 copy-done.43
  208.3 5.2 %convolution_convert_fusion.1 = bf16[2048,1536]{1,0:T(8,128)(2,1)} fusion(bf16[2048,384]{1,0:T(8,128)(2,1)S(1)} %bitcast.196, bf16[384,1536]{1,0:T(8,128)(2,1)S(1)} %copy-done.67), kind=kOutput, calls=%fused_computation.11 | convolution fusion | flops 2419064832 | bytes 9043968 | tf_op jit(solution)/shard_map/dot_general | solution.py:1399
  213.5 7.1 %convolution_convert_fusion.6 = bf16[384,1536]{1,0:T(8,128)(2,1)} fusion(bf16[2048,384]{1,0:T(8,128)(2,1)} %bitcast.197, bf16[2048,1536]{1,0:T(8,128)(2,1)} %bitcast.213), kind=kOutput, calls=%fused_computation.73 | convolution fusion | flops 2416508928 | bytes 9043968 | tf_op jit(solution)/shard_map/dot_general | solution.py:26
  220.6 3.5 fusion.84
  224.1 3.4 fusion.51
  227.5 4.6 convolution_convert_fusion.5
  232.2 0.6 copy-done.16
  232.9 0.5 copy-done.17
  233.4 109.7 %scan_adjoint.1 = (bf16[2,2,1024,384]{3,2,1,0:T(8,128)(2,1)}, bf16[2,2,1024,384]{3,2,1,0:T(8,128)(2,1)}, bf16[2,2,1024,128]{3,2,1,0:T(8,128)(2,1)S(1)}, f32[2,2,...) custom-call(bf16[2,2,1024,512]{3,2,1,0:T(8,128)(2,1)} %get-tuple-ele, ...), custom_call_target="tpu_custom_call" | custom-call | flops 99999997952 | bytes 104857600 | tf_op jit(solution)/shard_map/scan_adjoint/pallas_call | solution.py:548
  343.1 1.0 copy-done.9
  344.1 0.6 copy-done.13
  344.7 1.1 copy-done.18
  345.8 26.5 %sum_5.1 = bf16[4,4,2,128,128]{4,3,2,1,0:T(8,128)(2,1)S(1)} custom-call(bf16[4,4,2,128,128]{4,3,2,1,0:T(8,128)(2,1)S(1)} %bitcast.162), custom_call_target="tpu_custom_call" | custom-call | flops 24999999488 | bytes 1048576 | tf_op jit(solution)/shard_map/sum_5/pallas_call | solution.py:748
  372.5 2.8 fusion.31
  375.3 6.7 %fusion.81 = (bf16[384]{0:T(512)(128)(2,1)S(1)}, bf16[384]{0:T(512)(128)(2,1)S(1)}, bf16[384]{0:T(512)(128)(2,1)}, bf16[384]{0:T(512)(128)(2,1)S(1)}, bf16[384]{...) fusion(bf16[2,1024,768]{2,1,0:T(8,128)(2,1)S(1)} %bitcast.170, ...), kind=kOutput, calls=%fused_computation.184 | convolution fusion | flops 238285056 | bytes 11650560 | tf_op jit(solution)/shard_map/dot_general | solution.py:30
  382.0 2.9 add_convert_fusion
  385.2 0.8 copy-done.31
  386.0 1.1 copy-done.38
  387.1 7.3 %fusion.6 = (bf16[2,1536]{1,0:T(2,128)(2,1)S(1)}, bf16[2048,1536]{1,0:T(8,128)(2,1)}) fusion(bf16[2,1024,1536]{2,1,0:T(8,128)(2,1)S(1)} %bitcast.164, f32[2,1024]{1,0:T(2,128)S(1)} %copy-done.55, f32[2,1024]{1,0:T(2,128)S(1)} %copy-done.51, bf16[2048,768]{1,0:T(8,128)(2,1)S(1)} %bitcast.166, bf16[1536,768]{1,0:T(8,128)(2,1)S(1)} %bitcast.188), kind=kOutput, calls=%fused_computation.8 | convolution fusion | flops 4853855232 | bytes 18110464 | tf_op jit(solution)/shard_map/dot_general | solution.py:30
  394.5 2.4 copy.59
  396.9 2.0 fusion.82
  398.9 2.6 copy.63
  401.5 2.7 copy.62
  404.8 1.8 bitcast_convert_fusion
  406.6 0.8 copy-done.34
  407.3 0.7 fusion.50
  408.6 2.2 convolution_convert_fusion.8
  410.8 2.0 convolution_convert_fusion.9
  412.9 0.4 fusion.45
  413.3 4.1 bitcast_reduce_fusion
  417.4 3.5 convolution_convert_fusion.4
  421.0 61.8 %weight_sums.1 = (f32[4,2,4608]{2,1,0:T(2,128)S(1)}, f32[192,6144]{1,0:T(8,128)S(1)}, f32[384,256]{1,0:T(8,128)S(1)}, f32[96,6144]{1,0:T(8,128)S(1)}, f32[16,614...) custom-call(bf16[2,4608]{1,0:T(2,128)(2,1)S(1)} %pad_maximum_fusion., ...), custom_call_target="tpu_custom_call" | custom-call | flops 60000002048 | bytes 1048576 | tf_op jit(solution)/shard_map/weight_sums/pallas_call | solution.py:1256
  482.8 2.2 copy-done.2
  485.0 1.4 copy-done.5
  486.5 0.7 reduce_sum.229
  487.2 1.8 fusion.49
  489.0 4.2 fusion.67
  493.2 3.2 fusion.48
  496.4 2.4 copy.100
  498.8 0.7 copy.101
  499.8 1.4 copy.102
  501.2 0.6 copy.103
  501.8 0.6 copy.104
  502.4 0.6 copy.105
  503.0 0.7 copy.106
  503.8 0.6 copy.107
  (224 shorter events, 4.2 us)
Async XLA Ops:
  7.2 3.4 copy-start.61
  7.2 3.4 copy-start.70
  7.2 3.5 copy-start.69
  7.2 3.5 copy-start.71
  7.2 206.3 %all-gather.2.cloned.1.call-start = ((), (), s32[]{:S(2)}) async-start(), calls=%async_computation.2 | async-start | bytes 7077888 | tf_op jit(solution)/shard_map/all_gather | solution.py:1380
  8.9 2.1 copy-start.42
  10.7 81.3 %copy-start.62 = (f32[2]{0:T(128)}, f32[2]{0:T(128)S(1)}, u32[]{:S(2)}) copy-start(f32[2]{0:T(128)S(1)} %dynamic-slice_convert_fusion.1) | copy-start | bytes 28
  11.0 74.6 %copy-start.64 = (bf16[8,1536]{1,0:T(8,128)(2,1)}, bf16[8,1536]{1,0:T(8,128)(2,1)S(1)}, u32[]{:S(2)}) copy-start(bf16[8,1536]{1,0:T(8,128)(2,1)S(1)} %multiply_convert_fusion.1) | copy-start | bytes 73732
  85.6 4.6 copy-start.20
  90.2 2.0 copy-start.50
  92.0 2.9 copy-start.54
  92.1 2.8 copy-start.48
  92.1 10.4 %copy-start.52 = (f32[2,1536]{1,0:T(2,128)}, f32[2,1536]{1,0:T(2,128)S(1)}, u32[]{:S(2)}) copy-start(f32[2,1536]{1,0:T(2,128)S(1)} %get-tuple-element.129) | copy-start | bytes 36868
  92.2 2.8 copy-start.37
  94.9 5.3 %copy-start.30 = (bf16[2,1024,1536]{2,1,0:T(8,128)(2,1)}, bf16[2,1024,1536]{2,1,0:T(8,128)(2,1)S(1)}, u32[]{:S(2)}) copy-start(bf16[2,1024,1536]{2,1,0:T(8,128)(2,1)S(1)} %fusion.5) | copy-start | bytes 18874372
  100.2 1.9 copy-start.46
  100.2 2.3 copy-start.26
  102.0 37.6 %copy-start.7 = (bf16[2,1024,384]{2,1,0:T(8,128)(2,1)}, bf16[2,1024,384]{2,1,0:T(8,128)(2,1)S(1)}, u32[]{:S(2)}) copy-start(bf16[2,1024,384]{2,1,0:T(8,128)(2,1)S(1)} %slice.189.x_ref) | copy-start | bytes 4718596
  103.6 39.1 %copy-start.44 = (bf16[96,6144]{1,0:T(8,128)(2,1)S(1)}, bf16[96,6144]{1,0:T(8,128)(2,1)}, u32[]{:S(2)}) copy-start(bf16[96,6144]{1,0:T(8,128)(2,1)} %param.25) | copy-start | bytes 3538948
  142.4 203.4 %reduce-scatter.3.cloned.1.call-start = ((), (), s32[]{:S(2)}) async-start(), calls=%async_computation.3 | async-start | bytes 7077888 | tf_op jit(solution)/shard_map/reduce_scatter | solution.py:1413
  143.5 62.5 %copy-start.15 = (f32[2,16,384]{2,1,0:T(8,128)}, f32[2,16,384]{2,1,0:T(8,128)S(1)}, u32[]{:S(2)}) copy-start(f32[2,16,384]{2,1,0:T(8,128)S(1)} %fusion.60.r_ref) | copy-start | bytes 147460
  144.7 61.2 %copy-start.23 = (bf16[2048,768]{1,0:T(8,128)(2,1)S(1)}, bf16[2048,768]{1,0:T(8,128)(2,1)}, u32[]{:S(2)}) copy-start(bf16[2048,768]{1,0:T(8,128)(2,1)} %copy-done.22) | copy-start | bytes 9437188
  205.9 2.3 copy-start.67
  213.5 7.1 %copy-start.66 = (bf16[2,1024,1536]{2,1,0:T(8,128)(2,1)S(1)}, bf16[2,1024,1536]{2,1,0:T(8,128)(2,1)}, u32[]{:S(2)}) copy-start(bf16[2,1024,1536]{2,1,0:T(8,128)(2,1)} %all-gather.2.cloned.1.call-done) | copy-start | bytes 18874372
  213.5 7.1 %copy-start.68 = (bf16[384,1536]{1,0:T(8,128)(2,1)S(1)}, bf16[384,1536]{1,0:T(8,128)(2,1)}, u32[]{:S(2)}) copy-start(bf16[384,1536]{1,0:T(8,128)(2,1)} %param.22) | copy-start | bytes 3538948
  213.5 14.0 %slice-start.4 = ((s8[6291456]{0:T(1024)(128)(4,1)}), s8[4194304]{0:T(1024)(128)(4,1)S(1)}, s32[]{:S(2)}) async-start(s8[6291456]{0:T(1024)(128)(4,1)} %bitcast.178), calls=%async_computation.9 | async-start | bytes 8388608
  220.6 3.5 copy-start.24
  220.6 6.9 %slice-start.5 = ((s8[6291456]{0:T(1024)(128)(4,1)}), s8[2097152]{0:T(1024)(128)(4,1)S(1)}, s32[]{:S(2)}) async-start(s8[6291456]{0:T(1024)(128)(4,1)} %bitcast.178), calls=%async_computation.10 | async-start | bytes 4194304
  227.4 4.7 copy-start.28
  232.1 254.3 %reduce-scatter.5.cloned.1.call-start = ((), (), s32[]{:S(2)}) async-start(), calls=%async_computation.4 | async-start | bytes 7077888 | tf_op jit(solution)/shard_map/reduce_scatter | solution.py:1473
  345.8 26.7 %copy-start.8 = (bf16[2,1024,384]{2,1,0:T(8,128)(2,1)S(1)}, bf16[2,1024,384]{2,1,0:T(8,128)(2,1)}, u32[]{:S(2)}) copy-start(bf16[2,1024,384]{2,1,0:T(8,128)(2,1)} %copy-done.7) | copy-start | bytes 4718596
  345.8 26.7 %copy-start.47 = (bf16[384,256]{1,0:T(8,128)(2,1)S(1)}, bf16[384,256]{1,0:T(8,128)(2,1)}, u32[]{:S(2)}) copy-start(bf16[384,256]{1,0:T(8,128)(2,1)} %param.23) | copy-start | bytes 589828
  345.8 26.7 %copy-start.72 = (bf16[2,2,1024,384]{3,2,1,0:T(8,128)(2,1)S(1)}, bf16[2,2,1024,384]{3,2,1,0:T(8,128)(2,1)}, u32[]{:S(2)}) copy-start(bf16[2,2,1024,384]{3,2,1,0:T(8,128)(2,1)} %get-tuple-element.71) | copy-start | bytes 9437188
  372.4 2.8 copy-start.41
  372.4 2.8 copy-start.39
  372.5 2.8 copy-start.25
  372.5 13.5 %slice-start.2 = ((s8[6291456]{0:T(1024)(128)(4,1)}), s8[4194304]{0:T(1024)(128)(4,1)S(1)}, s32[]{:S(2)}) async-start(s8[6291456]{0:T(1024)(128)(4,1)} %bitcast.163), calls=%async_computation.7 | async-start | bytes 8388608
  375.3 10.7 %slice-start.3 = ((s8[6291456]{0:T(1024)(128)(4,1)}), s8[2097152]{0:T(1024)(128)(4,1)S(1)}, s32[]{:S(2)}) async-start(s8[6291456]{0:T(1024)(128)(4,1)} %bitcast.163), calls=%async_computation.8 | async-start | bytes 4194304
  382.0 2.9 copy-start.29
  384.9 2.2 copy-start.38
  384.9 2.2 copy-start.51
  384.9 2.2 copy-start.55
  394.4 2.4 copy-start.4
  398.9 5.3 %copy-start.21 = (bf16[2,128,1536]{2,1,0:T(8,128)(2,1)S(1)}, bf16[2,128,1536]{2,1,0:T(8,128)(2,1)}, u32[]{:S(2)}) copy-start(bf16[2,128,1536]{2,1,0:T(8,128)(2,1)} %t_ref.1) | copy-start | bytes 2359300
  401.5 3.2 copy-start.10
  404.2 2.4 copy-start.33
  404.2 3.1 copy-start.34
  404.8 3.3 copy-start.14
  408.0 2.8 copy-start.40
  408.0 4.8 copy-start.27
  408.1 4.8 copy-start.35
  408.1 4.8 copy-start.63
  408.5 8.8 %slice-start.6 = ((s8[6291456]{0:T(1024)(128)(4,1)}), s8[4194304]{0:T(1024)(128)(4,1)S(1)}, s32[]{:S(2)}) async-start(s8[6291456]{0:T(1024)(128)(4,1)} %bitcast.181), calls=%async_computation.11 | async-start | bytes 8388608
  412.9 4.5 slice-start.7
  413.3 4.1 copy-start.32
  417.4 3.5 copy-start.19
  420.9 66.2 %copy-start.49 = (f32[2,1536]{1,0:T(2,128)S(1)}, f32[2,1536]{1,0:T(2,128)}, u32[]{:S(2)}) copy-start(f32[2,1536]{1,0:T(2,128)} %copy-done.48) | copy-start | bytes 36868
  482.8 2.2 copy-start.2
  486.4 6.8 %copy-start.53 = (f32[2,1536]{1,0:T(2,128)S(1)}, f32[2,1536]{1,0:T(2,128)}, u32[]{:S(2)}) copy-start(f32[2,1536]{1,0:T(2,128)} %copy-done.52) | copy-start | bytes 36868
  487.2 6.0 %copy-start.36 = (bf16[2,128,1536]{2,1,0:T(8,128)(2,1)S(1)}, bf16[2,128,1536]{2,1,0:T(8,128)(2,1)}, u32[]{:S(2)}) copy-start(bf16[2,128,1536]{2,1,0:T(8,128)(2,1)} %reduce-scatter.5.cloned.1.call-done) | copy-start | bytes 2359300
  487.2 9.2 %slice-start = ((s8[4718592]{0:T(1024)(128)(4,1)}), s8[4194304]{0:T(1024)(128)(4,1)S(1)}, s32[]{:S(2)}) async-start(s8[4718592]{0:T(1024)(128)(4,1)} %bitcast.151), calls=%async_computation.5 | async-start | bytes 8388608
  489.0 7.4 %slice-start.1 = ((s8[4718592]{0:T(1024)(128)(4,1)}), s8[524288]{0:T(1024)(128)(4,1)S(1)}, s32[]{:S(2)}) async-start(s8[4718592]{0:T(1024)(128)(4,1)} %bitcast.151), calls=%async_computation.6 | async-start | bytes 1048576
  496.4 3.4 copy-start.6
  496.4 8.0 %copy-start.1 = (bf16[192,6144]{1,0:T(8,128)(2,1)S(1)}, bf16[192,6144]{1,0:T(8,128)(2,1)}, u32[]{:S(2)}) copy-start(bf16[192,6144]{1,0:T(8,128)(2,1)} %param.21) | copy-start | bytes 7077892
  (20 other events, 28.5 us)
Sparse Core Ops, SparseCore 0:
  142.5 69.2 all-gather.1
  232.2 79.1 reduce-scatter.2
  394.6 86.7 reduce-scatter.4
